TPU v7x, 512 devices: a whole 4x8x8 slice. The times are simulated.
512 devices in a mesh: lon: 64 (over z, y_lo, core), lat: 8 (over x, y_hi).
Axes of the slice: x: 4, y: 8 (y_hi: 2, y_lo: 4; y = y_hi * 4 + y_lo), z: 8, core: 2. Of those that a mesh axis runs over, the one named last changes fastest.
Arguments:
- potential_warmth: float32 [16, 128, 8192], P(None, 'lat', 'lon'), may hold values from -6 to 6
- saltiness_anomaly: float32 [16, 128, 8192], P(None, 'lat', 'lon'), may hold values from -6 to 6
- zonal_face_fraction: float32 [16, 128, 8192], P(None, 'lat', 'lon'), may hold values from -0.45 to 0.45
- poleward_face_fraction: float32 [16, 128, 8192], P(None, 'lat', 'lon'), may hold values from -0.45 to 0.45
- water_indicator: int32 [128, 8192], P('lat', 'lon'), may hold values 0 or 1
- water_depth_layers: int32 [128, 8192], P('lat', 'lon'), may hold values from 0 to 16
- hyperdiffusion_factor: float32 [16], replicated, may hold values from 0.005 to 0.03
Outputs:
- transported_warmth: float32 [16, 128, 8192], P(None, 'lat', 'lon')
- transported_saltiness: float32 [16, 128, 8192], P(None, 'lat', 'lon')
- zonal_flow_damped: float32 [16, 128, 8192], P(None, 'lat', 'lon')
- poleward_flow_damped: float32 [16, 128, 8192], P(None, 'lat', 'lon')
All inputs are finite; a program needn't handle non-finite values. No bound on the sum of `water_indicator` on one device may be relied on, other than what follows from the above.
Results may differ from a plain program's by a relative error of at most 0.0003.
Values sent between devices are 32-bit elements; how exact they have to be, the bound alone decides.
No kernel may reach another device: no remote copies, remote signals or barrier semaphores. Data moves between devices by JAX's collectives and lax.ppermute only.
A program may use at most 64 MiB of HBM per device.

v0:
```python
import jax
import jax.numpy as jnp
from jax import lax
from jax.sharding import PartitionSpec as P


def partner(value, axis, bit):
    return lax.ppermute(value, axis, [(i, i ^ 1 << bit) for i in range(lax.axis_size(axis))])


def with_halo(value, sides, width, wrap):
    for axis, dim in sides:
        size, length = (lax.axis_size(axis), value.shape[dim])
        up = [(i, (i + 1) % size) for i in range(size if wrap else size - 1)]
        down = [(j, i) for i, j in up]
        last = lax.slice_in_dim(value, length - width, length, axis=dim)
        first = lax.slice_in_dim(value, 0, width, axis=dim)
        before = lax.ppermute(last, axis, up)
        after = lax.ppermute(first, axis, down)
        value = jnp.concatenate([before, value, after], axis=dim)
    return value


def cut_along(source, start_at, count_of, along):
    return lax.slice_in_dim(source, start_at, start_at + count_of, axis=source.ndim + along)


def parabolic_update(tracer, courant, wet_cells, length, along):
    far_left = cut_along(tracer, 0, length + 3, along)
    near_left = cut_along(tracer, 1, length + 3, along)
    near_right = cut_along(tracer, 2, length + 3, along)
    far_right = cut_along(tracer, 3, length + 3, along)
    edges = 7.0 / 12.0 * (near_left + near_right) - 1.0 / 12.0 * (far_left + far_right)
    edges = jnp.clip(edges, jnp.minimum(near_left, near_right), jnp.maximum(near_left, near_right))
    left_edge = cut_along(edges, 0, length + 2, along)
    right_edge = cut_along(edges, 1, length + 2, along)
    middle = cut_along(tracer, 2, length + 2, along)
    flatten = (right_edge - middle) * (middle - left_edge) <= 0.0
    left_edge = jnp.where(flatten, middle, left_edge)
    right_edge = jnp.where(flatten, middle, right_edge)
    steepness = right_edge - left_edge
    bending = steepness * (middle - 0.5 * (left_edge + right_edge))
    bound_cap = steepness * steepness / 6.0
    left_final = jnp.where(bending > bound_cap, 3.0 * middle - 2.0 * right_edge, left_edge)
    right_final = jnp.where(bending < -bound_cap, 3.0 * middle - 2.0 * left_edge, right_edge)
    steepness = right_final - left_final
    curvature = 6.0 * middle - 3.0 * (left_final + right_final)
    from_left = cut_along(right_final, 0, length + 1, along) - 0.5 * courant * (
        cut_along(steepness, 0, length + 1, along)
        - (1.0 - 2.0 / 3.0 * courant) * cut_along(curvature, 0, length + 1, along)
    )
    reverse = -courant
    from_right = cut_along(left_final, 1, length + 1, along) + 0.5 * reverse * (
        cut_along(steepness, 1, length + 1, along)
        + (1.0 - 2.0 / 3.0 * reverse) * cut_along(curvature, 1, length + 1, along)
    )
    face_flux = courant * jnp.where(courant > 0.0, from_left, from_right)
    face_flux = (
        face_flux
        * cut_along(wet_cells, 0, length + 1, along)
        * cut_along(wet_cells, 1, length + 1, along)
    )
    return cut_along(tracer, 3, length, along) - (
        cut_along(face_flux, 1, length, along) - cut_along(face_flux, 0, length, along)
    )


def laplace(source, wet_cells):
    centre = source[..., 1:-1, 1:-1]
    wet_centre = wet_cells[..., 1:-1, 1:-1]
    total = wet_centre * wet_cells[..., 2:, 1:-1] * (source[..., 2:, 1:-1] - centre)
    total = total + wet_centre * wet_cells[..., :-2, 1:-1] * (source[..., :-2, 1:-1] - centre)
    total = total + wet_centre * wet_cells[..., 1:-1, 2:] * (source[..., 1:-1, 2:] - centre)
    total = total + wet_centre * wet_cells[..., 1:-1, :-2] * (source[..., 1:-1, :-2] - centre)
    return total


def folded_rows(block, width, fold_signs):
    shard_parallels = block.shape[1]
    upper_rows = block[:, shard_parallels - width :, :][:, ::-1, :][..., ::-1] * fold_signs
    for bit_index in range(lax.axis_size("lon").bit_length() - 1):
        upper_rows = partner(upper_rows, "lon", bit_index)
    return upper_rows


def close_north(extended, folded, shard_parallels, width):
    lower_rows = extended[:, : shard_parallels + width, :]
    north_rows = jnp.where(
        lax.axis_index("lat") == lax.axis_size("lat") - 1,
        folded,
        extended[:, shard_parallels + width :, :],
    )
    return jnp.concatenate([lower_rows, north_rows], axis=1)


def body(
    potential_warmth,
    saltiness_anomaly,
    zonal_face_fraction,
    poleward_face_fraction,
    water_indicator,
    water_depth_layers,
    hyperdiffusion_factor,
):
    layer_sequence, shard_parallels, shard_meridians = potential_warmth.shape
    depth_stack = (water_indicator * water_depth_layers).astype(jnp.float32)[None]
    stacked = jnp.concatenate(
        [
            potential_warmth,
            saltiness_anomaly,
            zonal_face_fraction,
            poleward_face_fraction,
            depth_stack,
        ],
        axis=0,
    )
    lon_cycle = with_halo(stacked, (("lon", 2),), 3, True)
    level_index = jnp.arange(layer_sequence, dtype=jnp.float32)[:, None, None]
    margin = 1
    fold_signs = jnp.concatenate(
        [-jnp.ones((2 * layer_sequence, 1, 1), jnp.float32), jnp.ones((1, 1, 1), jnp.float32)],
        axis=0,
    )
    flow_part = lon_cycle[2 * layer_sequence :, :, 3 - margin : 3 + shard_meridians + margin]
    flow_lat = with_halo(flow_part, (("lat", 1),), margin, False)
    flow_ext = close_north(
        flow_lat, folded_rows(flow_part, margin, fold_signs), shard_parallels, margin
    )
    wet_x = (level_index < lon_cycle[4 * layer_sequence :, :, 2 : shard_meridians + 4]).astype(
        jnp.float32
    )
    courant_x = lon_cycle[2 * layer_sequence : 3 * layer_sequence, :, 2 : shard_meridians + 3]
    tracers = lon_cycle[: 2 * layer_sequence].reshape(
        2, layer_sequence, shard_parallels, shard_meridians + 6
    )
    swept_x = parabolic_update(tracers, courant_x, wet_x, shard_meridians, -1)
    swept_flat = swept_x.reshape(2 * layer_sequence, shard_parallels, shard_meridians)
    plus_signs = jnp.ones((2 * layer_sequence, 1, 1), jnp.float32)
    swept_lat = with_halo(swept_flat, (("lat", 1),), 3, False)
    swept_ext = close_north(swept_lat, folded_rows(swept_flat, 3, plus_signs), shard_parallels, 3)
    depth_ext = flow_ext[2 * layer_sequence :]
    wet_y = (
        level_index
        < depth_ext[:, margin - 1 : margin + shard_parallels + 1, margin : margin + shard_meridians]
    ).astype(jnp.float32)
    courant_y = flow_ext[
        layer_sequence : 2 * layer_sequence,
        margin - 1 : margin + shard_parallels,
        margin : margin + shard_meridians,
    ]
    swept_y = parabolic_update(
        swept_ext.reshape(2, layer_sequence, shard_parallels + 6, shard_meridians),
        courant_y,
        wet_y,
        shard_parallels,
        -2,
    )
    both_levels = jnp.concatenate([level_index, level_index], axis=0)
    velocity = flow_ext[: 2 * layer_sequence]
    wet_all = (both_levels < depth_ext).astype(jnp.float32)
    inner = laplace(velocity, wet_all)
    inner_cycle = with_halo(inner, (("lon", 2),), 1, True)
    inner_lat = with_halo(inner_cycle, (("lat", 1),), 1, False)
    smoothed = close_north(
        inner_lat, folded_rows(inner_cycle, 1, fold_signs[: 2 * layer_sequence]), shard_parallels, 1
    )
    fourth = laplace(smoothed, wet_all)
    centre = velocity[:, margin : margin + shard_parallels, margin : margin + shard_meridians]
    coefficient = jnp.concatenate([hyperdiffusion_factor, hyperdiffusion_factor], axis=0)[
        :, None, None
    ]
    velocity_next = centre - coefficient * fourth
    return (swept_y[0], swept_y[1], velocity_next[:layer_sequence], velocity_next[layer_sequence:])


def solution(mesh):
    in_specs = (
        P(None, "lat", "lon"),
        P(None, "lat", "lon"),
        P(None, "lat", "lon"),
        P(None, "lat", "lon"),
        P("lat", "lon"),
        P("lat", "lon"),
        P(),
    )
    out_specs = (
        P(None, "lat", "lon"),
        P(None, "lat", "lon"),
        P(None, "lat", "lon"),
        P(None, "lat", "lon"),
    )
    return jax.shard_map(body, mesh=mesh, in_specs=in_specs, out_specs=out_specs, check_vma=False)
```

profile of v0, /device:TPU:6, one launch (start us, length us, event | category | flops | bytes accessed | tf_op | source)
XLA Modules:
  0.0 167.0 jit_solution(1849918960225155397)
XLA Ops:
  0.7 0.9 constant_dynamic-update-slice_fusion.4
  1.6 0.9 constant_dynamic-update-slice_fusion.3
  2.5 0.9 constant_dynamic-update-slice_fusion.6
  3.4 0.9 constant_dynamic-update-slice_fusion.5
  4.9 13.4 %collective-permute-start.1 = (f32[65,16,3]{0,1,2:T(8,128)S(1)}, f32[65,16,3]{0,1,2:T(8,128)S(1)}, u32[]{:S(2)}, u32[]{:S(2)}) collective-permute-start(f32[65,16,3]{0,1,2:T(8,128)S(1)} %copy.42), channel_id=1, source_target_pairs={{8,0},{16,8},{24,16},{32,24},{40,32},{48,40},{56,48},{64,56},{72,6... | collective-permute-start | bytes 37448 | tf_op jit(solution)/shard_map/ppermute | solution.py:19
  18.6 1.9 %collective-permute-start = (f32[65,16,3]{0,1,2:T(8,128)S(1)}, f32[65,16,3]{0,1,2:T(8,128)S(1)}, u32[]{:S(2)}, u32[]{:S(2)}) collective-permute-start(f32[65,16,3]{0,1,2:T(8,128)S(1)} %copy.41), channel_id=1, source_target_pairs={{0,8},{8,16},{16,24},{24,32},{32,40},{40,48},{48,56},{56,64},{64,7... | collective-permute-start | bytes 37448 | tf_op jit(solution)/shard_map/ppermute | solution.py:18
  20.6 7.0 %collective-permute-done = f32[65,16,3]{0,1,2:T(8,128)S(1)} collective-permute-done((f32[65,16,3]{0,1,2:T(8,128)S(1)}, f32[65,16,3]{0,1,2:T(8,128)S(1)}, u32[]{:S(2)}, u32[]{:S(2)}) %collective-permute-start) | collective-permute-done | bytes 12512 | tf_op jit(solution)/shard_map/ppermute | solution.py:18
  28.5 1.0 pad_maximum_fusion.16
  30.0 5.0 %collective-permute-start.2 = (f32[33,1,130]{2,1,0:T(1,128)}, f32[33,1,130]{2,1,0:T(1,128)S(1)}, u32[]{:S(2)}, u32[]{:S(2)}) collective-permute-start(f32[33,1,130]{2,1,0:T(1,128)} %get-tuple-element.19), channel_id=1, source_target_pairs={{0,1},{1,2},{2,3},{3,4},{4,5},{5,6},{6,7},{8,9},{9,10},{10,11},{11... | collective-permute-start | bytes 51488 | tf_op jit(solution)/shard_map/ppermute | solution.py:18
  35.0 1.0 reverse.1
  36.3 1.9 %collective-permute-start.11 = (f32[33,1,130]{2,1,0:T(1,128)S(1)}, f32[33,1,130]{2,1,0:T(1,128)S(1)}, u32[]{:S(2)}, u32[]{:S(2)}) collective-permute-start(f32[33,1,130]{2,1,0:T(1,128)S(1)} %broadcast_multiply_fusion.2), channel_id=1, source_target_pairs={{0,8},{8,0},{16,24},{24,16},{32,40},{40,32},{48,56},{56,48},{64,72... | collective-permute-start | bytes 51488 | tf_op jit(solution)/shard_map/ppermute | solution.py:8
  38.2 5.6 %collective-permute-start.17 = (f32[33,1,130]{2,1,0:T(1,128)}, f32[33,1,130]{2,1,0:T(1,128)S(1)}, u32[]{:S(2)}, u32[]{:S(2)}) collective-permute-start(f32[33,1,130]{2,1,0:T(1,128)} %get-tuple-element.18), channel_id=1, source_target_pairs={{1,0},{2,1},{3,2},{4,3},{5,4},{6,5},{7,6},{9,8},{10,9},{11,10},{12... | collective-permute-start | bytes 51488 | tf_op jit(solution)/shard_map/ppermute | solution.py:19
  44.9 1.9 %collective-permute-start.12 = (f32[33,1,130]{2,1,0:T(1,128)S(1)}, f32[33,1,130]{2,1,0:T(1,128)S(1)}, u32[]{:S(2)}, u32[]{:S(2)}) collective-permute-start(f32[33,1,130]{2,1,0:T(1,128)S(1)} %collective-permute-done.11), channel_id=1, source_target_pairs={{0,16},{8,24},{16,0},{24,8},{32,48},{40,56},{48,32},{56,40},{64,80... | collective-permute-start | bytes 51488 | tf_op jit(solution)/shard_map/ppermute | solution.py:8
  47.0 3.6 %collective-permute-done.12 = f32[33,1,130]{2,1,0:T(1,128)S(1)} collective-permute-done((f32[33,1,130]{2,1,0:T(1,128)S(1)}, f32[33,1,130]{2,1,0:T(1,128)S(1)}, u32[]{:S(2)}, u32[]{:S(2)}) %collective-permute-start.12) | collective-permute-done | bytes 17192 | tf_op jit(solution)/shard_map/ppermute | solution.py:8
  50.7 1.9 %collective-permute-start.13 = (f32[33,1,130]{2,1,0:T(1,128)S(1)}, f32[33,1,130]{2,1,0:T(1,128)S(1)}, u32[]{:S(2)}, u32[]{:S(2)}) collective-permute-start(f32[33,1,130]{2,1,0:T(1,128)S(1)} %collective-permute-done.12), channel_id=1, source_target_pairs={{0,32},{8,40},{16,48},{24,56},{32,0},{40,8},{48,16},{56,24},{64,96... | collective-permute-start | bytes 51488 | tf_op jit(solution)/shard_map/ppermute | solution.py:8
  52.7 4.7 %collective-permute-done.13 = f32[33,1,130]{2,1,0:T(1,128)S(1)} collective-permute-done((f32[33,1,130]{2,1,0:T(1,128)S(1)}, f32[33,1,130]{2,1,0:T(1,128)S(1)}, u32[]{:S(2)}, u32[]{:S(2)}) %collective-permute-start.13) | collective-permute-done | bytes 17192 | tf_op jit(solution)/shard_map/ppermute | solution.py:8
  57.4 1.9 %collective-permute-start.14 = (f32[33,1,130]{2,1,0:T(1,128)S(1)}, f32[33,1,130]{2,1,0:T(1,128)S(1)}, u32[]{:S(2)}, u32[]{:S(2)}) collective-permute-start(f32[33,1,130]{2,1,0:T(1,128)S(1)} %collective-permute-done.13), channel_id=1, source_target_pairs={{0,64},{8,72},{16,80},{24,88},{32,96},{40,104},{48,112},{56,120},{... | collective-permute-start | bytes 51488 | tf_op jit(solution)/shard_map/ppermute | solution.py:8
  59.3 3.9 %collective-permute-done.14 = f32[33,1,130]{2,1,0:T(1,128)S(1)} collective-permute-done((f32[33,1,130]{2,1,0:T(1,128)S(1)}, f32[33,1,130]{2,1,0:T(1,128)S(1)}, u32[]{:S(2)}, u32[]{:S(2)}) %collective-permute-start.14) | collective-permute-done | bytes 17192 | tf_op jit(solution)/shard_map/ppermute | solution.py:8
  63.2 1.9 %collective-permute-start.15 = (f32[33,1,130]{2,1,0:T(1,128)S(1)}, f32[33,1,130]{2,1,0:T(1,128)S(1)}, u32[]{:S(2)}, u32[]{:S(2)}) collective-permute-start(f32[33,1,130]{2,1,0:T(1,128)S(1)} %collective-permute-done.14), channel_id=1, source_target_pairs={{0,128},{8,136},{16,144},{24,152},{32,160},{40,168},{48,176},{56,1... | collective-permute-start | bytes 51488 | tf_op jit(solution)/shard_map/ppermute | solution.py:8
  65.3 4.6 %collective-permute-done.15 = f32[33,1,130]{2,1,0:T(1,128)S(1)} collective-permute-done((f32[33,1,130]{2,1,0:T(1,128)S(1)}, f32[33,1,130]{2,1,0:T(1,128)S(1)}, u32[]{:S(2)}, u32[]{:S(2)}) %collective-permute-start.15) | collective-permute-done | bytes 17192 | tf_op jit(solution)/shard_map/ppermute | solution.py:8
  69.9 1.9 %collective-permute-start.16 = (f32[33,1,130]{2,1,0:T(1,128)S(1)}, f32[33,1,130]{2,1,0:T(1,128)S(1)}, u32[]{:S(2)}, u32[]{:S(2)}) collective-permute-start(f32[33,1,130]{2,1,0:T(1,128)S(1)} %collective-permute-done.15), channel_id=1, source_target_pairs={{0,256},{8,264},{16,272},{24,280},{32,288},{40,296},{48,304},{56,3... | collective-permute-start | bytes 51488 | tf_op jit(solution)/shard_map/ppermute | solution.py:8
  73.3 6.4 %collective-permute-done.16 = f32[33,1,130]{2,1,0:T(1,128)S(1)} collective-permute-done((f32[33,1,130]{2,1,0:T(1,128)S(1)}, f32[33,1,130]{2,1,0:T(1,128)S(1)}, u32[]{:S(2)}, u32[]{:S(2)}) %collective-permute-start.16) | collective-permute-done | bytes 17192 | tf_op jit(solution)/shard_map/ppermute | solution.py:8
  79.8 0.8 fusion.47
  80.8 1.9 %collective-permute-start.19 = (f32[32,16,1]{2,1,0:T(8,128)S(1)}, f32[32,16,1]{2,1,0:T(8,128)S(1)}, u32[]{:S(2)}, u32[]{:S(2)}) collective-permute-start(f32[32,16,1]{2,1,0:T(8,128)S(1)} %get-tuple-element.26), channel_id=1, source_target_pairs={{8,0},{16,8},{24,16},{32,24},{40,32},{48,40},{56,48},{64,56},{72,6... | collective-permute-start | bytes 6152 | tf_op jit(solution)/shard_map/ppermute | solution.py:19
  82.7 2.4 %collective-permute-start.18 = (f32[32,16,1]{2,1,0:T(8,128)S(1)}, f32[32,16,1]{2,1,0:T(8,128)S(1)}, u32[]{:S(2)}, u32[]{:S(2)}) collective-permute-start(f32[32,16,1]{2,1,0:T(8,128)S(1)} %get-tuple-element.27), channel_id=1, source_target_pairs={{0,8},{8,16},{16,24},{24,32},{32,40},{40,48},{48,56},{56,64},{64,7... | collective-permute-start | bytes 6152 | tf_op jit(solution)/shard_map/ppermute | solution.py:18
  85.3 2.2 %collective-permute-done.19 = f32[32,16,1]{2,1,0:T(8,128)S(1)} collective-permute-done((f32[32,16,1]{2,1,0:T(8,128)S(1)}, f32[32,16,1]{2,1,0:T(8,128)S(1)}, u32[]{:S(2)}, u32[]{:S(2)}) %collective-permute-start.19) | collective-permute-done | bytes 2080 | tf_op jit(solution)/shard_map/ppermute | solution.py:19
  87.6 6.7 %collective-permute-done.18 = f32[32,16,1]{2,1,0:T(8,128)S(1)} collective-permute-done((f32[32,16,1]{2,1,0:T(8,128)S(1)}, f32[32,16,1]{2,1,0:T(8,128)S(1)}, u32[]{:S(2)}, u32[]{:S(2)}) %collective-permute-start.18) | collective-permute-done | bytes 2080 | tf_op jit(solution)/shard_map/ppermute | solution.py:18
  95.1 1.9 %collective-permute-start.20 = (f32[32,1,130]{2,1,0:T(1,128)S(1)}, f32[32,1,130]{2,1,0:T(1,128)S(1)}, u32[]{:S(2)}, u32[]{:S(2)}) collective-permute-start(f32[32,1,130]{2,1,0:T(1,128)S(1)} %broadcast_multiply_fusion.3), channel_id=1, source_target_pairs={{0,8},{8,0},{16,24},{24,16},{32,40},{40,32},{48,56},{56,48},{64,72... | collective-permute-start | bytes 49928 | tf_op jit(solution)/shard_map/ppermute | solution.py:8
  97.8 2.4 %collective-permute-start.4 = (f32[32,3,128]{2,1,0:T(4,128)S(1)}, f32[32,3,128]{2,1,0:T(4,128)S(1)}, u32[]{:S(2)}, u32[]{:S(2)}) collective-permute-start(f32[32,3,128]{2,1,0:T(4,128)S(1)} %rev.10), channel_id=1, source_target_pairs={{0,8},{8,0},{16,24},{24,16},{32,40},{40,32},{48,56},{56,48},{64,72... | collective-permute-start | bytes 147464 | tf_op jit(solution)/shard_map/ppermute | solution.py:8
  100.3 1.9 %collective-permute-start.21 = (f32[32,1,130]{2,1,0:T(1,128)S(1)}, f32[32,1,130]{2,1,0:T(1,128)S(1)}, u32[]{:S(2)}, u32[]{:S(2)}) collective-permute-start(f32[32,1,130]{2,1,0:T(1,128)S(1)} %collective-permute-done.20), channel_id=1, source_target_pairs={{0,16},{8,24},{16,0},{24,8},{32,48},{40,56},{48,32},{56,40},{64,80... | collective-permute-start | bytes 49928 | tf_op jit(solution)/shard_map/ppermute | solution.py:8
  102.3 4.1 %collective-permute-start.3 = (f32[32,3,128]{2,1,0:T(4,128)S(1)}, f32[32,3,128]{2,1,0:T(4,128)S(1)}, u32[]{:S(2)}, u32[]{:S(2)}) collective-permute-start(f32[32,3,128]{2,1,0:T(4,128)S(1)} %get-tuple-element.31), channel_id=1, source_target_pairs={{0,1},{1,2},{2,3},{3,4},{4,5},{5,6},{6,7},{8,9},{9,10},{10,11},{11... | collective-permute-start | bytes 147464 | tf_op jit(solution)/shard_map/ppermute | solution.py:18
  106.4 6.5 %collective-permute-start.10 = (f32[32,3,128]{2,1,0:T(4,128)}, f32[32,3,128]{2,1,0:T(4,128)S(1)}, u32[]{:S(2)}, u32[]{:S(2)}) collective-permute-start(f32[32,3,128]{2,1,0:T(4,128)} %get-tuple-element.30), channel_id=1, source_target_pairs={{1,0},{2,1},{3,2},{4,3},{5,4},{6,5},{7,6},{9,8},{10,9},{11,10},{12... | collective-permute-start | bytes 147464 | tf_op jit(solution)/shard_map/ppermute | solution.py:19
  112.9 3.9 %collective-permute-start.5 = (f32[32,3,128]{2,1,0:T(4,128)S(1)}, f32[32,3,128]{2,1,0:T(4,128)S(1)}, u32[]{:S(2)}, u32[]{:S(2)}) collective-permute-start(f32[32,3,128]{2,1,0:T(4,128)S(1)} %collective-permute-done.4), channel_id=1, source_target_pairs={{0,16},{8,24},{16,0},{24,8},{32,48},{40,56},{48,32},{56,40},{64,80... | collective-permute-start | bytes 147464 | tf_op jit(solution)/shard_map/ppermute | solution.py:8
  116.9 1.9 %collective-permute-start.22 = (f32[32,1,130]{2,1,0:T(1,128)S(1)}, f32[32,1,130]{2,1,0:T(1,128)S(1)}, u32[]{:S(2)}, u32[]{:S(2)}) collective-permute-start(f32[32,1,130]{2,1,0:T(1,128)S(1)} %collective-permute-done.21), channel_id=1, source_target_pairs={{0,32},{8,40},{16,48},{24,56},{32,0},{40,8},{48,16},{56,24},{64,96... | collective-permute-start | bytes 49928 | tf_op jit(solution)/shard_map/ppermute | solution.py:8
  119.1 4.7 %collective-permute-start.6 = (f32[32,3,128]{2,1,0:T(4,128)S(1)}, f32[32,3,128]{2,1,0:T(4,128)S(1)}, u32[]{:S(2)}, u32[]{:S(2)}) collective-permute-start(f32[32,3,128]{2,1,0:T(4,128)S(1)} %collective-permute-done.5), channel_id=1, source_target_pairs={{0,32},{8,40},{16,48},{24,56},{32,0},{40,8},{48,16},{56,24},{64,96... | collective-permute-start | bytes 147464 | tf_op jit(solution)/shard_map/ppermute | solution.py:8
  123.9 1.9 %collective-permute-start.23 = (f32[32,1,130]{2,1,0:T(1,128)S(1)}, f32[32,1,130]{2,1,0:T(1,128)S(1)}, u32[]{:S(2)}, u32[]{:S(2)}) collective-permute-start(f32[32,1,130]{2,1,0:T(1,128)S(1)} %collective-permute-done.22), channel_id=1, source_target_pairs={{0,64},{8,72},{16,80},{24,88},{32,96},{40,104},{48,112},{56,120},{... | collective-permute-start | bytes 49928 | tf_op jit(solution)/shard_map/ppermute | solution.py:8
  125.9 3.8 %collective-permute-done.23 = f32[32,1,130]{2,1,0:T(1,128)S(1)} collective-permute-done((f32[32,1,130]{2,1,0:T(1,128)S(1)}, f32[32,1,130]{2,1,0:T(1,128)S(1)}, u32[]{:S(2)}, u32[]{:S(2)}) %collective-permute-start.23) | collective-permute-done | bytes 16672 | tf_op jit(solution)/shard_map/ppermute | solution.py:8
  129.7 1.9 %collective-permute-start.24 = (f32[32,1,130]{2,1,0:T(1,128)S(1)}, f32[32,1,130]{2,1,0:T(1,128)S(1)}, u32[]{:S(2)}, u32[]{:S(2)}) collective-permute-start(f32[32,1,130]{2,1,0:T(1,128)S(1)} %collective-permute-done.23), channel_id=1, source_target_pairs={{0,128},{8,136},{16,144},{24,152},{32,160},{40,168},{48,176},{56,1... | collective-permute-start | bytes 49928 | tf_op jit(solution)/shard_map/ppermute | solution.py:8
  131.6 3.5 %collective-permute-start.26 = (f32[32,1,130]{2,1,0:T(1,128)S(1)}, f32[32,1,130]{2,1,0:T(1,128)S(1)}, u32[]{:S(2)}, u32[]{:S(2)}) collective-permute-start(f32[32,1,130]{2,1,0:T(1,128)S(1)} %get-tuple-element.20), channel_id=1, source_target_pairs={{1,0},{2,1},{3,2},{4,3},{5,4},{6,5},{7,6},{9,8},{10,9},{11,10},{12... | collective-permute-start | bytes 49928 | tf_op jit(solution)/shard_map/ppermute | solution.py:19
  135.2 1.9 %collective-permute-start.7 = (f32[32,3,128]{2,1,0:T(4,128)S(1)}, f32[32,3,128]{2,1,0:T(4,128)S(1)}, u32[]{:S(2)}, u32[]{:S(2)}) collective-permute-start(f32[32,3,128]{2,1,0:T(4,128)S(1)} %collective-permute-done.6), channel_id=1, source_target_pairs={{0,64},{8,72},{16,80},{24,88},{32,96},{40,104},{48,112},{56,120},{... | collective-permute-start | bytes 147464 | tf_op jit(solution)/shard_map/ppermute | solution.py:8
  137.1 4.1 %collective-permute-start.25 = (f32[32,1,130]{2,1,0:T(1,128)S(1)}, f32[32,1,130]{2,1,0:T(1,128)S(1)}, u32[]{:S(2)}, u32[]{:S(2)}) collective-permute-start(f32[32,1,130]{2,1,0:T(1,128)S(1)} %collective-permute-done.24), channel_id=1, source_target_pairs={{0,256},{8,264},{16,272},{24,280},{32,288},{40,296},{48,304},{56,3... | collective-permute-start | bytes 49928 | tf_op jit(solution)/shard_map/ppermute | solution.py:8
  141.4 6.2 %collective-permute-start.27 = (f32[32,1,130]{2,1,0:T(1,128)S(1)}, f32[32,1,130]{2,1,0:T(1,128)S(1)}, u32[]{:S(2)}, u32[]{:S(2)}) collective-permute-start(f32[32,1,130]{2,1,0:T(1,128)S(1)} %get-tuple-element.21), channel_id=1, source_target_pairs={{0,1},{1,2},{2,3},{3,4},{4,5},{5,6},{6,7},{8,9},{9,10},{10,11},{11... | collective-permute-start | bytes 49928 | tf_op jit(solution)/shard_map/ppermute | solution.py:18
  147.6 2.6 %collective-permute-start.8 = (f32[32,3,128]{2,1,0:T(4,128)S(1)}, f32[32,3,128]{2,1,0:T(4,128)S(1)}, u32[]{:S(2)}, u32[]{:S(2)}) collective-permute-start(f32[32,3,128]{2,1,0:T(4,128)S(1)} %collective-permute-done.7), channel_id=1, source_target_pairs={{0,128},{8,136},{16,144},{24,152},{32,160},{40,168},{48,176},{56,1... | collective-permute-start | bytes 147464 | tf_op jit(solution)/shard_map/ppermute | solution.py:8
  150.2 1.7 %collective-permute-done.27 = f32[32,1,130]{2,1,0:T(1,128)S(1)} collective-permute-done((f32[32,1,130]{2,1,0:T(1,128)S(1)}, f32[32,1,130]{2,1,0:T(1,128)S(1)}, u32[]{:S(2)}, u32[]{:S(2)}) %collective-permute-start.27) | collective-permute-done | bytes 16672 | tf_op jit(solution)/shard_map/ppermute | solution.py:18
  152.0 0.8 fusion.36
  152.8 2.3 %collective-permute-done.8 = f32[32,3,128]{2,1,0:T(4,128)S(1)} collective-permute-done((f32[32,3,128]{2,1,0:T(4,128)S(1)}, f32[32,3,128]{2,1,0:T(4,128)S(1)}, u32[]{:S(2)}, u32[]{:S(2)}) %collective-permute-start.8) | collective-permute-done | bytes 49184 | tf_op jit(solution)/shard_map/ppermute | solution.py:8
  155.1 5.2 %collective-permute-start.9 = (f32[32,3,128]{2,1,0:T(4,128)S(1)}, f32[32,3,128]{2,1,0:T(4,128)S(1)}, u32[]{:S(2)}, u32[]{:S(2)}) collective-permute-start(f32[32,3,128]{2,1,0:T(4,128)S(1)} %collective-permute-done.8), channel_id=1, source_target_pairs={{0,256},{8,264},{16,272},{24,280},{32,288},{40,296},{48,304},{56,3... | collective-permute-start | bytes 147464 | tf_op jit(solution)/shard_map/ppermute | solution.py:8
  161.0 4.1 %collective-permute-done.9 = f32[32,3,128]{2,1,0:T(4,128)S(1)} collective-permute-done((f32[32,3,128]{2,1,0:T(4,128)S(1)}, f32[32,3,128]{2,1,0:T(4,128)S(1)}, u32[]{:S(2)}, u32[]{:S(2)}) %collective-permute-start.9) | collective-permute-done | bytes 49184 | tf_op jit(solution)/shard_map/ppermute | solution.py:8
  (73 shorter events, 10.7 us)
Async XLA Ops:
  0.6 3.7 %copy-start.3 = (s32[16,128]{1,0:T(8,128)S(1)}, s32[16,128]{1,0:T(8,128)}, u32[]{:S(2)}) copy-start(s32[16,128]{1,0:T(8,128)} %param.12) | copy-start | bytes 24580
  0.6 3.7 %copy-start.2 = (s32[16,128]{1,0:T(8,128)S(1)}, s32[16,128]{1,0:T(8,128)}, u32[]{:S(2)}) copy-start(s32[16,128]{1,0:T(8,128)} %param.11) | copy-start | bytes 24580
  4.9 23.3 %collective-permute-start.1 = (f32[65,16,3]{0,1,2:T(8,128)S(1)}, f32[65,16,3]{0,1,2:T(8,128)S(1)}, u32[]{:S(2)}, u32[]{:S(2)}) collective-permute-start(f32[65,16,3]{0,1,2:T(8,128)S(1)} %copy.42), channel_id=1, source_target_pairs={{8,0},{16,8},{24,16},{32,24},{40,32},{48,40},{56,48},{64,56},{72,6... | collective-permute-start | bytes 37448 | tf_op jit(solution)/shard_map/ppermute | solution.py:19
  18.6 9.0 %collective-permute-start = (f32[65,16,3]{0,1,2:T(8,128)S(1)}, f32[65,16,3]{0,1,2:T(8,128)S(1)}, u32[]{:S(2)}, u32[]{:S(2)}) collective-permute-start(f32[65,16,3]{0,1,2:T(8,128)S(1)} %copy.41), channel_id=1, source_target_pairs={{0,8},{8,16},{16,24},{24,32},{32,40},{40,48},{48,56},{56,64},{64,7... | collective-permute-start | bytes 37448 | tf_op jit(solution)/shard_map/ppermute | solution.py:18
  29.5 6.6 %copy-start.4 = (f32[33]{0:T(128)S(1)}, f32[33]{0:T(128)}, u32[]{:S(2)}) copy-start(f32[33]{0:T(128)} %constant.26.clone.1) | copy-start | bytes 400
  30.0 13.9 %copy-start = (f32[65,16,134]{2,1,0:T(8,128)}, f32[65,16,134]{2,1,0:T(8,128)S(1)}, u32[]{:S(2)}) copy-start(f32[65,16,134]{2,1,0:T(8,128)S(1)} %pad_maximum_fusion) | copy-start | bytes 1672324
  30.0 49.7 %collective-permute-start.2 = (f32[33,1,130]{2,1,0:T(1,128)}, f32[33,1,130]{2,1,0:T(1,128)S(1)}, u32[]{:S(2)}, u32[]{:S(2)}) collective-permute-start(f32[33,1,130]{2,1,0:T(1,128)} %get-tuple-element.19), channel_id=1, source_target_pairs={{0,1},{1,2},{2,3},{3,4},{4,5},{5,6},{6,7},{8,9},{9,10},{10,11},{11... | collective-permute-start | bytes 51488 | tf_op jit(solution)/shard_map/ppermute | solution.py:18
  36.3 8.6 %collective-permute-start.11 = (f32[33,1,130]{2,1,0:T(1,128)S(1)}, f32[33,1,130]{2,1,0:T(1,128)S(1)}, u32[]{:S(2)}, u32[]{:S(2)}) collective-permute-start(f32[33,1,130]{2,1,0:T(1,128)S(1)} %broadcast_multiply_fusion.2), channel_id=1, source_target_pairs={{0,8},{8,0},{16,24},{24,16},{32,40},{40,32},{48,56},{56,48},{64,72... | collective-permute-start | bytes 51488 | tf_op jit(solution)/shard_map/ppermute | solution.py:8
  38.2 35.1 %collective-permute-start.17 = (f32[33,1,130]{2,1,0:T(1,128)}, f32[33,1,130]{2,1,0:T(1,128)S(1)}, u32[]{:S(2)}, u32[]{:S(2)}) collective-permute-start(f32[33,1,130]{2,1,0:T(1,128)} %get-tuple-element.18), channel_id=1, source_target_pairs={{1,0},{2,1},{3,2},{4,3},{5,4},{6,5},{7,6},{9,8},{10,9},{11,10},{12... | collective-permute-start | bytes 51488 | tf_op jit(solution)/shard_map/ppermute | solution.py:19
  44.9 5.8 %collective-permute-start.12 = (f32[33,1,130]{2,1,0:T(1,128)S(1)}, f32[33,1,130]{2,1,0:T(1,128)S(1)}, u32[]{:S(2)}, u32[]{:S(2)}) collective-permute-start(f32[33,1,130]{2,1,0:T(1,128)S(1)} %collective-permute-done.11), channel_id=1, source_target_pairs={{0,16},{8,24},{16,0},{24,8},{32,48},{40,56},{48,32},{56,40},{64,80... | collective-permute-start | bytes 51488 | tf_op jit(solution)/shard_map/ppermute | solution.py:8
  50.7 6.7 %collective-permute-start.13 = (f32[33,1,130]{2,1,0:T(1,128)S(1)}, f32[33,1,130]{2,1,0:T(1,128)S(1)}, u32[]{:S(2)}, u32[]{:S(2)}) collective-permute-start(f32[33,1,130]{2,1,0:T(1,128)S(1)} %collective-permute-done.12), channel_id=1, source_target_pairs={{0,32},{8,40},{16,48},{24,56},{32,0},{40,8},{48,16},{56,24},{64,96... | collective-permute-start | bytes 51488 | tf_op jit(solution)/shard_map/ppermute | solution.py:8
  57.4 5.8 %collective-permute-start.14 = (f32[33,1,130]{2,1,0:T(1,128)S(1)}, f32[33,1,130]{2,1,0:T(1,128)S(1)}, u32[]{:S(2)}, u32[]{:S(2)}) collective-permute-start(f32[33,1,130]{2,1,0:T(1,128)S(1)} %collective-permute-done.13), channel_id=1, source_target_pairs={{0,64},{8,72},{16,80},{24,88},{32,96},{40,104},{48,112},{56,120},{... | collective-permute-start | bytes 51488 | tf_op jit(solution)/shard_map/ppermute | solution.py:8
  63.2 6.7 %collective-permute-start.15 = (f32[33,1,130]{2,1,0:T(1,128)S(1)}, f32[33,1,130]{2,1,0:T(1,128)S(1)}, u32[]{:S(2)}, u32[]{:S(2)}) collective-permute-start(f32[33,1,130]{2,1,0:T(1,128)S(1)} %collective-permute-done.14), channel_id=1, source_target_pairs={{0,128},{8,136},{16,144},{24,152},{32,160},{40,168},{48,176},{56,1... | collective-permute-start | bytes 51488 | tf_op jit(solution)/shard_map/ppermute | solution.py:8
  69.9 9.7 %collective-permute-start.16 = (f32[33,1,130]{2,1,0:T(1,128)S(1)}, f32[33,1,130]{2,1,0:T(1,128)S(1)}, u32[]{:S(2)}, u32[]{:S(2)}) collective-permute-start(f32[33,1,130]{2,1,0:T(1,128)S(1)} %collective-permute-done.15), channel_id=1, source_target_pairs={{0,256},{8,264},{16,272},{24,280},{32,288},{40,296},{48,304},{56,3... | collective-permute-start | bytes 51488 | tf_op jit(solution)/shard_map/ppermute | solution.py:8
  71.8 1.2 copy-start.1
  80.8 6.8 %collective-permute-start.19 = (f32[32,16,1]{2,1,0:T(8,128)S(1)}, f32[32,16,1]{2,1,0:T(8,128)S(1)}, u32[]{:S(2)}, u32[]{:S(2)}) collective-permute-start(f32[32,16,1]{2,1,0:T(8,128)S(1)} %get-tuple-element.26), channel_id=1, source_target_pairs={{8,0},{16,8},{24,16},{32,24},{40,32},{48,40},{56,48},{64,56},{72,6... | collective-permute-start | bytes 6152 | tf_op jit(solution)/shard_map/ppermute | solution.py:19
  82.7 19.5 %copy-start.5 = (f32[16]{0:T(128)S(1)}, f32[16]{0:T(128)}, u32[]{:S(2)}) copy-start(f32[16]{0:T(128)} %param.13) | copy-start | bytes 196
  82.7 11.6 %collective-permute-start.18 = (f32[32,16,1]{2,1,0:T(8,128)S(1)}, f32[32,16,1]{2,1,0:T(8,128)S(1)}, u32[]{:S(2)}, u32[]{:S(2)}) collective-permute-start(f32[32,16,1]{2,1,0:T(8,128)S(1)} %get-tuple-element.27), channel_id=1, source_target_pairs={{0,8},{8,16},{16,24},{24,32},{32,40},{40,48},{48,56},{56,64},{64,7... | collective-permute-start | bytes 6152 | tf_op jit(solution)/shard_map/ppermute | solution.py:18
  95.1 5.2 %collective-permute-start.20 = (f32[32,1,130]{2,1,0:T(1,128)S(1)}, f32[32,1,130]{2,1,0:T(1,128)S(1)}, u32[]{:S(2)}, u32[]{:S(2)}) collective-permute-start(f32[32,1,130]{2,1,0:T(1,128)S(1)} %broadcast_multiply_fusion.3), channel_id=1, source_target_pairs={{0,8},{8,0},{16,24},{24,16},{32,40},{40,32},{48,56},{56,48},{64,72... | collective-permute-start | bytes 49928 | tf_op jit(solution)/shard_map/ppermute | solution.py:8
  97.8 15.1 %collective-permute-start.4 = (f32[32,3,128]{2,1,0:T(4,128)S(1)}, f32[32,3,128]{2,1,0:T(4,128)S(1)}, u32[]{:S(2)}, u32[]{:S(2)}) collective-permute-start(f32[32,3,128]{2,1,0:T(4,128)S(1)} %rev.10), channel_id=1, source_target_pairs={{0,8},{8,0},{16,24},{24,16},{32,40},{40,32},{48,56},{56,48},{64,72... | collective-permute-start | bytes 147464 | tf_op jit(solution)/shard_map/ppermute | solution.py:8
  100.3 16.6 %collective-permute-start.21 = (f32[32,1,130]{2,1,0:T(1,128)S(1)}, f32[32,1,130]{2,1,0:T(1,128)S(1)}, u32[]{:S(2)}, u32[]{:S(2)}) collective-permute-start(f32[32,1,130]{2,1,0:T(1,128)S(1)} %collective-permute-done.20), channel_id=1, source_target_pairs={{0,16},{8,24},{16,0},{24,8},{32,48},{40,56},{48,32},{56,40},{64,80... | collective-permute-start | bytes 49928 | tf_op jit(solution)/shard_map/ppermute | solution.py:8
  102.3 62.9 %collective-permute-start.3 = (f32[32,3,128]{2,1,0:T(4,128)S(1)}, f32[32,3,128]{2,1,0:T(4,128)S(1)}, u32[]{:S(2)}, u32[]{:S(2)}) collective-permute-start(f32[32,3,128]{2,1,0:T(4,128)S(1)} %get-tuple-element.31), channel_id=1, source_target_pairs={{0,1},{1,2},{2,3},{3,4},{4,5},{5,6},{6,7},{8,9},{9,10},{10,11},{11... | collective-permute-start | bytes 147464 | tf_op jit(solution)/shard_map/ppermute | solution.py:18
  106.4 54.6 %collective-permute-start.10 = (f32[32,3,128]{2,1,0:T(4,128)}, f32[32,3,128]{2,1,0:T(4,128)S(1)}, u32[]{:S(2)}, u32[]{:S(2)}) collective-permute-start(f32[32,3,128]{2,1,0:T(4,128)} %get-tuple-element.30), channel_id=1, source_target_pairs={{1,0},{2,1},{3,2},{4,3},{5,4},{6,5},{7,6},{9,8},{10,9},{11,10},{12... | collective-permute-start | bytes 147464 | tf_op jit(solution)/shard_map/ppermute | solution.py:19
  112.9 6.2 %collective-permute-start.5 = (f32[32,3,128]{2,1,0:T(4,128)S(1)}, f32[32,3,128]{2,1,0:T(4,128)S(1)}, u32[]{:S(2)}, u32[]{:S(2)}) collective-permute-start(f32[32,3,128]{2,1,0:T(4,128)S(1)} %collective-permute-done.4), channel_id=1, source_target_pairs={{0,16},{8,24},{16,0},{24,8},{32,48},{40,56},{48,32},{56,40},{64,80... | collective-permute-start | bytes 147464 | tf_op jit(solution)/shard_map/ppermute | solution.py:8
  116.9 7.0 %collective-permute-start.22 = (f32[32,1,130]{2,1,0:T(1,128)S(1)}, f32[32,1,130]{2,1,0:T(1,128)S(1)}, u32[]{:S(2)}, u32[]{:S(2)}) collective-permute-start(f32[32,1,130]{2,1,0:T(1,128)S(1)} %collective-permute-done.21), channel_id=1, source_target_pairs={{0,32},{8,40},{16,48},{24,56},{32,0},{40,8},{48,16},{56,24},{64,96... | collective-permute-start | bytes 49928 | tf_op jit(solution)/shard_map/ppermute | solution.py:8
  119.1 16.1 %collective-permute-start.6 = (f32[32,3,128]{2,1,0:T(4,128)S(1)}, f32[32,3,128]{2,1,0:T(4,128)S(1)}, u32[]{:S(2)}, u32[]{:S(2)}) collective-permute-start(f32[32,3,128]{2,1,0:T(4,128)S(1)} %collective-permute-done.5), channel_id=1, source_target_pairs={{0,32},{8,40},{16,48},{24,56},{32,0},{40,8},{48,16},{56,24},{64,96... | collective-permute-start | bytes 147464 | tf_op jit(solution)/shard_map/ppermute | solution.py:8
  123.9 5.8 %collective-permute-start.23 = (f32[32,1,130]{2,1,0:T(1,128)S(1)}, f32[32,1,130]{2,1,0:T(1,128)S(1)}, u32[]{:S(2)}, u32[]{:S(2)}) collective-permute-start(f32[32,1,130]{2,1,0:T(1,128)S(1)} %collective-permute-done.22), channel_id=1, source_target_pairs={{0,64},{8,72},{16,80},{24,88},{32,96},{40,104},{48,112},{56,120},{... | collective-permute-start | bytes 49928 | tf_op jit(solution)/shard_map/ppermute | solution.py:8
  129.7 7.4 %collective-permute-start.24 = (f32[32,1,130]{2,1,0:T(1,128)S(1)}, f32[32,1,130]{2,1,0:T(1,128)S(1)}, u32[]{:S(2)}, u32[]{:S(2)}) collective-permute-start(f32[32,1,130]{2,1,0:T(1,128)S(1)} %collective-permute-done.23), channel_id=1, source_target_pairs={{0,128},{8,136},{16,144},{24,152},{32,160},{40,168},{48,176},{56,1... | collective-permute-start | bytes 49928 | tf_op jit(solution)/shard_map/ppermute | solution.py:8
  131.6 9.7 %collective-permute-start.26 = (f32[32,1,130]{2,1,0:T(1,128)S(1)}, f32[32,1,130]{2,1,0:T(1,128)S(1)}, u32[]{:S(2)}, u32[]{:S(2)}) collective-permute-start(f32[32,1,130]{2,1,0:T(1,128)S(1)} %get-tuple-element.20), channel_id=1, source_target_pairs={{1,0},{2,1},{3,2},{4,3},{5,4},{6,5},{7,6},{9,8},{10,9},{11,10},{12... | collective-permute-start | bytes 49928 | tf_op jit(solution)/shard_map/ppermute | solution.py:19
  135.2 12.4 %collective-permute-start.7 = (f32[32,3,128]{2,1,0:T(4,128)S(1)}, f32[32,3,128]{2,1,0:T(4,128)S(1)}, u32[]{:S(2)}, u32[]{:S(2)}) collective-permute-start(f32[32,3,128]{2,1,0:T(4,128)S(1)} %collective-permute-done.6), channel_id=1, source_target_pairs={{0,64},{8,72},{16,80},{24,88},{32,96},{40,104},{48,112},{56,120},{... | collective-permute-start | bytes 147464 | tf_op jit(solution)/shard_map/ppermute | solution.py:8
  137.1 13.1 %collective-permute-start.25 = (f32[32,1,130]{2,1,0:T(1,128)S(1)}, f32[32,1,130]{2,1,0:T(1,128)S(1)}, u32[]{:S(2)}, u32[]{:S(2)}) collective-permute-start(f32[32,1,130]{2,1,0:T(1,128)S(1)} %collective-permute-done.24), channel_id=1, source_target_pairs={{0,256},{8,264},{16,272},{24,280},{32,288},{40,296},{48,304},{56,3... | collective-permute-start | bytes 49928 | tf_op jit(solution)/shard_map/ppermute | solution.py:8
  141.4 10.6 %collective-permute-start.27 = (f32[32,1,130]{2,1,0:T(1,128)S(1)}, f32[32,1,130]{2,1,0:T(1,128)S(1)}, u32[]{:S(2)}, u32[]{:S(2)}) collective-permute-start(f32[32,1,130]{2,1,0:T(1,128)S(1)} %get-tuple-element.21), channel_id=1, source_target_pairs={{0,1},{1,2},{2,3},{3,4},{4,5},{5,6},{6,7},{8,9},{9,10},{10,11},{11... | collective-permute-start | bytes 49928 | tf_op jit(solution)/shard_map/ppermute | solution.py:18
  147.6 7.5 %collective-permute-start.8 = (f32[32,3,128]{2,1,0:T(4,128)S(1)}, f32[32,3,128]{2,1,0:T(4,128)S(1)}, u32[]{:S(2)}, u32[]{:S(2)}) collective-permute-start(f32[32,3,128]{2,1,0:T(4,128)S(1)} %collective-permute-done.7), channel_id=1, source_target_pairs={{0,128},{8,136},{16,144},{24,152},{32,160},{40,168},{48,176},{56,1... | collective-permute-start | bytes 147464 | tf_op jit(solution)/shard_map/ppermute | solution.py:8
  155.1 10.1 %collective-permute-start.9 = (f32[32,3,128]{2,1,0:T(4,128)S(1)}, f32[32,3,128]{2,1,0:T(4,128)S(1)}, u32[]{:S(2)}, u32[]{:S(2)}) collective-permute-start(f32[32,3,128]{2,1,0:T(4,128)S(1)} %collective-permute-done.8), channel_id=1, source_target_pairs={{0,256},{8,264},{16,272},{24,280},{32,288},{40,296},{48,304},{56,3... | collective-permute-start | bytes 147464 | tf_op jit(solution)/shard_map/ppermute | solution.py:8
where the time goes:
time: 168 us; the launch traced here: 167 us
  starting transfers between devices  96.6 us (58%)
  waiting for transfers between devices  51.4 us (31%)
  local copies, waits for them, and re-layouts  9.74 us (6%)
  other arithmetic  7.97 us (5%)
    ppermute x18, starting transfers between devices, partner(): lax.ppermute(value, axis, [(i, i ^ 1 << bit) for i in range(lax.axis_size...  46 us
    ppermute x18, waiting for transfers between devices, partner(): lax.ppermute(value, axis, [(i, i ^ 1 << bit) for i in range(lax.axis_size...  33.6 us
    ppermute x5, starting transfers between devices, with_halo(): after = lax.ppermute(first, axis, down)  31 us
    ppermute x5, starting transfers between devices, with_halo(): before = lax.ppermute(last, axis, up)  19.7 us
    ppermute x5, waiting for transfers between devices, with_halo(): before = lax.ppermute(last, axis, up)  15.5 us
    unnamed x17, local copies, waits for them, and re-layouts  4.72 us
  transfers between devices with their start and end apart: 28, of which 15 were waited for; matrix products, arithmetic and copies ran while one was open for 4% of the time, Pallas kernels for 0%

commit v1 on v0

v1 whole, which is shorter than its diff:
```python
import functools

import jax
import jax.numpy as jnp
from jax import lax
from jax.experimental import pallas as pl
from jax.experimental.pallas import tpu as pltpu
from jax.sharding import PartitionSpec as P

K, J, W = 16, 16, 128
WIN = 6
SEND_ROWS = 23
F32 = jnp.float32


def lanes():
    return lax.broadcasted_iota(jnp.int32, (K, W), 1)


def levels():
    return lax.broadcasted_iota(jnp.int32, (K, W), 0).astype(F32)


def low_half(lane):
    return lane - WIN * ((lane * 43) >> 8) < WIN // 2


def roll(x, shift):
    shift %= W
    return x if shift == 0 else pltpu.roll(x, shift, 1)


def load_row(ref, j):
    return ref[pl.ds(j, K, stride=J), :]


def store_row(ref, j, value):
    ref[pl.ds(j, K, stride=J), :] = value


def depth_row(indicator, layers, j):
    row = (indicator[j : j + 1, :] * layers[j : j + 1, :]).astype(F32)
    return jnp.broadcast_to(row, (K, W))


def wet_of(depth):
    return jnp.where(levels() < depth, 1.0, 0.0).astype(F32)


def unpack(packed, j):
    return roll(packed, -(WIN * j + 3))


def east(x, halo, lane):
    return roll(jnp.where(lane < 1, halo, x), -1)


def west(x, halo, lane):
    return roll(jnp.where(lane == W - 1, halo, x), 1)


def edge_between(far_left, near_left, near_right, far_right):
    edge = (7.0 / 12.0) * (near_left + near_right) - (1.0 / 12.0) * (far_left + far_right)
    return jnp.clip(edge, jnp.minimum(near_left, near_right), jnp.maximum(near_left, near_right))


def limited(q, left, right):
    flat = (right - q) * (q - left) <= 0.0
    left = jnp.where(flat, q, left)
    right = jnp.where(flat, q, right)
    steep = right - left
    bend = steep * (q - 0.5 * (left + right))
    cap = steep * steep * (1.0 / 6.0)
    q3 = 3.0 * q
    left_out = jnp.where(bend > cap, q3 - 2.0 * right, left)
    right_out = jnp.where(bend < -cap, q3 - 2.0 * left, right)
    return left_out, right_out, right_out - left_out, 6.0 * q - 3.0 * (left_out + right_out)


def out_right(cell, c):
    _, right, steep, curve = cell
    return right - 0.5 * c * (steep - (1.0 - (2.0 / 3.0) * c) * curve)


def out_left(cell, c):
    left, _, steep, curve = cell
    return left - 0.5 * c * (steep + (1.0 + (2.0 / 3.0) * c) * curve)


def pack_columns(rows):
    lane = lanes()
    packed = jnp.zeros((K, W), F32)
    for j, row in enumerate(rows):
        mine = (lane >= WIN * j) & (lane < WIN * j + WIN)
        packed = jnp.where(mine, roll(row, WIN * j + 3), packed)
    return packed


def pack_kernel(t_ref, s_ref, u_ref, v_ref, ind_ref, lay_ref, own_ref, ev_ref, od_ref):
    fields = [pack_columns([load_row(r, j) for j in range(J)]) for r in (t_ref, s_ref, u_ref)]
    fields.append(pack_columns([depth_row(ind_ref, lay_ref, j) for j in range(J)]))
    fields.append(pack_columns([load_row(v_ref, j) for j in range(J)]))
    for n, x in enumerate(fields):
        own_ref[:, n * W : (n + 1) * W] = x
    t, s, u, d, v = fields
    low = low_half(lanes())
    even = (lax.axis_index("lon") & 1) == 0
    for n, (a, b) in enumerate(((t, s), (u, d), (v, v))):
        to_east = jnp.where(low, a, roll(b, 3))
        to_west = jnp.where(low, roll(b, -3), a)
        at = slice(n * W, (n + 1) * W)
        ev_ref[:, at] = jnp.where(even, to_east, to_west)
        od_ref[:, at] = jnp.where(even, to_west, to_east)


def seams(own_ref, ev_ref, od_ref):
    low = low_half(lanes())
    even = (lax.axis_index("lon") & 1) == 0
    mate = pl.multiple_of(jnp.where(even, K, 0), K)
    out = []
    for n in range(5):
        at = slice((n // 2) * W, (n // 2 + 1) * W)
        ev = ev_ref[pl.ds(mate, K), at]
        od = od_ref[:, at]
        from_west = jnp.where(even, od, ev)
        from_east = jnp.where(even, ev, od)
        if n in (1, 3):
            from_west, from_east = roll(from_west, -3), roll(from_east, 3)
        own = own_ref[:, n * W : (n + 1) * W]
        out.append(
            (
                jnp.where(low, from_west, from_east),
                jnp.where(low, from_west, own),
                jnp.where(low, own, from_east),
            )
        )
    return out


def seam_flux(q, c, wet):
    edge = edge_between(roll(q, 1), q, roll(q, -1), roll(q, -2))
    cell = limited(q, roll(edge, 1), edge)
    flux = jnp.where(c > 0.0, out_right(cell, c), roll(out_left(cell, roll(c, 1)), -1))
    return edge, c * wet * roll(wet, -1) * flux


class Zonal:
    def __init__(self, packs, u_ref, ind_ref, lay_ref):
        self.packs, self.u_ref, self.ind, self.lay = packs, u_ref, ind_ref, lay_ref
        lane = lanes()
        third = lane - WIN * ((lane * 43) >> 8) == 2
        _, uw, ue = packs[2]
        _, dw, de = packs[3]
        ww, we = wet_of(dw), wet_of(de)
        self.fix = []
        for n in range(2):
            edge_w, flux_w = seam_flux(packs[n][1], uw, ww)
            _, flux_e = seam_flux(packs[n][2], ue, we)
            self.fix.append((jnp.where(third, flux_e, roll(edge_w, 1)), flux_w))

    def row(self, refs, j):
        lane = lanes()
        u = load_row(self.u_ref, j)
        wet = wet_of(depth_row(self.ind, self.lay, j))
        halo_wet = wet_of(unpack(self.packs[3][0], j))
        c_west = west(u, unpack(self.packs[2][0], j), lane)
        face = u * wet * east(wet, halo_wet, lane)
        forward = u > 0.0
        out = []
        for n, ref in enumerate(refs):
            q = load_row(ref, j)
            halo = unpack(self.packs[n][0], j)
            fix, flux_in = (unpack(x, j) for x in self.fix[n])
            edge = edge_between(
                west(q, halo, lane),
                q,
                east(q, halo, lane),
                roll(jnp.where(lane < 2, halo, q), -2),
            )
            cell = limited(q, jnp.where(lane == 0, fix, roll(edge, 1)), edge)
            flux = face * jnp.where(
                forward, out_right(cell, u), roll(out_left(cell, c_west), -1)
            )
            last = lane == W - 1
            flux_west = roll(jnp.where(last, flux_in, flux), 1)
            out.append(q - (jnp.where(last, fix, flux) - flux_west))
        return out


def zonal_lap(f, halo, wet, halo_wet, lane):
    grad = wet * east(wet, halo_wet, lane) * (east(f, halo, lane) - f)
    grad_w = wet * west(wet, halo_wet, lane) * (f - west(f, halo, lane))
    return grad - grad_w


def seam_lap(f, wet):
    total = None
    for shift in (1, -1, WIN, -WIN):
        term = wet * roll(wet, shift) * (roll(f, shift) - f)
        total = term if total is None else total + term
    return total


def edge_kernel(
    t_ref, s_ref, u_ref, v_ref, ind_ref, lay_ref, own_ref, ev_ref, od_ref, swept_ref, e_ref, o_ref
):
    lane = lanes()
    packs = seams(own_ref, ev_ref, od_ref)
    zonal = Zonal(packs, u_ref, ind_ref, lay_ref)
    halves = []
    for rows in ((J - 1, J - 2, J - 3), (0, 1, 2)):
        planes = [zonal.row((t_ref, s_ref), j) for j in rows]
        for j, (t, s) in zip(rows, planes):
            swept_ref[j if j < 3 else j - 10] = t
            swept_ref[6 + (j if j < 3 else j - 10)] = s
        half = [p[0] for p in planes] + [p[1] for p in planes]
        j, inward = rows[0], rows[1]
        depth = depth_row(ind_ref, lay_ref, j)
        halo_depth = unpack(packs[3][0], j)
        wet, halo_wet = wet_of(depth), wet_of(halo_depth)
        to_inner = wet * wet_of(depth_row(ind_ref, lay_ref, inward))
        corner = roll(halo_depth, 2)
        corner = jnp.where(lane < W // 2, corner, roll(halo_depth, -2))
        for ref, pack, reach in ((v_ref, packs[4], 1), (u_ref, packs[2], 0)):
            halo = unpack(pack[0], j)
            f = load_row(ref, j)
            partial = zonal_lap(f, halo, wet, halo_wet, lane) + to_inner * (load_row(ref, inward) - f)
            half[6:6] = [f, partial]
            take = jnp.where(lane < W // 2, roll(halo, reach), roll(halo, -reach))
            corner = jnp.where((lane == reach) | (lane == W - 1 - reach), take, corner)
        halves.append((half + [corner], depth[:8]))
    lat = lax.axis_index("lat")
    even = (lat & 1) == 0
    top = lat == lax.axis_size("lat") - 1
    (north, north_d), (south, south_d) = halves
    for n, (a, b) in enumerate(zip(north, south)):
        e_ref[2 * n : 2 * n + 2] = jnp.where(even, a, b).reshape(2, 8, W)
        o_ref[2 * n : 2 * n + 2] = jnp.where(even, b, a).reshape(2, 8, W)
    e_ref[SEND_ROWS - 1] = jnp.where(even, north_d, south_d)
    o_ref[SEND_ROWS - 1] = jnp.where(even, south_d, north_d)

    @pl.when(top)
    def _():
        mirror = W - 1 - lax.broadcasted_iota(jnp.int32, (8, W), 1)
        lane8 = lax.broadcasted_iota(jnp.int32, (8, W), 1)
        for n in range(SEND_ROWS):
            x = jnp.take_along_axis(o_ref[n], mirror, axis=1)
            if 12 <= n < 20:
                x = -x
            elif 20 <= n < 22:
                x = jnp.where((lane8 < 2) | (lane8 > W - 3), -x, x)
            o_ref[n] = x


def merid_cell(q, j):
    return limited(
        q[j],
        edge_between(q[j - 2], q[j - 1], q[j], q[j + 1]),
        edge_between(q[j - 1], q[j], q[j + 1], q[j + 2]),
    )


AUX_TRACER, AUX_FLOW = 12, 10


def inner_kernel(
    t_ref,
    s_ref,
    u_ref,
    v_ref,
    ind_ref,
    lay_ref,
    visc_ref,
    own_ref,
    ev_ref,
    od_ref,
    swept_ref,
    t_out,
    s_out,
    u_out,
    v_out,
    aux_ref,
):
    lane = lanes()
    packs = seams(own_ref, ev_ref, od_ref)
    zonal = Zonal(packs, u_ref, ind_ref, lay_ref)
    rows = [{}, {}]
    for j in (0, 1, 2, 13, 14, 15):
        for n in range(2):
            rows[n][j] = swept_ref[6 * n + (j if j < 3 else j - 10)]
    for j in range(3, 13):
        rows[0][j], rows[1][j] = zonal.row((t_ref, s_ref), j)
    wet = [wet_of(depth_row(ind_ref, lay_ref, j)) for j in range(J)]
    for n, out in enumerate((t_out, s_out)):
        q = rows[n]
        for at, j in enumerate((0, 1, 2, 3, 4, 11, 12, 13, 14, 15)):
            aux_ref[AUX_TRACER * n + at] = q[j]
        cell = merid_cell(q, 2)
        before = None
        for j in range(2, 13):
            after = merid_cell(q, j + 1)
            c = load_row(v_ref, j)
            flux = c * wet[j] * wet[j + 1] * jnp.where(c > 0.0, out_right(cell, c), out_left(after, c))
            if j == 2:
                aux_ref[AUX_TRACER * n + 10] = flux
            else:
                store_row(out, j, q[j] - (flux - before))
            if j == 12:
                aux_ref[AUX_TRACER * n + 11] = flux
            cell, before = after, flux
    wet_w, wet_e = wet_of(packs[3][1]), wet_of(packs[3][2])
    low = low_half(lane)
    visc = viscosity(visc_ref)
    halo_wet = [wet_of(unpack(packs[3][0], j)) for j in range(J)]
    for n, (ref, pack, out) in enumerate(((u_ref, packs[2], u_out), (v_ref, packs[4], v_out))):
        base = 2 * AUX_TRACER + AUX_FLOW * n
        halo_lap = jnp.where(low, seam_lap(pack[1], wet_w), seam_lap(pack[2], wet_e))
        f = [load_row(ref, j) for j in range(J)]
        lap = []
        step = None
        for j in range(J):
            total = zonal_lap(f[j], unpack(pack[0], j), wet[j], halo_wet[j], lane)
            if step is not None:
                total = total - step
            if j < J - 1:
                step = wet[j] * wet[j + 1] * (f[j + 1] - f[j])
                total = total + step
            lap.append(total)
        step = None
        for j in range(1, J - 1):
            total = zonal_lap(lap[j], unpack(halo_lap, j), wet[j], halo_wet[j], lane)
            if step is not None:
                total = total - step
            if j < J - 2:
                step = wet[j] * wet[j + 1] * (lap[j + 1] - lap[j])
                total = total + step
            if j == 1:
                aux_ref[base + 2] = total
            elif j == J - 2:
                aux_ref[base + 5] = total
            else:
                store_row(out, j, f[j] - visc * total)
        aux_ref[base + 0] = lap[0]
        aux_ref[base + 1] = lap[1]
        aux_ref[base + 3] = lap[J - 1]
        aux_ref[base + 4] = lap[J - 2]
        aux_ref[base + 6] = unpack(halo_lap, 0)
        aux_ref[base + 7] = unpack(halo_lap, J - 1)
        aux_ref[base + 8] = unpack(pack[0], 0)
        aux_ref[base + 9] = unpack(pack[0], J - 1)
    aux_ref[2 * AUX_TRACER + 2 * AUX_FLOW] = halo_wet[0]
    aux_ref[2 * AUX_TRACER + 2 * AUX_FLOW + 1] = halo_wet[J - 1]


def viscosity(visc_ref):
    level = lax.broadcasted_iota(jnp.int32, (K, W), 0)
    visc = jnp.zeros((K, W), F32)
    for k in range(K):
        visc = jnp.where(level == k, visc_ref[k], visc)
    return visc


def finish_kernel(
    u_ref,
    v_ref,
    ind_ref,
    lay_ref,
    visc_ref,
    t_in,
    s_in,
    u_in,
    v_in,
    aux_ref,
    e_ref,
    o_ref,
    t_out,
    s_out,
    u_out,
    v_out,
):
    lane = lanes()
    for src, dst, lo in ((t_in, t_out, 3), (s_in, s_out, 3), (u_in, u_out, 2), (v_in, v_out, 2)):
        for j in range(lo, J - lo):
            store_row(dst, j, load_row(src, j))
    even = (lax.axis_index("lat") & 1) == 0
    visc = viscosity(visc_ref)
    halo_at = 2 * AUX_TRACER + 2 * AUX_FLOW

    def recv(side, n):
        e, o = e_ref[2 * n : 2 * n + 2].reshape(K, W), o_ref[2 * n : 2 * n + 2].reshape(K, W)
        return jnp.where(even, e, o) if side == 0 else jnp.where(even, o, e)

    def recv_depth(side):
        e, o = e_ref[SEND_ROWS - 1], o_ref[SEND_ROWS - 1]
        x = jnp.where(even, e, o) if side == 0 else jnp.where(even, o, e)
        return jnp.concatenate([x, x], axis=0)

    for side in (0, 1):
        edge, inward = (J - 1, J - 2) if side == 0 else (0, 1)
        wet = {j: wet_of(depth_row(ind_ref, lay_ref, j)) for j in ((12, 13, 14, 15) if side == 0 else (0, 1, 2, 3))}
        out_depth = recv_depth(side)
        wet_out = wet_of(out_depth)
        v_beyond = recv(side, 8)
        corner = recv(side, 10)
        for n, out in enumerate((t_out, s_out)):
            aux = AUX_TRACER * n
            if side == 0:
                q = {11: aux_ref[aux + 5], 12: aux_ref[aux + 6], 13: aux_ref[aux + 7], 14: aux_ref[aux + 8], 15: aux_ref[aux + 9]}
                q.update({16 + m: recv(side, 3 * n + m) for m in range(3)})
                wet[16] = wet_out
                before, faces = aux_ref[aux + 11], (13, 14, 15)
            else:
                q = {j: aux_ref[aux + j] for j in range(5)}
                q.update({-1 - m: recv(side, 3 * n + m) for m in range(3)})
                wet[-1] = wet_out
                before, faces = None, (-1, 0, 1)
            cell = merid_cell(q, faces[0])
            for j in faces:
                after = merid_cell(q, j + 1)
                c = v_beyond if j < 0 else load_row(v_ref, j)
                flux = c * wet[j] * wet[j + 1] * jnp.where(c > 0.0, out_right(cell, c), out_left(after, c))
                if before is not None:
                    store_row(out, j, q[j] - (flux - before))
                cell, before = after, flux
            if side == 1:
                store_row(out, 2, q[2] - (aux_ref[aux + 10] - before))
        halo_wet = aux_ref[halo_at + (1 if side == 0 else 0)]
        corner_depth = jnp.where(lane < W // 2, roll(corner, -2), roll(corner, 2))
        corner_wet = halo_wet * wet_of(corner_depth)
        for n, (ref, out) in enumerate(((u_ref, u_out), (v_ref, v_out))):
            base = 2 * AUX_TRACER + AUX_FLOW * n
            at = (3, 4, 5, 7, 9) if side == 0 else (0, 1, 2, 6, 8)
            lap_edge, lap_in, partial, halo_lap, halo_f = (aux_ref[base + a] for a in at)
            f, f_in = load_row(ref, edge), load_row(ref, inward)
            f_out, lap_out = recv(side, 6 + 2 * n), recv(side, 7 + 2 * n)
            step = wet[edge] * wet_out * (f_out - f)
            lap_edge = lap_edge + step
            lap_out = lap_out - step
            if n == 0:
                corner_f = corner
            else:
                corner_f = jnp.where(lane < W // 2, roll(corner, -1), roll(corner, 1))
            halo_lap = halo_lap + corner_wet * (corner_f - halo_f)
            inner_step = wet[edge] * wet[inward] * (lap_in - lap_edge)
            total = (
                zonal_lap(lap_edge, halo_lap, wet[edge], halo_wet, lane)
                + inner_step
                + wet[edge] * wet_out * (lap_out - lap_edge)
            )
            store_row(out, edge, f - visc * total)
            store_row(out, inward, f_in - visc * (partial - inner_step))


VMEM = pl.BlockSpec(memory_space=pltpu.VMEM)
SMEM = pl.BlockSpec(memory_space=pltpu.SMEM)


def call(kernel, in_specs, out_shapes, flops, *args):
    return pl.pallas_call(
        kernel,
        out_shape=[jax.ShapeDtypeStruct(s, F32) for s in out_shapes],
        in_specs=in_specs,
        out_specs=[VMEM] * len(out_shapes),
        cost_estimate=pl.CostEstimate(flops=flops, bytes_accessed=1 << 20, transcendentals=0),
        compiler_params=pltpu.CompilerParams(vmem_limit_bytes=32 << 20),
    )(*args)


def body(t, s, u, v, ind, lay, visc):
    flat = (K * J, W)
    t, s, u, v = (x.reshape(flat) for x in (t, s, u, v))
    n_lon, n_lat = lax.axis_size("lon"), lax.axis_size("lat")
    own, ev, od = call(
        pack_kernel, [VMEM] * 6, [(K, 5 * W), (K, 3 * W), (K, 3 * W)], 1 << 20, t, s, u, v, ind, lay
    )
    od = lax.ppermute(od, "lon", [(i, (((i + 1) ^ 1) - 1) % n_lon) for i in range(n_lon)])
    ev = lax.all_gather(
        ev, "lon", axis_index_groups=[[i, i + 1] for i in range(0, n_lon, 2)], tiled=True
    )
    swept, edge_e, edge_o = call(
        edge_kernel,
        [VMEM] * 9,
        [(12, K, W), (SEND_ROWS, 8, W), (SEND_ROWS, 8, W)],
        1 << 20,
        *(t, s, u, v, ind, lay, own, ev, od),
    )
    pairs_e, pairs_o = [], []
    for p in range(n_lon):
        for l in range(n_lat):
            pairs_e.append((p * n_lat + l, p * n_lat + (l ^ 1)))
            if 0 < l < n_lat - 1:
                pairs_o.append((p * n_lat + l, p * n_lat + ((l + 1) ^ 1) - 1))
        top = n_lat - 1
        pairs_o.append((p * n_lat + top, (n_lon - 1 - p) * n_lat + top))
    got_o = lax.ppermute(edge_o, ("lon", "lat"), pairs_o)
    got_e = lax.ppermute(edge_e, ("lon", "lat"), pairs_e)
    *parts, aux = call(
        inner_kernel,
        [VMEM] * 6 + [SMEM] + [VMEM] * 4,
        [flat] * 4 + [(2 * AUX_TRACER + 2 * AUX_FLOW + 2, K, W)],
        1 << 24,
        *(t, s, u, v, ind, lay, visc, own, ev, od, swept),
    )
    outs = call(
        finish_kernel,
        [VMEM] * 4 + [SMEM] + [VMEM] * 7,
        [flat] * 4,
        1 << 22,
        *(u, v, ind, lay, visc, *parts, aux, got_e, got_o),
    )
    return tuple(x.reshape(K, J, W) for x in outs)


def solution(mesh):
    field, flat = P(None, "lat", "lon"), P("lat", "lon")
    return jax.shard_map(
        body,
        mesh=mesh,
        in_specs=(field, field, field, field, flat, flat, P()),
        out_specs=(field,) * 4,
        check_vma=False,
    )
```

time: 168 us -> 42.1 us (0.25)
  starting transfers between devices: 96.6 us -> 23.4 us
  waiting for transfers between devices: 51.4 us -> 0.32 us
  Pallas kernels: 0 us -> 9.75 us
  other arithmetic: 7.97 us -> 0 us
  local copies, waits for them, and re-layouts: 9.74 us -> 5.67 us
  blocking collectives: 0 us -> 1.84 us
    ppermute x28 -> x3, starting transfers between devices: 96.6 us -> 23.4 us  [the longest x1 13.4 us: body(): lax.ppermute(od, 'lon', [(i, ((i + 1 ^ 1) - 1) % n_lon) for i in range(n_...]
    ppermute x28 -> x3, waiting for transfers between devices: 51.4 us -> 0.32 us  [the longest x1 0.31 us: body(): lax.ppermute(od, 'lon', [(i, ((i + 1 ^ 1) - 1) % n_lon) for i in range(n_...]
    pallas_call x0 -> x4, Pallas kernels: none -> 9.75 us  [call(): pl.pallas_call(kernel, out_shape=[jax.ShapeDtypeStruct(s, F32) for s in o...]
    slice x8 -> x0, local copies, waits for them, and re-layouts: 2.5 us -> none  [the longest x3 1.06 us: with_halo(): first = lax.slice_in_dim(value, 0, width, axis=dim)]
    sub x7 -> x0, other arithmetic: 2.28 us -> none  [the longest x2 0.87 us: parabolic_update(): steepness = right_final - left_final]
    all_gather x0 -> x1, blocking collectives: none -> 1.84 us  [body(): lax.all_gather(ev, 'lon', axis_index_groups=[[i, i + 1] for i in range(0,...]
    unnamed x17 -> x22, local copies, waits for them, and re-layouts: 4.72 us -> 5.67 us
  transfers between devices with their start and end apart: 28 -> 3, of which waited for: 15 -> 1; matrix products, arithmetic and copies ran while one was open for 4% -> 0% of each run, Pallas kernels for 0% -> 17%
where the time goes in v1:
time: 42.1 us; the launch traced here: 41.8 us
  starting transfers between devices  23.4 us (56%)
  Pallas kernels  9.75 us (23%)
  local copies, waits for them, and re-layouts  5.67 us (13%)
  blocking collectives  1.84 us (4%)
  between operations  0.77 us (2%)
    ppermute x1, starting transfers between devices, body(): lax.ppermute(od, 'lon', [(i, ((i + 1 ^ 1) - 1) % n_lon) for i in range(n_...  13.4 us
    pallas_call x4, Pallas kernels, call(): pl.pallas_call(kernel, out_shape=[jax.ShapeDtypeStruct(s, F32) for s in o...  9.75 us
    unnamed x22, local copies, waits for them, and re-layouts  5.67 us
    ppermute x1, starting transfers between devices, body(): got_o = lax.ppermute(edge_o, ('lon', 'lat'), pairs_o)  5.2 us
    ppermute x1, starting transfers between devices, body(): got_e = lax.ppermute(edge_e, ('lon', 'lat'), pairs_e)  4.82 us
    all_gather x1, blocking collectives, body(): lax.all_gather(ev, 'lon', axis_index_groups=[[i, i + 1] for i in range(0,...  1.84 us
  transfers between devices with their start and end apart: 3, of which 1 were waited for; matrix products, arithmetic and copies ran while one was open for 0% of the time, Pallas kernels for 17%

profile of v1, /device:TPU:6, one launch (start us, length us, event | category | flops | bytes accessed | tf_op | source)
XLA Modules:
  0.0 41.8 jit_solution(8387935849293715637)
XLA Ops:
  0.6 0.0 copy-start
  0.6 0.9 %copy-done = f32[16,16,128]{2,1,0:T(8,128)S(1)} copy-done((f32[16,16,128]{2,1,0:T(8,128)S(1)}, f32[16,16,128]{2,1,0:T(8,128)}, u32[]{:S(2)}) %copy-start) | copy-done | bytes 131096
  1.5 0.0 copy-start.2
  1.5 0.9 %copy-done.2 = f32[16,16,128]{2,1,0:T(8,128)S(1)} copy-done((f32[16,16,128]{2,1,0:T(8,128)S(1)}, f32[16,16,128]{2,1,0:T(8,128)}, u32[]{:S(2)}) %copy-start.2) | copy-done | bytes 131096
  2.4 0.0 copy-start.4
  2.4 0.9 %copy-done.4 = f32[16,16,128]{2,1,0:T(8,128)S(1)} copy-done((f32[16,16,128]{2,1,0:T(8,128)S(1)}, f32[16,16,128]{2,1,0:T(8,128)}, u32[]{:S(2)}) %copy-start.4) | copy-done | bytes 131096
  3.3 0.0 copy-start.5
  3.3 0.9 %copy-done.5 = f32[16,16,128]{2,1,0:T(8,128)S(1)} copy-done((f32[16,16,128]{2,1,0:T(8,128)S(1)}, f32[16,16,128]{2,1,0:T(8,128)}, u32[]{:S(2)}) %copy-start.5) | copy-done | bytes 131096
  4.3 0.0 copy-start.6
  4.3 0.7 %copy-done.6 = s32[16,128]{1,0:T(8,128)S(1)} copy-done((s32[16,128]{1,0:T(8,128)S(1)}, s32[16,128]{1,0:T(8,128)}, u32[]{:S(2)}) %copy-start.6) | copy-done | bytes 8216
  4.9 0.0 copy-start.8
  5.0 0.7 %copy-done.8 = s32[16,128]{1,0:T(8,128)S(1)} copy-done((s32[16,128]{1,0:T(8,128)S(1)}, s32[16,128]{1,0:T(8,128)}, u32[]{:S(2)}) %copy-start.8) | copy-done | bytes 8216
  5.6 0.3 shard_map.102
  5.9 13.4 %collective-permute-start = (f32[16,384]{1,0:T(8,128)S(1)}, f32[16,384]{1,0:T(8,128)S(1)}, u32[]{:S(2)}, u32[]{:S(2)}) collective-permute-start(f32[16,384]{1,0:T(8,128)S(1)} %get-tuple-element.21), channel_id=1, source_target_pairs={{0,504},{8,16},{16,8},{24,32},{32,24},{40,48},{48,40},{56,64},{64,... | collective-permute-start | bytes 73736 | tf_op jit(solution)/shard_map/ppermute | solution.py:476
  19.3 1.8 %all_gather.3.ev_ref = f32[32,384]{1,0:T(8,128)S(1)} all-gather(f32[16,384]{1,0:T(8,128)S(1)} %get-tuple-element.20), channel_id=1, replica_groups={{0,8},{16,24},{32,40},{48,56},{64,72},{80,88},{96,104},{112,120},{128,1..., dimensions={0}, use_global_device_ids=true | all-gather | bytes 73728 | tf_op jit(solution)/shard_map/all_gather | solution.py:477
  21.2 0.3 collective-permute-done.od_ref
  21.5 0.8 %shard_map.103 = (f32[12,16,128]{2,1,0:T(8,128)S(1)}, f32[23,8,128]{2,1,0:T(8,128)S(1)}, f32[23,8,128]{2,1,0:T(8,128)S(1)}) custom-call(f32[256,128]{1,0:T(8,128)S(1)} %bitcast.17, f32[256,128]{1,0:T(8,128)S(1)} %bitcast.20, f32[256,128]{1,0:T(8,128)S(1)} %bitcast.9, f32[256,128]{1,0:T(8,128)S(1)} %bitcast.13, s32[16,128]{1,0:T(8,128)S(1)} %copy-done.6, ...), custom_call_target="tpu_custom_call" | custom-call | flops 1048576 | bytes 1048576 | tf_op jit(solution)/shard_map/pallas_call | solution.py:459
  22.3 4.8 %collective-permute-start.1 = (f32[23,8,128]{2,1,0:T(8,128)S(1)}, f32[23,8,128]{2,1,0:T(8,128)S(1)}, u32[]{:S(2)}, u32[]{:S(2)}) collective-permute-start(f32[23,8,128]{2,1,0:T(8,128)S(1)} %get-tuple-element.28), channel_id=1, source_target_pairs={{0,1},{1,0},{2,3},{3,2},{4,5},{5,4},{6,7},{7,6},{8,9},{9,8},{10,11... | collective-permute-start | bytes 282632 | tf_op jit(solution)/shard_map/ppermute | solution.py:496
  27.1 0.0 copy-start.10
  27.1 5.2 %collective-permute-start.2 = (f32[23,8,128]{2,1,0:T(8,128)S(1)}, f32[23,8,128]{2,1,0:T(8,128)S(1)}, u32[]{:S(2)}, u32[]{:S(2)}) collective-permute-start(f32[23,8,128]{2,1,0:T(8,128)S(1)} %get-tuple-element.29), channel_id=1, source_target_pairs={{1,2},{2,1},{3,4},{4,3},{5,6},{6,5},{7,511},{9,10},{10,9},{11,12},... | collective-permute-start | bytes 282632 | tf_op jit(solution)/shard_map/ppermute | solution.py:495
  32.3 0.0 copy-done.10
  32.3 0.0 copy-start.1
  32.3 0.0 copy-start.3
  32.4 0.0 copy-start.9
  32.4 6.9 %shard_map.104 = (f32[256,128]{1,0:T(8,128)S(1)}, f32[256,128]{1,0:T(8,128)S(1)}, f32[256,128]{1,0:T(8,128)S(1)}, f32[256,128]{1,0:T(8,128)S(1)}, f32[46,16,128]{2,1,0:T(8,128)S(1)}) custom-call(f32[256,128]{1,0:T(8,128)S(1)} %bitcast.18, f32[256,128]{1,0:T(8,128)S(1)} %bitcast.21, f32[256,128]{1,0:T(8,128)S(1)} %bitcast.10, f32[256,128]{1,0:T(8,128)S(1)} %bitcast.14, ...), custom_call_target="tpu_custom_call" | custom-call | flops 16777216 | bytes 1048576 | tf_op jit(solution)/shard_map/pallas_call | solution.py:459
  39.3 0.0 copy-start.7
  39.3 0.0 collective-permute-done.1.e_ref
  39.3 0.0 collective-permute-done.2.o_ref
  39.3 0.0 copy-done.1
  39.4 0.0 copy-done.3
  39.4 0.0 copy-done.9
  39.4 0.6 %copy-done.7 = s32[16,128]{1,0:T(8,128)S(1)} copy-done((s32[16,128]{1,0:T(8,128)S(1)}, s32[16,128]{1,0:T(8,128)}, u32[]{:S(2)}) %copy-start.7) | copy-done | bytes 8216
  40.0 1.8 %shard_map.105 = (f32[256,128]{1,0:T(8,128)}, f32[256,128]{1,0:T(8,128)}, f32[256,128]{1,0:T(8,128)}, f32[256,128]{1,0:T(8,128)}) custom-call(f32[256,128]{1,0:T(8,128)S(1)} %bitcast.11, f32[256,128]{1,0:T(8,128)S(1)} %bitcast.15, s32[16,128]{1,0:T(8,128)S(1)} %copy-done.7, s32[16,128]{1,0:T(8,128)S(1)} %copy-done.9, f32[16]{0:T(128)S(1)} %copy-done.10, ...), custom_call_target="tpu_custom_call" | custom-call | flops 4194304 | bytes 1048576 | tf_op jit(solution)/shard_map/pallas_call | solution.py:459
Async XLA Ops:
  0.6 0.9 %copy-start = (f32[16,16,128]{2,1,0:T(8,128)S(1)}, f32[16,16,128]{2,1,0:T(8,128)}, u32[]{:S(2)}) copy-start(f32[16,16,128]{2,1,0:T(8,128)} %param.9) | copy-start | bytes 393220
  1.5 0.9 %copy-start.2 = (f32[16,16,128]{2,1,0:T(8,128)S(1)}, f32[16,16,128]{2,1,0:T(8,128)}, u32[]{:S(2)}) copy-start(f32[16,16,128]{2,1,0:T(8,128)} %param.10) | copy-start | bytes 393220
  2.4 0.9 %copy-start.4 = (f32[16,16,128]{2,1,0:T(8,128)S(1)}, f32[16,16,128]{2,1,0:T(8,128)}, u32[]{:S(2)}) copy-start(f32[16,16,128]{2,1,0:T(8,128)} %param.7) | copy-start | bytes 393220
  3.3 0.9 %copy-start.5 = (f32[16,16,128]{2,1,0:T(8,128)S(1)}, f32[16,16,128]{2,1,0:T(8,128)}, u32[]{:S(2)}) copy-start(f32[16,16,128]{2,1,0:T(8,128)} %param.8) | copy-start | bytes 393220
  4.3 0.7 %copy-start.6 = (s32[16,128]{1,0:T(8,128)S(1)}, s32[16,128]{1,0:T(8,128)}, u32[]{:S(2)}) copy-start(s32[16,128]{1,0:T(8,128)} %ind_ref.7) | copy-start | bytes 24580
  4.9 0.7 %copy-start.8 = (s32[16,128]{1,0:T(8,128)S(1)}, s32[16,128]{1,0:T(8,128)}, u32[]{:S(2)}) copy-start(s32[16,128]{1,0:T(8,128)} %lay_ref.7) | copy-start | bytes 24580
  5.9 15.6 %collective-permute-start = (f32[16,384]{1,0:T(8,128)S(1)}, f32[16,384]{1,0:T(8,128)S(1)}, u32[]{:S(2)}, u32[]{:S(2)}) collective-permute-start(f32[16,384]{1,0:T(8,128)S(1)} %get-tuple-element.21), channel_id=1, source_target_pairs={{0,504},{8,16},{16,8},{24,32},{32,24},{40,48},{48,40},{56,64},{64,... | collective-permute-start | bytes 73736 | tf_op jit(solution)/shard_map/ppermute | solution.py:476
  22.3 17.0 %collective-permute-start.1 = (f32[23,8,128]{2,1,0:T(8,128)S(1)}, f32[23,8,128]{2,1,0:T(8,128)S(1)}, u32[]{:S(2)}, u32[]{:S(2)}) collective-permute-start(f32[23,8,128]{2,1,0:T(8,128)S(1)} %get-tuple-element.28), channel_id=1, source_target_pairs={{0,1},{1,0},{2,3},{3,2},{4,5},{5,4},{6,7},{7,6},{8,9},{9,8},{10,11... | collective-permute-start | bytes 282632 | tf_op jit(solution)/shard_map/ppermute | solution.py:496
  27.1 5.2 %copy-start.10 = (f32[16]{0:T(128)S(1)}, f32[16]{0:T(128)}, u32[]{:S(2)}) copy-start(f32[16]{0:T(128)} %visc_ref.3) | copy-start | bytes 196
  27.1 12.2 %collective-permute-start.2 = (f32[23,8,128]{2,1,0:T(8,128)S(1)}, f32[23,8,128]{2,1,0:T(8,128)S(1)}, u32[]{:S(2)}, u32[]{:S(2)}) collective-permute-start(f32[23,8,128]{2,1,0:T(8,128)S(1)} %get-tuple-element.29), channel_id=1, source_target_pairs={{1,2},{2,1},{3,4},{4,3},{5,6},{6,5},{7,511},{9,10},{10,9},{11,12},... | collective-permute-start | bytes 282632 | tf_op jit(solution)/shard_map/ppermute | solution.py:495
  32.3 7.0 %copy-start.1 = (f32[16,16,128]{2,1,0:T(8,128)S(1)}, f32[16,16,128]{2,1,0:T(8,128)}, u32[]{:S(2)}) copy-start(f32[16,16,128]{2,1,0:T(8,128)} %param.9) | copy-start | bytes 393220
  32.3 7.0 %copy-start.3 = (f32[16,16,128]{2,1,0:T(8,128)S(1)}, f32[16,16,128]{2,1,0:T(8,128)}, u32[]{:S(2)}) copy-start(f32[16,16,128]{2,1,0:T(8,128)} %param.10) | copy-start | bytes 393220
  32.4 7.0 %copy-start.9 = (s32[16,128]{1,0:T(8,128)S(1)}, s32[16,128]{1,0:T(8,128)}, u32[]{:S(2)}) copy-start(s32[16,128]{1,0:T(8,128)} %lay_ref.7) | copy-start | bytes 24580
  39.3 0.7 %copy-start.7 = (s32[16,128]{1,0:T(8,128)S(1)}, s32[16,128]{1,0:T(8,128)}, u32[]{:S(2)}) copy-start(s32[16,128]{1,0:T(8,128)} %ind_ref.7) | copy-start | bytes 24580

commit v2 on v1

v2 whole, which is shorter than its diff:
```python
import jax
import jax.numpy as jnp
from jax import lax
from jax.experimental import pallas as pl
from jax.experimental.pallas import tpu as pltpu
from jax.sharding import PartitionSpec as P

K, J, W = 16, 16, 128
WIN = 6
SEND_ROWS = 23
F32 = jnp.float32


def lanes():
    return lax.broadcasted_iota(jnp.int32, (K, W), 1)


def levels():
    return lax.broadcasted_iota(jnp.int32, (K, W), 0).astype(F32)


def low_half(lane):
    return lane - WIN * ((lane * 43) >> 8) < WIN // 2


def roll(x, shift):
    shift %= W
    return x if shift == 0 else pltpu.roll(x, shift, 1)


def load_row(ref, j):
    return ref[pl.ds(j, K, stride=J), :]


def store_row(ref, j, value):
    ref[pl.ds(j, K, stride=J), :] = value


def depth_row(depth_ref, j):
    return jnp.broadcast_to(depth_ref[pl.ds(j, 1), :], (K, W))


def wet_of(depth):
    return jnp.where(levels() < depth, 1.0, 0.0).astype(F32)


def unpack(packed, j):
    return roll(packed, -(WIN * j + 3))


def east(x, halo, lane):
    return roll(jnp.where(lane < 1, halo, x), -1)


def west(x, halo, lane):
    return roll(jnp.where(lane == W - 1, halo, x), 1)


def minmod(a, b):
    return jnp.maximum(jnp.minimum(a, jnp.maximum(b, 0.0)), jnp.minimum(b, 0.0))


def rise_fall(before, here, after):
    rise = minmod(0.5 * here + (1.0 / 12.0) * (before - after), here)
    return rise, here - rise


def limited(fall, rise):
    return minmod(fall, rise + rise), minmod(rise, fall + fall)


def weights(c):
    size = jnp.abs(c)
    rest = 1.0 - size
    return size * rest, rest * rest


def pack_columns(rows):
    lane = lanes()
    packed = jnp.zeros((K, W), F32)
    for j, row in enumerate(rows):
        mine = (lane >= WIN * j) & (lane < WIN * j + WIN)
        packed = jnp.where(mine, roll(row, WIN * j + 3), packed)
    return packed


def pack_kernel(*refs):
    sources, (t_ref, s_ref, u_ref, v_ref, d_ref, own_ref, ev_ref, od_ref) = refs[:6], refs[6:14]
    ind_ref, lay_ref, sems = refs[14:]
    copies = [
        pltpu.make_async_copy(src, dst, sems.at[n])
        for n, (src, dst) in enumerate(zip(sources, (t_ref, s_ref, u_ref, v_ref, ind_ref, lay_ref)))
    ]
    for n in (4, 5, 0, 1, 2, 3):
        copies[n].start()
    copies[4].wait()
    copies[5].wait()
    d_ref[...] = (ind_ref[...] * lay_ref[...]).astype(F32)
    d = pack_columns([depth_row(d_ref, j) for j in range(J)])
    fields = []
    for n, ref in enumerate((t_ref, s_ref, u_ref, v_ref)):
        copies[n].wait()
        fields.append(pack_columns([load_row(ref, j) for j in range(J)]))
    fields.insert(3, d)
    for n, x in enumerate(fields):
        own_ref[:, n * W : (n + 1) * W] = x
    t, s, u, d, v = fields
    low = low_half(lanes())
    even = (lax.axis_index("lon") & 1) == 0
    for n, (a, b) in enumerate(((t, s), (u, d), (v, v))):
        to_east = jnp.where(low, a, roll(b, 3))
        to_west = jnp.where(low, roll(b, -3), a)
        at = slice(n * W, (n + 1) * W)
        ev_ref[:, at] = jnp.where(even, to_east, to_west)
        od_ref[:, at] = jnp.where(even, to_west, to_east)


def seams(own_ref, ev_ref, od_ref):
    low = low_half(lanes())
    even = (lax.axis_index("lon") & 1) == 0
    mate = pl.multiple_of(jnp.where(even, K, 0), K)
    out = []
    for n in range(5):
        at = slice((n // 2) * W, (n // 2 + 1) * W)
        ev = ev_ref[pl.ds(mate, K), at]
        od = od_ref[:, at]
        from_west = jnp.where(even, od, ev)
        from_east = jnp.where(even, ev, od)
        if n in (1, 3):
            from_west, from_east = roll(from_west, -3), roll(from_east, 3)
        own = own_ref[:, n * W : (n + 1) * W]
        out.append(
            (
                jnp.where(low, from_west, from_east),
                jnp.where(low, from_west, own),
                jnp.where(low, own, from_east),
            )
        )
    return out


def seam_flux(q, c, wet):
    step = roll(q, -1) - q
    rise, fall = rise_fall(roll(step, 1), step, roll(step, -1))
    down, up = limited(roll(fall, 1), rise)
    near, far = weights(c)
    out_right = q + (near * down + far * up)
    near, far = weights(roll(c, 1))
    out_left = q - (near * up + far * down)
    return fall, c * wet * roll(wet, -1) * jnp.where(c > 0.0, out_right, roll(out_left, -1))


class Zonal:
    def __init__(self, packs, u_ref, d_ref):
        self.packs, self.u_ref, self.d_ref = packs, u_ref, d_ref
        lane = lanes()
        third = lane - WIN * ((lane * 43) >> 8) == 2
        _, uw, ue = packs[2]
        _, dw, de = packs[3]
        ww, we = wet_of(dw), wet_of(de)
        self.fix = []
        for n in range(2):
            fall_w, flux_w = seam_flux(packs[n][1], uw, ww)
            _, flux_e = seam_flux(packs[n][2], ue, we)
            self.fix.append((jnp.where(third, flux_e, roll(fall_w, 1)), flux_w))

    def row(self, refs, j):
        lane = lanes()
        last = lane == W - 1
        u = load_row(self.u_ref, j)
        wet = wet_of(depth_row(self.d_ref, j))
        halo_wet = wet_of(unpack(self.packs[3][0], j))
        near, far = weights(u)
        near_w, far_w = weights(west(u, unpack(self.packs[2][0], j), lane))
        face = u * wet * east(wet, halo_wet, lane)
        forward = u > 0.0
        out = []
        for n, ref in enumerate(refs):
            q = load_row(ref, j)
            halo = unpack(self.packs[n][0], j)
            fix, flux_in = (unpack(x, j) for x in self.fix[n])
            right = east(q, halo, lane)
            rise, fall = rise_fall(
                q - west(q, halo, lane),
                right - q,
                roll(jnp.where(lane < 2, halo, q), -2) - right,
            )
            down, up = limited(jnp.where(lane == 0, fix, roll(fall, 1)), rise)
            flux = face * jnp.where(
                forward, q + (near * down + far * up), roll(q - (near_w * up + far_w * down), -1)
            )
            flux_west = roll(jnp.where(last, flux_in, flux), 1)
            out.append(q - (jnp.where(last, fix, flux) - flux_west))
        return out


def zonal_masks(wet, halo_wet, lane):
    return wet * east(wet, halo_wet, lane), wet * west(wet, halo_wet, lane)


def zonal_lap(f, halo, masks, lane):
    return masks[0] * (east(f, halo, lane) - f) - masks[1] * (f - west(f, halo, lane))


def seam_lap(f, wet):
    total = None
    for shift in (1, -1, WIN, -WIN):
        term = wet * roll(wet, shift) * (roll(f, shift) - f)
        total = term if total is None else total + term
    return total


def edge_kernel(
    t_ref, s_ref, u_ref, v_ref, d_ref, own_ref, ev_ref, od_ref, swept_ref, e_ref, o_ref
):
    lane = lanes()
    packs = seams(own_ref, ev_ref, od_ref)
    zonal = Zonal(packs, u_ref, d_ref)
    halves = []
    for rows in ((J - 1, J - 2, J - 3), (0, 1, 2)):
        planes = [zonal.row((t_ref, s_ref), j) for j in rows]
        for j, (t, s) in zip(rows, planes):
            swept_ref[j if j < 3 else j - 10] = t
            swept_ref[6 + (j if j < 3 else j - 10)] = s
        half = [p[0] for p in planes] + [p[1] for p in planes]
        j, inward = rows[0], rows[1]
        depth = depth_row(d_ref, j)
        halo_depth = unpack(packs[3][0], j)
        wet, halo_wet = wet_of(depth), wet_of(halo_depth)
        masks = zonal_masks(wet, halo_wet, lane)
        to_inner = wet * wet_of(depth_row(d_ref, inward))
        corner = roll(halo_depth, 2)
        corner = jnp.where(lane < W // 2, corner, roll(halo_depth, -2))
        for ref, pack, reach in ((v_ref, packs[4], 1), (u_ref, packs[2], 0)):
            halo = unpack(pack[0], j)
            f = load_row(ref, j)
            partial = zonal_lap(f, halo, masks, lane) + to_inner * (load_row(ref, inward) - f)
            half[6:6] = [f, partial]
            take = jnp.where(lane < W // 2, roll(halo, reach), roll(halo, -reach))
            corner = jnp.where((lane == reach) | (lane == W - 1 - reach), take, corner)
        halves.append((half + [corner], depth[:8]))
    lat = lax.axis_index("lat")
    even = (lat & 1) == 0
    top = lat == lax.axis_size("lat") - 1
    (north, north_d), (south, south_d) = halves
    for n, (a, b) in enumerate(zip(north, south)):
        e_ref[2 * n : 2 * n + 2] = jnp.where(even, a, b).reshape(2, 8, W)
        o_ref[2 * n : 2 * n + 2] = jnp.where(even, b, a).reshape(2, 8, W)
    e_ref[SEND_ROWS - 1] = jnp.where(even, north_d, south_d)
    o_ref[SEND_ROWS - 1] = jnp.where(even, south_d, north_d)

    @pl.when(top)
    def _():
        mirror = W - 1 - lax.broadcasted_iota(jnp.int32, (8, W), 1)
        lane8 = lax.broadcasted_iota(jnp.int32, (8, W), 1)
        for n in range(SEND_ROWS):
            x = jnp.take_along_axis(o_ref[n], mirror, axis=1)
            if 12 <= n < 20:
                x = -x
            elif 20 <= n < 22:
                x = jnp.where((lane8 < 2) | (lane8 > W - 3), -x, x)
            o_ref[n] = x


def merid_cell(step, fall_before, j):
    rise, fall = rise_fall(step[j - 1], step[j], step[j + 1])
    down, up = limited(fall_before, rise)
    return down, up, fall


def merid_flux(c, wet_pair, q, q_next, cell, cell_next):
    forward = c > 0.0
    rest = 1.0 - jnp.abs(c)
    square = rest * rest
    near = jnp.where(forward, cell[0], cell_next[1])
    far = jnp.where(forward, cell[1], cell_next[0])
    return c * wet_pair * (
        jnp.where(forward, q, q_next) + (c * rest * near + jnp.where(forward, square, -square) * far)
    )


AUX_TRACER, AUX_FLOW = 12, 10


def inner_kernel(
    t_ref,
    s_ref,
    u_ref,
    v_ref,
    d_ref,
    visc_hbm,
    own_ref,
    ev_ref,
    od_ref,
    swept_ref,
    t_out,
    s_out,
    u_out,
    v_out,
    aux_ref,
    visc_ref,
    sem,
):
    copy = pltpu.make_async_copy(visc_hbm, visc_ref, sem)
    copy.start()
    lane = lanes()
    packs = seams(own_ref, ev_ref, od_ref)
    zonal = Zonal(packs, u_ref, d_ref)
    rows = [{}, {}]
    for j in (0, 1, 2, 13, 14, 15):
        for n in range(2):
            rows[n][j] = swept_ref[6 * n + (j if j < 3 else j - 10)]
    for j in range(3, 13):
        rows[0][j], rows[1][j] = zonal.row((t_ref, s_ref), j)
    wet = [wet_of(depth_row(d_ref, j)) for j in range(J)]
    for n, out in enumerate((t_out, s_out)):
        q = rows[n]
        for at, j in enumerate((0, 1, 2, 3, 4, 11, 12, 13, 14, 15)):
            aux_ref[AUX_TRACER * n + at] = q[j]
        step = [q[j + 1] - q[j] for j in range(J - 1)]
        cell = merid_cell(step, rise_fall(step[0], step[1], step[2])[1], 2)
        before = None
        for j in range(2, 13):
            after = merid_cell(step, cell[2], j + 1)
            flux = merid_flux(load_row(v_ref, j), wet[j] * wet[j + 1], q[j], q[j + 1], cell, after)
            if j == 2:
                aux_ref[AUX_TRACER * n + 10] = flux
            else:
                store_row(out, j, q[j] - (flux - before))
            if j == 12:
                aux_ref[AUX_TRACER * n + 11] = flux
            cell, before = after, flux
    wet_w, wet_e = wet_of(packs[3][1]), wet_of(packs[3][2])
    low = low_half(lane)
    copy.wait()
    visc = viscosity(visc_ref)
    halo_wet = [wet_of(unpack(packs[3][0], j)) for j in range(J)]
    masks = [zonal_masks(wet[j], halo_wet[j], lane) for j in range(J)]
    pair = [wet[j] * wet[j + 1] for j in range(J - 1)]
    for n, (ref, pack, out) in enumerate(((u_ref, packs[2], u_out), (v_ref, packs[4], v_out))):
        base = 2 * AUX_TRACER + AUX_FLOW * n
        halo_lap = jnp.where(low, seam_lap(pack[1], wet_w), seam_lap(pack[2], wet_e))
        f = [load_row(ref, j) for j in range(J)]
        lap = []
        step = None
        for j in range(J):
            total = zonal_lap(f[j], unpack(pack[0], j), masks[j], lane)
            if step is not None:
                total = total - step
            if j < J - 1:
                step = pair[j] * (f[j + 1] - f[j])
                total = total + step
            lap.append(total)
        step = None
        for j in range(1, J - 1):
            total = zonal_lap(lap[j], unpack(halo_lap, j), masks[j], lane)
            if step is not None:
                total = total - step
            if j < J - 2:
                step = pair[j] * (lap[j + 1] - lap[j])
                total = total + step
            if j == 1:
                aux_ref[base + 2] = total
            elif j == J - 2:
                aux_ref[base + 5] = total
            else:
                store_row(out, j, f[j] - visc * total)
        aux_ref[base + 0] = lap[0]
        aux_ref[base + 1] = lap[1]
        aux_ref[base + 3] = lap[J - 1]
        aux_ref[base + 4] = lap[J - 2]
        aux_ref[base + 6] = unpack(halo_lap, 0)
        aux_ref[base + 7] = unpack(halo_lap, J - 1)
        aux_ref[base + 8] = unpack(pack[0], 0)
        aux_ref[base + 9] = unpack(pack[0], J - 1)
    aux_ref[2 * AUX_TRACER + 2 * AUX_FLOW] = halo_wet[0]
    aux_ref[2 * AUX_TRACER + 2 * AUX_FLOW + 1] = halo_wet[J - 1]
    aux_ref[2 * AUX_TRACER + 2 * AUX_FLOW + 2] = visc


def viscosity(visc_ref):
    level = lax.broadcasted_iota(jnp.int32, (K, W), 0)
    visc = jnp.zeros((K, W), F32)
    for k in range(K):
        visc = jnp.where(level == k, visc_ref[k], visc)
    return visc


def finish_kernel(
    u_ref, v_ref, d_ref, t_in, s_in, u_in, v_in, aux_ref, e_ref, o_ref, *outs
):
    finals, (t_out, s_out, u_out, v_out), sems = outs[:4], outs[4:8], outs[8]
    lane = lanes()
    copies = [
        pltpu.make_async_copy(src, dst, sems.at[n])
        for n, (src, dst) in enumerate(zip((t_out, s_out, u_out, v_out), finals))
    ]
    even = (lax.axis_index("lat") & 1) == 0
    halo_at = 2 * AUX_TRACER + 2 * AUX_FLOW
    visc = aux_ref[halo_at + 2]

    def recv(side, n):
        e, o = e_ref[2 * n : 2 * n + 2].reshape(K, W), o_ref[2 * n : 2 * n + 2].reshape(K, W)
        return jnp.where(even, e, o) if side == 0 else jnp.where(even, o, e)

    def recv_depth(side):
        e, o = e_ref[SEND_ROWS - 1], o_ref[SEND_ROWS - 1]
        x = jnp.where(even, e, o) if side == 0 else jnp.where(even, o, e)
        return jnp.concatenate([x, x], axis=0)

    wet = {j: wet_of(depth_row(d_ref, j)) for j in (0, 1, 2, 13, 14, 15)}
    wet[16], wet[-1] = wet_of(recv_depth(0)), wet_of(recv_depth(1))
    courant = {j: load_row(v_ref, j) for j in (0, 1, 13, 14, 15)}
    courant[-1] = recv(1, 8)
    for n, (src, out) in enumerate(((t_in, t_out), (s_in, s_out))):
        aux = AUX_TRACER * n
        for j in range(3, 13):
            store_row(out, j, load_row(src, j))
        for side in (0, 1):
            if side == 0:
                q = {11 + m: aux_ref[aux + 5 + m] for m in range(5)}
                q.update({16 + m: recv(side, 3 * n + m) for m in range(3)})
                before, faces = aux_ref[aux + 11], (13, 14, 15)
            else:
                q = {j: aux_ref[aux + j] for j in range(5)}
                q.update({-1 - m: recv(side, 3 * n + m) for m in range(3)})
                before, faces = None, (-1, 0, 1)
            step = {j: q[j + 1] - q[j] for j in q if j + 1 in q}
            first = faces[0]
            fall = rise_fall(step[first - 2], step[first - 1], step[first])[1]
            cell = merid_cell(step, fall, first)
            for j in faces:
                after = merid_cell(step, cell[2], j + 1)
                flux = merid_flux(courant[j], wet[j] * wet[j + 1], q[j], q[j + 1], cell, after)
                if before is not None:
                    store_row(out, j, q[j] - (flux - before))
                cell, before = after, flux
            if side == 1:
                store_row(out, 2, q[2] - (aux_ref[aux + 10] - before))
        copies[n].start()
    for n, (ref, src, out) in enumerate(((u_ref, u_in, u_out), (v_ref, v_in, v_out))):
        base = 2 * AUX_TRACER + AUX_FLOW * n
        for j in range(2, 14):
            store_row(out, j, load_row(src, j))
        for side in (0, 1):
            edge, inward, beyond = (15, 14, 16) if side == 0 else (0, 1, -1)
            halo_wet = aux_ref[halo_at + 1 - side]
            corner = recv(side, 10)
            corner_depth = jnp.where(lane < W // 2, roll(corner, -2), roll(corner, 2))
            corner_wet = halo_wet * wet_of(corner_depth)
            masks = zonal_masks(wet[edge], halo_wet, lane)
            at = (3, 4, 5, 7, 9) if side == 0 else (0, 1, 2, 6, 8)
            lap_edge, lap_in, partial, halo_lap, halo_f = (aux_ref[base + a] for a in at)
            f, f_in = load_row(ref, edge), load_row(ref, inward)
            f_out, lap_out = recv(side, 6 + 2 * n), recv(side, 7 + 2 * n)
            across = wet[edge] * wet[beyond]
            step = across * (f_out - f)
            lap_edge = lap_edge + step
            lap_out = lap_out - step
            if n == 0:
                corner_f = corner
            else:
                corner_f = jnp.where(lane < W // 2, roll(corner, -1), roll(corner, 1))
            halo_lap = halo_lap + corner_wet * (corner_f - halo_f)
            inner_step = wet[edge] * wet[inward] * (lap_in - lap_edge)
            total = (
                zonal_lap(lap_edge, halo_lap, masks, lane)
                + inner_step
                + across * (lap_out - lap_edge)
            )
            store_row(out, edge, f - visc * total)
            store_row(out, inward, f_in - visc * (partial - inner_step))
        copies[2 + n].start()
    for copy in copies:
        copy.wait()


VMEM = pl.BlockSpec(memory_space=pltpu.VMEM)
HBM = pl.BlockSpec(memory_space=pltpu.HBM)
FLAT = (K * J, W)
AUX = 2 * AUX_TRACER + 2 * AUX_FLOW + 3


def call(kernel, in_specs, out_specs, out_shapes, flops, args, scratch=()):
    return pl.pallas_call(
        kernel,
        out_shape=[jax.ShapeDtypeStruct(s, F32) for s in out_shapes],
        in_specs=in_specs,
        out_specs=out_specs,
        scratch_shapes=list(scratch),
        cost_estimate=pl.CostEstimate(flops=flops, bytes_accessed=1 << 20, transcendentals=0),
        compiler_params=pltpu.CompilerParams(vmem_limit_bytes=32 << 20),
    )(*args)


def body(t, s, u, v, ind, lay, visc):
    t, s, u, v = (x.reshape(FLAT) for x in (t, s, u, v))
    n_lon, n_lat = lax.axis_size("lon"), lax.axis_size("lat")
    t, s, u, v, depth, own, ev, od = call(
        pack_kernel,
        [HBM] * 6,
        [VMEM] * 8,
        [FLAT] * 4 + [(J, W), (K, 5 * W), (K, 3 * W), (K, 3 * W)],
        1 << 20,
        (t, s, u, v, ind, lay),
        [pltpu.VMEM((J, W), jnp.int32)] * 2 + [pltpu.SemaphoreType.DMA((6,))],
    )
    od = lax.ppermute(od, "lon", [(i, (((i + 1) ^ 1) - 1) % n_lon) for i in range(n_lon)])
    ev = lax.all_gather(
        ev, "lon", axis_index_groups=[[i, i + 1] for i in range(0, n_lon, 2)], tiled=True
    )
    swept, edge_e, edge_o = call(
        edge_kernel,
        [VMEM] * 8,
        [VMEM] * 3,
        [(12, K, W), (SEND_ROWS, 8, W), (SEND_ROWS, 8, W)],
        1 << 20,
        (t, s, u, v, depth, own, ev, od),
    )
    pairs_e, pairs_o = [], []
    top = n_lat - 1
    for p in range(n_lon):
        for l in range(n_lat):
            pairs_e.append((p * n_lat + l, p * n_lat + (l ^ 1)))
            if 0 < l < top:
                pairs_o.append((p * n_lat + l, p * n_lat + ((l + 1) ^ 1) - 1))
        pairs_o.append((p * n_lat + top, (n_lon - 1 - p) * n_lat + top))
    got_o = lax.ppermute(edge_o, ("lon", "lat"), pairs_o)
    got_e = lax.ppermute(edge_e, ("lon", "lat"), pairs_e)
    *parts, aux = call(
        inner_kernel,
        [VMEM] * 5 + [HBM] + [VMEM] * 4,
        [VMEM] * 5,
        [FLAT] * 4 + [(AUX, K, W)],
        1 << 24,
        (t, s, u, v, depth, visc, own, ev, od, swept),
        [pltpu.SMEM((K,), F32), pltpu.SemaphoreType.DMA],
    )
    outs = call(
        finish_kernel,
        [VMEM] * 10,
        [HBM] * 4,
        [FLAT] * 4,
        1 << 22,
        (u, v, depth, *parts, aux, got_e, got_o),
        [pltpu.VMEM(FLAT, F32)] * 4 + [pltpu.SemaphoreType.DMA((4,))],
    )
    return tuple(x.reshape(K, J, W) for x in outs)


def solution(mesh):
    field, flat = P(None, "lat", "lon"), P("lat", "lon")
    return jax.shard_map(
        body,
        mesh=mesh,
        in_specs=(field, field, field, field, flat, flat, P()),
        out_specs=(field,) * 4,
        check_vma=False,
    )
```

time: 42.1 us -> 41 us (0.974)
  Pallas kernels: 9.75 us -> 7.69 us
  waiting for transfers between devices: 0.32 us -> 1.97 us
  local copies, waits for them, and re-layouts: 5.67 us -> 5.01 us
    pallas_call x4, Pallas kernels: 9.75 us -> 7.69 us  [call(): pl.pallas_call(kernel, out_shape=[jax.ShapeDtypeStruct(s, F32) for s in o...]
    ppermute x1, waiting for transfers between devices: 0.01 us -> 1.66 us  [body(): got_o = lax.ppermute(edge_o, ('lon', 'lat'), pairs_o)]
    unnamed x22 -> x14, local copies, waits for them, and re-layouts: 5.67 us -> 5.01 us
  transfers between devices with their start and end apart: 3 -> 3, of which waited for: 1 -> 2; matrix products, arithmetic and copies ran while one was open for 0% -> 0% of each run, Pallas kernels for 17% -> 11%
where the time goes in v2:
time: 41 us; the launch traced here: 40.7 us
  starting transfers between devices  23.4 us (57%)
  Pallas kernels  7.69 us (19%)
  local copies, waits for them, and re-layouts  5.01 us (12%)
  waiting for transfers between devices  1.97 us (5%)
  blocking collectives  1.84 us (4%)
  between operations  0.72 us (2%)
    ppermute x1, starting transfers between devices, body(): lax.ppermute(od, 'lon', [(i, ((i + 1 ^ 1) - 1) % n_lon) for i in range(n_...  13.4 us
    pallas_call x4, Pallas kernels, call(): pl.pallas_call(kernel, out_shape=[jax.ShapeDtypeStruct(s, F32) for s in o...  7.69 us
    ppermute x1, starting transfers between devices, body(): got_o = lax.ppermute(edge_o, ('lon', 'lat'), pairs_o)  5.2 us
    unnamed x14, local copies, waits for them, and re-layouts  5.01 us
    ppermute x1, starting transfers between devices, body(): got_e = lax.ppermute(edge_e, ('lon', 'lat'), pairs_e)  4.82 us
    all_gather x1, blocking collectives, body(): lax.all_gather(ev, 'lon', axis_index_groups=[[i, i + 1] for i in range(0,...  1.84 us
    ppermute x1, waiting for transfers between devices, body(): got_o = lax.ppermute(edge_o, ('lon', 'lat'), pairs_o)  1.66 us
  transfers between devices with their start and end apart: 3, of which 2 were waited for; matrix products, arithmetic and copies ran while one was open for 0% of the time, Pallas kernels for 11%

profile of v2, /device:TPU:6, one launch (start us, length us, event | category | flops | bytes accessed | tf_op | source)
XLA Modules:
  0.0 40.7 jit_solution(2093757627356908632)
XLA Ops:
  0.6 0.0 copy-start
  0.6 0.9 %copy-done = f32[16,16,128]{2,1,0:T(8,128)S(1)} copy-done((f32[16,16,128]{2,1,0:T(8,128)S(1)}, f32[16,16,128]{2,1,0:T(8,128)}, u32[]{:S(2)}) %copy-start) | copy-done | bytes 131096
  1.5 0.0 copy-start.1
  1.5 0.9 %copy-done.1 = f32[16,16,128]{2,1,0:T(8,128)S(1)} copy-done((f32[16,16,128]{2,1,0:T(8,128)S(1)}, f32[16,16,128]{2,1,0:T(8,128)}, u32[]{:S(2)}) %copy-start.1) | copy-done | bytes 131096
  2.4 0.0 copy-start.2
  2.4 0.9 %copy-done.2 = f32[16,16,128]{2,1,0:T(8,128)S(1)} copy-done((f32[16,16,128]{2,1,0:T(8,128)S(1)}, f32[16,16,128]{2,1,0:T(8,128)}, u32[]{:S(2)}) %copy-start.2) | copy-done | bytes 131096
  3.3 0.0 copy-start.3
  3.3 0.9 %copy-done.3 = f32[16,16,128]{2,1,0:T(8,128)S(1)} copy-done((f32[16,16,128]{2,1,0:T(8,128)S(1)}, f32[16,16,128]{2,1,0:T(8,128)}, u32[]{:S(2)}) %copy-start.3) | copy-done | bytes 131096
  4.3 0.0 copy-start.4
  4.3 0.7 %copy-done.4 = s32[16,128]{1,0:T(8,128)S(1)} copy-done((s32[16,128]{1,0:T(8,128)S(1)}, s32[16,128]{1,0:T(8,128)}, u32[]{:S(2)}) %copy-start.4) | copy-done | bytes 8216
  4.9 0.0 copy-start.5
  5.0 0.7 %copy-done.5 = s32[16,128]{1,0:T(8,128)S(1)} copy-done((s32[16,128]{1,0:T(8,128)S(1)}, s32[16,128]{1,0:T(8,128)}, u32[]{:S(2)}) %copy-start.5) | copy-done | bytes 8216
  5.6 1.3 %shard_map.102 = (f32[256,128]{1,0:T(8,128)S(1)}, f32[256,128]{1,0:T(8,128)S(1)}, f32[256,128]{1,0:T(8,128)S(1)}, f32[256,128]{1,0:T(8,128)S(1)}, f32[16,128]{1,...) custom-call(f32[256,128]{1,0:T(8,128)S(1)} %bitcast.8, ...), custom_call_target="tpu_custom_call" | custom-call | flops 1048576 | bytes 1048576 | tf_op jit(solution)/shard_map/pallas_call | solution.py:485
  7.0 13.4 %collective-permute-start = (f32[16,384]{1,0:T(8,128)S(1)}, f32[16,384]{1,0:T(8,128)S(1)}, u32[]{:S(2)}, u32[]{:S(2)}) collective-permute-start(f32[16,384]{1,0:T(8,128)S(1)} %get-tuple-element.31), channel_id=1, source_target_pairs={{0,504},{8,16},{16,8},{24,32},{32,24},{40,48},{48,40},{56,64},{64,... | collective-permute-start | bytes 73736 | tf_op jit(solution)/shard_map/ppermute | solution.py:508
  20.4 1.8 %all_gather.3.ev_ref = f32[32,384]{1,0:T(8,128)S(1)} all-gather(f32[16,384]{1,0:T(8,128)S(1)} %get-tuple-element.30), channel_id=1, replica_groups={{0,8},{16,24},{32,40},{48,56},{64,72},{80,88},{96,104},{112,120},{128,1..., dimensions={0}, use_global_device_ids=true | all-gather | bytes 73728 | tf_op jit(solution)/shard_map/all_gather | solution.py:509
  22.2 0.3 collective-permute-done.od_ref
  22.6 0.8 %shard_map.103 = (f32[12,16,128]{2,1,0:T(8,128)S(1)}, f32[23,8,128]{2,1,0:T(8,128)S(1)}, f32[23,8,128]{2,1,0:T(8,128)S(1)}) custom-call(f32[256,128]{1,0:T(8,128)S(1)} %get-tuple-element.27.t_ref, f32[256,128]{1,0:T(8,128)S(1)} %get-tuple-element.28.s_ref, f32[256,128]{1,0:T(8,128)S(1)} %get-tuple-element.24.u_ref, f32[256,128]{1,0:T(8,128)S(1)} %get-tuple-element.25.v_ref, ...), custom_call_target="tpu_custom_call" | custom-call | flops 1048576 | bytes 1048576 | tf_op jit(solution)/shard_map/pallas_call | solution.py:485
  23.4 4.8 %collective-permute-start.1 = (f32[23,8,128]{2,1,0:T(8,128)S(1)}, f32[23,8,128]{2,1,0:T(8,128)S(1)}, u32[]{:S(2)}, u32[]{:S(2)}) collective-permute-start(f32[23,8,128]{2,1,0:T(8,128)S(1)} %get-tuple-element.38), channel_id=1, source_target_pairs={{0,1},{1,0},{2,3},{3,2},{4,5},{5,4},{6,7},{7,6},{8,9},{9,8},{10,11... | collective-permute-start | bytes 282632 | tf_op jit(solution)/shard_map/ppermute | solution.py:529
  28.2 0.0 copy-start.6
  28.2 5.2 %collective-permute-start.2 = (f32[23,8,128]{2,1,0:T(8,128)S(1)}, f32[23,8,128]{2,1,0:T(8,128)S(1)}, u32[]{:S(2)}, u32[]{:S(2)}) collective-permute-start(f32[23,8,128]{2,1,0:T(8,128)S(1)} %get-tuple-element.39), channel_id=1, source_target_pairs={{1,2},{2,1},{3,4},{4,3},{5,6},{6,5},{7,511},{9,10},{10,9},{11,12},... | collective-permute-start | bytes 282632 | tf_op jit(solution)/shard_map/ppermute | solution.py:528
  33.4 0.0 copy-done.6
  33.4 4.4 %shard_map.104 = (f32[256,128]{1,0:T(8,128)S(1)}, f32[256,128]{1,0:T(8,128)S(1)}, f32[256,128]{1,0:T(8,128)S(1)}, f32[256,128]{1,0:T(8,128)S(1)}, f32[47,16,128]{2,1,0:T(8,128)S(1)}) custom-call(f32[256,128]{1,0:T(8,128)S(1)} %get-tuple-element.27.t_ref, f32[256,128]{1,0:T(8,128)S(1)} %get-tuple-element.28.s_ref, f32[256,128]{1,0:T(8,128)S(1)} %get-tuple-element.24.u_ref, ...), custom_call_target="tpu_custom_call" | custom-call | flops 16777216 | bytes 1048576 | tf_op jit(solution)/shard_map/pallas_call | solution.py:485
  37.8 0.0 collective-permute-done.1.e_ref
  37.8 1.7 %collective-permute-done.2.o_ref = f32[23,8,128]{2,1,0:T(8,128)S(1)} collective-permute-done((f32[23,8,128]{2,1,0:T(8,128)S(1)}, f32[23,8,128]{2,1,0:T(8,128)S(1)}, u32[]{:S(2)}, u32[]{:S(2)}) %collective-permute-start.2) | collective-permute-done | bytes 94240 | tf_op jit(solution)/shard_map/ppermute | solution.py:528
  39.5 1.2 %shard_map.105 = (f32[256,128]{1,0:T(8,128)}, f32[256,128]{1,0:T(8,128)}, f32[256,128]{1,0:T(8,128)}, f32[256,128]{1,0:T(8,128)}) custom-call(f32[256,128]{1,0:T(8,128)S(1)} %get-tuple-element.24.u_ref, f32[256,128]{1,0:T(8,128)S(1)} %get-tuple-element.25.v_ref, f32[16,128]{1,0:T(8,128)S(1)} %get-tuple-element.26.d_ref, ...), custom_call_target="tpu_custom_call" | custom-call | flops 4194304 | bytes 1048576 | tf_op jit(solution)/shard_map/pallas_call | solution.py:485
Async XLA Ops:
  0.6 0.9 %copy-start = (f32[16,16,128]{2,1,0:T(8,128)S(1)}, f32[16,16,128]{2,1,0:T(8,128)}, u32[]{:S(2)}) copy-start(f32[16,16,128]{2,1,0:T(8,128)} %param.7) | copy-start | bytes 393220
  1.5 0.9 %copy-start.1 = (f32[16,16,128]{2,1,0:T(8,128)S(1)}, f32[16,16,128]{2,1,0:T(8,128)}, u32[]{:S(2)}) copy-start(f32[16,16,128]{2,1,0:T(8,128)} %param.8) | copy-start | bytes 393220
  2.4 0.9 %copy-start.2 = (f32[16,16,128]{2,1,0:T(8,128)S(1)}, f32[16,16,128]{2,1,0:T(8,128)}, u32[]{:S(2)}) copy-start(f32[16,16,128]{2,1,0:T(8,128)} %param.9) | copy-start | bytes 393220
  3.3 0.9 %copy-start.3 = (f32[16,16,128]{2,1,0:T(8,128)S(1)}, f32[16,16,128]{2,1,0:T(8,128)}, u32[]{:S(2)}) copy-start(f32[16,16,128]{2,1,0:T(8,128)} %param.10) | copy-start | bytes 393220
  4.3 0.7 %copy-start.4 = (s32[16,128]{1,0:T(8,128)S(1)}, s32[16,128]{1,0:T(8,128)}, u32[]{:S(2)}) copy-start(s32[16,128]{1,0:T(8,128)} %refs_4_.1) | copy-start | bytes 24580
  4.9 0.7 %copy-start.5 = (s32[16,128]{1,0:T(8,128)S(1)}, s32[16,128]{1,0:T(8,128)}, u32[]{:S(2)}) copy-start(s32[16,128]{1,0:T(8,128)} %refs_5_.1) | copy-start | bytes 24580
  7.0 15.6 %collective-permute-start = (f32[16,384]{1,0:T(8,128)S(1)}, f32[16,384]{1,0:T(8,128)S(1)}, u32[]{:S(2)}, u32[]{:S(2)}) collective-permute-start(f32[16,384]{1,0:T(8,128)S(1)} %get-tuple-element.31), channel_id=1, source_target_pairs={{0,504},{8,16},{16,8},{24,32},{32,24},{40,48},{48,40},{56,64},{64,... | collective-permute-start | bytes 73736 | tf_op jit(solution)/shard_map/ppermute | solution.py:508
  23.4 14.4 %collective-permute-start.1 = (f32[23,8,128]{2,1,0:T(8,128)S(1)}, f32[23,8,128]{2,1,0:T(8,128)S(1)}, u32[]{:S(2)}, u32[]{:S(2)}) collective-permute-start(f32[23,8,128]{2,1,0:T(8,128)S(1)} %get-tuple-element.38), channel_id=1, source_target_pairs={{0,1},{1,0},{2,3},{3,2},{4,5},{5,4},{6,7},{7,6},{8,9},{9,8},{10,11... | collective-permute-start | bytes 282632 | tf_op jit(solution)/shard_map/ppermute | solution.py:529
  28.2 5.2 %copy-start.6 = (f32[16]{0:T(128)S(1)}, f32[16]{0:T(128)}, u32[]{:S(2)}) copy-start(f32[16]{0:T(128)} %visc_hbm.1) | copy-start | bytes 196
  28.2 11.3 %collective-permute-start.2 = (f32[23,8,128]{2,1,0:T(8,128)S(1)}, f32[23,8,128]{2,1,0:T(8,128)S(1)}, u32[]{:S(2)}, u32[]{:S(2)}) collective-permute-start(f32[23,8,128]{2,1,0:T(8,128)S(1)} %get-tuple-element.39), channel_id=1, source_target_pairs={{1,2},{2,1},{3,4},{4,3},{5,6},{6,5},{7,511},{9,10},{10,9},{11,12},... | collective-permute-start | bytes 282632 | tf_op jit(solution)/shard_map/ppermute | solution.py:528

commit v3 on v2

--- a/solution.py
+++ b/solution.py
@@ -502,7 +502,7 @@
         [VMEM] * 8,
         [FLAT] * 4 + [(J, W), (K, 5 * W), (K, 3 * W), (K, 3 * W)],
         1 << 20,
-        (t, s, u, v, ind, lay),
+        [pltpu.with_memory_space_constraint(x, pltpu.HBM) for x in (t, s, u, v, ind, lay)],
         [pltpu.VMEM((J, W), jnp.int32)] * 2 + [pltpu.SemaphoreType.DMA((6,))],
     )
     od = lax.ppermute(od, "lon", [(i, (((i + 1) ^ 1) - 1) % n_lon) for i in range(n_lon)])
@@ -525,15 +525,15 @@
             if 0 < l < top:
                 pairs_o.append((p * n_lat + l, p * n_lat + ((l + 1) ^ 1) - 1))
         pairs_o.append((p * n_lat + top, (n_lon - 1 - p) * n_lat + top))
+    got_e = lax.ppermute(edge_e, ("lon", "lat"), pairs_e)
     got_o = lax.ppermute(edge_o, ("lon", "lat"), pairs_o)
-    got_e = lax.ppermute(edge_e, ("lon", "lat"), pairs_e)
     *parts, aux = call(
         inner_kernel,
         [VMEM] * 5 + [HBM] + [VMEM] * 4,
         [VMEM] * 5,
         [FLAT] * 4 + [(AUX, K, W)],
         1 << 24,
-        (t, s, u, v, depth, visc, own, ev, od, swept),
+        (t, s, u, v, depth, pltpu.with_memory_space_constraint(visc, pltpu.HBM), own, ev, od, swept),
         [pltpu.SMEM((K,), F32), pltpu.SemaphoreType.DMA],
     )
     outs = call(

time: 41 us -> 36.1 us (0.88)
  local copies, waits for them, and re-layouts: 5.01 us -> 0 us
    unnamed x14 -> x0, local copies, waits for them, and re-layouts: 5.01 us -> none
  transfers between devices with their start and end apart: 3 -> 3, of which waited for: 2 -> 2; matrix products, arithmetic and copies ran while one was open for 0% -> 0% of each run, Pallas kernels for 11% -> 12%
where the time goes in v3:
time: 36.1 us; the launch traced here: 35.8 us
  starting transfers between devices  23.4 us (65%)
  Pallas kernels  7.82 us (22%)
  waiting for transfers between devices  2.01 us (6%)
  blocking collectives  1.84 us (5%)
  between operations  0.69 us (2%)
    ppermute x1, starting transfers between devices, body(): lax.ppermute(od, 'lon', [(i, ((i + 1 ^ 1) - 1) % n_lon) for i in range(n_...  13.4 us
    pallas_call x4, Pallas kernels, call(): pl.pallas_call(kernel, out_shape=[jax.ShapeDtypeStruct(s, F32) for s in o...  7.82 us
    ppermute x1, starting transfers between devices, body(): got_o = lax.ppermute(edge_o, ('lon', 'lat'), pairs_o)  5.2 us
    ppermute x1, starting transfers between devices, body(): got_e = lax.ppermute(edge_e, ('lon', 'lat'), pairs_e)  4.82 us
    all_gather x1, blocking collectives, body(): lax.all_gather(ev, 'lon', axis_index_groups=[[i, i + 1] for i in range(0,...  1.84 us
    ppermute x1, waiting for transfers between devices, body(): got_o = lax.ppermute(edge_o, ('lon', 'lat'), pairs_o)  1.69 us
  transfers between devices with their start and end apart: 3, of which 2 were waited for; matrix products, arithmetic and copies ran while one was open for 0% of the time, Pallas kernels for 12%

profile of v3, /device:TPU:6, one launch (start us, length us, event | category | flops | bytes accessed | tf_op | source)
XLA Modules:
  0.0 35.8 jit_solution(1360542781060580762)
XLA Ops:
  0.6 1.5 %shard_map.102 = (f32[256,128]{1,0:T(8,128)S(1)}, f32[256,128]{1,0:T(8,128)S(1)}, f32[256,128]{1,0:T(8,128)S(1)}, f32[256,128]{1,0:T(8,128)S(1)}, f32[16,128]{1,...) custom-call(f32[256,128]{1,0:T(8,128)} %bitcast.8, f32[256,128]{1,0:T(8,128)} %bitcast.9, ...), custom_call_target="tpu_custom_call" | custom-call | flops 1048576 | bytes 1048576 | tf_op jit(solution)/shard_map/pallas_call | solution.py:485
  2.1 13.4 %collective-permute-start = (f32[16,384]{1,0:T(8,128)S(1)}, f32[16,384]{1,0:T(8,128)S(1)}, u32[]{:S(2)}, u32[]{:S(2)}) collective-permute-start(f32[16,384]{1,0:T(8,128)S(1)} %get-tuple-element.31), channel_id=1, source_target_pairs={{0,504},{8,16},{16,8},{24,32},{32,24},{40,48},{48,40},{56,64},{64,... | collective-permute-start | bytes 73736 | tf_op jit(solution)/shard_map/ppermute | solution.py:508
  15.6 1.8 %all_gather.3.ev_ref = f32[32,384]{1,0:T(8,128)S(1)} all-gather(f32[16,384]{1,0:T(8,128)S(1)} %get-tuple-element.30), channel_id=1, replica_groups={{0,8},{16,24},{32,40},{48,56},{64,72},{80,88},{96,104},{112,120},{128,1..., dimensions={0}, use_global_device_ids=true | all-gather | bytes 73728 | tf_op jit(solution)/shard_map/all_gather | solution.py:509
  17.4 0.3 collective-permute-done.od_ref
  17.7 0.8 %shard_map.103 = (f32[12,16,128]{2,1,0:T(8,128)S(1)}, f32[23,8,128]{2,1,0:T(8,128)S(1)}, f32[23,8,128]{2,1,0:T(8,128)S(1)}) custom-call(f32[256,128]{1,0:T(8,128)S(1)} %get-tuple-element.27.t_ref, f32[256,128]{1,0:T(8,128)S(1)} %get-tuple-element.28.s_ref, f32[256,128]{1,0:T(8,128)S(1)} %get-tuple-element.24.u_ref, f32[256,128]{1,0:T(8,128)S(1)} %get-tuple-element.25.v_ref, ...), custom_call_target="tpu_custom_call" | custom-call | flops 1048576 | bytes 1048576 | tf_op jit(solution)/shard_map/pallas_call | solution.py:485
  18.5 4.8 %collective-permute-start.1 = (f32[23,8,128]{2,1,0:T(8,128)S(1)}, f32[23,8,128]{2,1,0:T(8,128)S(1)}, u32[]{:S(2)}, u32[]{:S(2)}) collective-permute-start(f32[23,8,128]{2,1,0:T(8,128)S(1)} %get-tuple-element.38), channel_id=1, source_target_pairs={{0,1},{1,0},{2,3},{3,2},{4,5},{5,4},{6,7},{7,6},{8,9},{9,8},{10,11... | collective-permute-start | bytes 282632 | tf_op jit(solution)/shard_map/ppermute | solution.py:528
  23.3 5.2 %collective-permute-start.2 = (f32[23,8,128]{2,1,0:T(8,128)S(1)}, f32[23,8,128]{2,1,0:T(8,128)S(1)}, u32[]{:S(2)}, u32[]{:S(2)}) collective-permute-start(f32[23,8,128]{2,1,0:T(8,128)S(1)} %get-tuple-element.39), channel_id=1, source_target_pairs={{1,2},{2,1},{3,4},{4,3},{5,6},{6,5},{7,511},{9,10},{10,9},{11,12},... | collective-permute-start | bytes 282632 | tf_op jit(solution)/shard_map/ppermute | solution.py:529
  28.5 4.4 %shard_map.104 = (f32[256,128]{1,0:T(8,128)S(1)}, f32[256,128]{1,0:T(8,128)S(1)}, f32[256,128]{1,0:T(8,128)S(1)}, f32[256,128]{1,0:T(8,128)S(1)}, f32[47,16,128]{2,1,0:T(8,128)S(1)}) custom-call(f32[256,128]{1,0:T(8,128)S(1)} %get-tuple-element.27.t_ref, f32[256,128]{1,0:T(8,128)S(1)} %get-tuple-element.28.s_ref, f32[256,128]{1,0:T(8,128)S(1)} %get-tuple-element.24.u_ref, ...), custom_call_target="tpu_custom_call" | custom-call | flops 16777216 | bytes 1048576 | tf_op jit(solution)/shard_map/pallas_call | solution.py:485
  32.9 0.0 collective-permute-done.1.e_ref
  32.9 1.7 %collective-permute-done.2.o_ref = f32[23,8,128]{2,1,0:T(8,128)S(1)} collective-permute-done((f32[23,8,128]{2,1,0:T(8,128)S(1)}, f32[23,8,128]{2,1,0:T(8,128)S(1)}, u32[]{:S(2)}, u32[]{:S(2)}) %collective-permute-start.2) | collective-permute-done | bytes 94240 | tf_op jit(solution)/shard_map/ppermute | solution.py:529
  34.6 1.2 %shard_map.105 = (f32[256,128]{1,0:T(8,128)}, f32[256,128]{1,0:T(8,128)}, f32[256,128]{1,0:T(8,128)}, f32[256,128]{1,0:T(8,128)}) custom-call(f32[256,128]{1,0:T(8,128)S(1)} %get-tuple-element.24.u_ref, f32[256,128]{1,0:T(8,128)S(1)} %get-tuple-element.25.v_ref, f32[16,128]{1,0:T(8,128)S(1)} %get-tuple-element.26.d_ref, ...), custom_call_target="tpu_custom_call" | custom-call | flops 4194304 | bytes 1048576 | tf_op jit(solution)/shard_map/pallas_call | solution.py:485
Async XLA Ops:
  2.1 15.6 %collective-permute-start = (f32[16,384]{1,0:T(8,128)S(1)}, f32[16,384]{1,0:T(8,128)S(1)}, u32[]{:S(2)}, u32[]{:S(2)}) collective-permute-start(f32[16,384]{1,0:T(8,128)S(1)} %get-tuple-element.31), channel_id=1, source_target_pairs={{0,504},{8,16},{16,8},{24,32},{32,24},{40,48},{48,40},{56,64},{64,... | collective-permute-start | bytes 73736 | tf_op jit(solution)/shard_map/ppermute | solution.py:508
  18.5 14.4 %collective-permute-start.1 = (f32[23,8,128]{2,1,0:T(8,128)S(1)}, f32[23,8,128]{2,1,0:T(8,128)S(1)}, u32[]{:S(2)}, u32[]{:S(2)}) collective-permute-start(f32[23,8,128]{2,1,0:T(8,128)S(1)} %get-tuple-element.38), channel_id=1, source_target_pairs={{0,1},{1,0},{2,3},{3,2},{4,5},{5,4},{6,7},{7,6},{8,9},{9,8},{10,11... | collective-permute-start | bytes 282632 | tf_op jit(solution)/shard_map/ppermute | solution.py:528
  23.3 11.3 %collective-permute-start.2 = (f32[23,8,128]{2,1,0:T(8,128)S(1)}, f32[23,8,128]{2,1,0:T(8,128)S(1)}, u32[]{:S(2)}, u32[]{:S(2)}) collective-permute-start(f32[23,8,128]{2,1,0:T(8,128)S(1)} %get-tuple-element.39), channel_id=1, source_target_pairs={{1,2},{2,1},{3,4},{4,3},{5,6},{6,5},{7,511},{9,10},{10,9},{11,12},... | collective-permute-start | bytes 282632 | tf_op jit(solution)/shard_map/ppermute | solution.py:529

commit v4 on v3

--- a/solution.py
+++ b/solution.py
@@ -7,7 +7,8 @@
 
 K, J, W = 16, 16, 128
 WIN = 6
-SEND_ROWS = 23
+PHASE = (0, 3, 0, 3, 0)
+SEND_ROWS = 21
 F32 = jnp.float32
 
 
@@ -75,12 +76,12 @@
     return size * rest, rest * rest
 
 
-def pack_columns(rows):
+def pack_columns(rows, phase):
     lane = lanes()
     packed = jnp.zeros((K, W), F32)
     for j, row in enumerate(rows):
-        mine = (lane >= WIN * j) & (lane < WIN * j + WIN)
-        packed = jnp.where(mine, roll(row, WIN * j + 3), packed)
+        first = WIN * j + phase
+        packed = jnp.where((lane >= first) & (lane < first + WIN), roll(row, first + 3), packed)
     return packed
 
 
@@ -96,11 +97,11 @@
     copies[4].wait()
     copies[5].wait()
     d_ref[...] = (ind_ref[...] * lay_ref[...]).astype(F32)
-    d = pack_columns([depth_row(d_ref, j) for j in range(J)])
+    d = pack_columns([depth_row(d_ref, j) for j in range(J)], 3)
     fields = []
     for n, ref in enumerate((t_ref, s_ref, u_ref, v_ref)):
         copies[n].wait()
-        fields.append(pack_columns([load_row(ref, j) for j in range(J)]))
+        fields.append(pack_columns([load_row(ref, j) for j in range(J)], 3 if n == 1 else 0))
     fields.insert(3, d)
     for n, x in enumerate(fields):
         own_ref[:, n * W : (n + 1) * W] = x
@@ -108,27 +109,30 @@
     low = low_half(lanes())
     even = (lax.axis_index("lon") & 1) == 0
     for n, (a, b) in enumerate(((t, s), (u, d), (v, v))):
-        to_east = jnp.where(low, a, roll(b, 3))
-        to_west = jnp.where(low, roll(b, -3), a)
+        to_east = jnp.where(low, a, b)
+        to_west = jnp.where(low, b, a)
         at = slice(n * W, (n + 1) * W)
         ev_ref[:, at] = jnp.where(even, to_east, to_west)
         od_ref[:, at] = jnp.where(even, to_west, to_east)
 
 
+def arrived(ev_ref, od_ref, n):
+    even = (lax.axis_index("lon") & 1) == 0
+    mate = pl.multiple_of(jnp.where(even, K, 0), K)
+    at = slice((n // 2) * W, (n // 2 + 1) * W)
+    ev = ev_ref[pl.ds(mate, K), at]
+    od = od_ref[:, at]
+    return jnp.where(even, od, ev), jnp.where(even, ev, od)
+
+
 def seams(own_ref, ev_ref, od_ref):
     low = low_half(lanes())
-    even = (lax.axis_index("lon") & 1) == 0
-    mate = pl.multiple_of(jnp.where(even, K, 0), K)
     out = []
     for n in range(5):
-        at = slice((n // 2) * W, (n // 2 + 1) * W)
-        ev = ev_ref[pl.ds(mate, K), at]
-        od = od_ref[:, at]
-        from_west = jnp.where(even, od, ev)
-        from_east = jnp.where(even, ev, od)
-        if n in (1, 3):
-            from_west, from_east = roll(from_west, -3), roll(from_east, 3)
+        from_west, from_east = arrived(ev_ref, od_ref, n)
         own = own_ref[:, n * W : (n + 1) * W]
+        if PHASE[n]:
+            from_west, from_east, own = (roll(x, -3) for x in (from_west, from_east, own))
         out.append(
             (
                 jnp.where(low, from_west, from_east),
@@ -148,6 +152,19 @@
     near, far = weights(roll(c, 1))
     out_left = q - (near * up + far * down)
     return fall, c * wet * roll(wet, -1) * jnp.where(c > 0.0, out_right, roll(out_left, -1))
+
+
+def in_step(walks):
+    out = [None] * len(walks)
+    live = list(range(len(walks)))
+    while live:
+        for n in tuple(live):
+            try:
+                next(walks[n])
+            except StopIteration as end:
+                out[n] = end.value
+                live.remove(n)
+    return out
 
 
 class Zonal:
@@ -169,29 +186,38 @@
         last = lane == W - 1
         u = load_row(self.u_ref, j)
         wet = wet_of(depth_row(self.d_ref, j))
-        halo_wet = wet_of(unpack(self.packs[3][0], j))
+        halo_wet = unpack(self.packs[3][0], j)
+        halo_u = unpack(self.packs[2][0], j)
+        halos = [unpack(self.packs[n][0], j) for n in range(2)]
+        fixes = [[unpack(x, j) for x in self.fix[n]] for n in range(2)]
+        q = [load_row(ref, j) for ref in refs]
+        yield
+        halo_wet = wet_of(halo_wet)
+        right = [east(q[n], halos[n], lane) for n in range(2)]
+        left = [west(q[n], halos[n], lane) for n in range(2)]
+        beyond = [roll(jnp.where(lane < 2, halos[n], q[n]), -2) for n in range(2)]
+        u_west = west(u, halo_u, lane)
+        wet_east = east(wet, halo_wet, lane)
+        yield
+        edges = [rise_fall(q[n] - left[n], right[n] - q[n], beyond[n] - right[n]) for n in range(2)]
+        falls = [roll(edges[n][1], 1) for n in range(2)]
+        yield
         near, far = weights(u)
-        near_w, far_w = weights(west(u, unpack(self.packs[2][0], j), lane))
-        face = u * wet * east(wet, halo_wet, lane)
+        near_w, far_w = weights(u_west)
+        face = u * wet * wet_east
         forward = u > 0.0
-        out = []
-        for n, ref in enumerate(refs):
-            q = load_row(ref, j)
-            halo = unpack(self.packs[n][0], j)
-            fix, flux_in = (unpack(x, j) for x in self.fix[n])
-            right = east(q, halo, lane)
-            rise, fall = rise_fall(
-                q - west(q, halo, lane),
-                right - q,
-                roll(jnp.where(lane < 2, halo, q), -2) - right,
-            )
-            down, up = limited(jnp.where(lane == 0, fix, roll(fall, 1)), rise)
-            flux = face * jnp.where(
-                forward, q + (near * down + far * up), roll(q - (near_w * up + far_w * down), -1)
-            )
-            flux_west = roll(jnp.where(last, flux_in, flux), 1)
-            out.append(q - (jnp.where(last, fix, flux) - flux_west))
-        return out
+        cells = [
+            limited(jnp.where(lane == 0, fixes[n][0], falls[n]), edges[n][0]) for n in range(2)
+        ]
+        from_right = [roll(q[n] - (near_w * cells[n][1] + far_w * cells[n][0]), -1) for n in range(2)]
+        yield
+        flux = [
+            face * jnp.where(forward, q[n] + (near * cells[n][0] + far * cells[n][1]), from_right[n])
+            for n in range(2)
+        ]
+        before = [roll(jnp.where(last, fixes[n][1], flux[n]), 1) for n in range(2)]
+        yield
+        return [q[n] - (jnp.where(last, fixes[n][0], flux[n]) - before[n]) for n in range(2)]
 
 
 def zonal_masks(wet, halo_wet, lane):
@@ -214,51 +240,58 @@
     t_ref, s_ref, u_ref, v_ref, d_ref, own_ref, ev_ref, od_ref, swept_ref, e_ref, o_ref
 ):
     lane = lanes()
+    lane8, sub8 = lane[:8], lax.broadcasted_iota(jnp.int32, (8, W), 0)
     packs = seams(own_ref, ev_ref, od_ref)
     zonal = Zonal(packs, u_ref, d_ref)
+    packs = [p[0] for p in packs]
+    wet = {j: wet_of(depth_row(d_ref, j)) for j in (0, 1, 2, 13, 14, 15)}
+    halo_wet = {j: wet_of(unpack(packs[3], j)) for j in (0, 15)}
     halves = []
-    for rows in ((J - 1, J - 2, J - 3), (0, 1, 2)):
-        planes = [zonal.row((t_ref, s_ref), j) for j in rows]
+    all_rows = (15, 14, 13, 0, 1, 2)
+    swept = []
+    for at in range(0, 6, 6):
+        swept += in_step([zonal.row((t_ref, s_ref), j) for j in all_rows[at : at + 6]])
+    planes_of = (swept[:3], swept[3:])
+    for side, rows in enumerate(((J - 1, J - 2, J - 3), (0, 1, 2))):
+        planes = planes_of[side]
         for j, (t, s) in zip(rows, planes):
             swept_ref[j if j < 3 else j - 10] = t
             swept_ref[6 + (j if j < 3 else j - 10)] = s
         half = [p[0] for p in planes] + [p[1] for p in planes]
         j, inward = rows[0], rows[1]
-        depth = depth_row(d_ref, j)
-        halo_depth = unpack(packs[3][0], j)
-        wet, halo_wet = wet_of(depth), wet_of(halo_depth)
-        masks = zonal_masks(wet, halo_wet, lane)
-        to_inner = wet * wet_of(depth_row(d_ref, inward))
-        corner = roll(halo_depth, 2)
-        corner = jnp.where(lane < W // 2, corner, roll(halo_depth, -2))
-        for ref, pack, reach in ((v_ref, packs[4], 1), (u_ref, packs[2], 0)):
-            halo = unpack(pack[0], j)
+        masks = zonal_masks(wet[j], halo_wet[j], lane)
+        to_inner = wet[j] * wet[inward]
+        for ref, pack in ((u_ref, packs[2]), (v_ref, packs[4])):
             f = load_row(ref, j)
-            partial = zonal_lap(f, halo, masks, lane) + to_inner * (load_row(ref, inward) - f)
-            half[6:6] = [f, partial]
-            take = jnp.where(lane < W // 2, roll(halo, reach), roll(halo, -reach))
-            corner = jnp.where((lane == reach) | (lane == W - 1 - reach), take, corner)
-        halves.append((half + [corner], depth[:8]))
+            partial = zonal_lap(f, unpack(pack, j), masks, lane) + to_inner * (load_row(ref, inward) - f)
+            half += [f, partial]
+        depth = depth_row(d_ref, j)[:8]
+        corner = jnp.where(sub8 < 4, depth, roll(depth, W // 2))
+        for at, (pack, top) in enumerate(
+            ((packs[2], 0), (packs[4], 0), (packs[2], 8), (packs[4], 8), (packs[3], 0))
+        ):
+            home = -(WIN * j + 3)
+            part = pack[top : top + 8]
+            corner = jnp.where(lane8 == at, roll(part, home + at), corner)
+            corner = jnp.where(lane8 == W - 1 - at, roll(part, home - at), corner)
+        halves.append((half, corner))
     lat = lax.axis_index("lat")
     even = (lat & 1) == 0
-    top = lat == lax.axis_size("lat") - 1
-    (north, north_d), (south, south_d) = halves
+    (north, north_c), (south, south_c) = halves
     for n, (a, b) in enumerate(zip(north, south)):
         e_ref[2 * n : 2 * n + 2] = jnp.where(even, a, b).reshape(2, 8, W)
         o_ref[2 * n : 2 * n + 2] = jnp.where(even, b, a).reshape(2, 8, W)
-    e_ref[SEND_ROWS - 1] = jnp.where(even, north_d, south_d)
-    o_ref[SEND_ROWS - 1] = jnp.where(even, south_d, north_d)
-
-    @pl.when(top)
+    e_ref[SEND_ROWS - 1] = jnp.where(even, north_c, south_c)
+    o_ref[SEND_ROWS - 1] = jnp.where(even, south_c, north_c)
+
+    @pl.when(lat == lax.axis_size("lat") - 1)
     def _():
-        mirror = W - 1 - lax.broadcasted_iota(jnp.int32, (8, W), 1)
-        lane8 = lax.broadcasted_iota(jnp.int32, (8, W), 1)
         for n in range(SEND_ROWS):
-            x = jnp.take_along_axis(o_ref[n], mirror, axis=1)
+            x = jnp.take_along_axis(o_ref[n], W - 1 - lane8, axis=1)
             if 12 <= n < 20:
                 x = -x
-            elif 20 <= n < 22:
-                x = jnp.where((lane8 < 2) | (lane8 > W - 3), -x, x)
+            elif n == 20:
+                x = jnp.where((lane8 < 4) | (lane8 > W - 5), -x, x)
             o_ref[n] = x
 
 
@@ -310,8 +343,10 @@
     for j in (0, 1, 2, 13, 14, 15):
         for n in range(2):
             rows[n][j] = swept_ref[6 * n + (j if j < 3 else j - 10)]
-    for j in range(3, 13):
-        rows[0][j], rows[1][j] = zonal.row((t_ref, s_ref), j)
+    for at in range(3, 13, 3):
+        group = range(at, min(at + 3, 13))
+        for j, (t, s) in zip(group, in_step([zonal.row((t_ref, s_ref), j) for j in group])):
+            rows[0][j], rows[1][j] = t, s
     wet = [wet_of(depth_row(d_ref, j)) for j in range(J)]
     for n, out in enumerate((t_out, s_out)):
         q = rows[n]
@@ -387,7 +422,7 @@
 
 
 def finish_kernel(
-    u_ref, v_ref, d_ref, t_in, s_in, u_in, v_in, aux_ref, e_ref, o_ref, *outs
+    u_ref, v_ref, d_ref, _t, _s, _u, _v, aux_ref, e_ref, o_ref, *outs
 ):
     finals, (t_out, s_out, u_out, v_out), sems = outs[:4], outs[4:8], outs[8]
     lane = lanes()
@@ -403,19 +438,25 @@
         e, o = e_ref[2 * n : 2 * n + 2].reshape(K, W), o_ref[2 * n : 2 * n + 2].reshape(K, W)
         return jnp.where(even, e, o) if side == 0 else jnp.where(even, o, e)
 
-    def recv_depth(side):
+    wet = {j: wet_of(depth_row(d_ref, j)) for j in (0, 1, 2, 13, 14, 15)}
+    corner_u, corner_v, corner_wet = [], [], []
+    for side in (0, 1):
         e, o = e_ref[SEND_ROWS - 1], o_ref[SEND_ROWS - 1]
-        x = jnp.where(even, e, o) if side == 0 else jnp.where(even, o, e)
-        return jnp.concatenate([x, x], axis=0)
-
-    wet = {j: wet_of(depth_row(d_ref, j)) for j in (0, 1, 2, 13, 14, 15)}
-    wet[16], wet[-1] = wet_of(recv_depth(0)), wet_of(recv_depth(1))
+        tile = jnp.where(even, e, o) if side == 0 else jnp.where(even, o, e)
+        lane8 = lane[:8]
+        inside = (lane8 > 4) & (lane8 < W - 5)
+        row = jnp.where(inside[:1], tile[:1], roll(tile, W // 2)[4:5])
+        wet[16 if side == 0 else -1] = wet_of(jnp.broadcast_to(row, (K, W)))
+        part = [tile] + [
+            jnp.where(lane8 < W // 2, roll(tile, -m), roll(tile, m)) for m in range(1, 5)
+        ]
+        corner_u.append(jnp.concatenate([part[0], part[2]], axis=0))
+        corner_v.append(jnp.concatenate([part[1], part[3]], axis=0))
+        corner_wet.append(wet_of(jnp.concatenate([part[4], part[4]], axis=0)))
     courant = {j: load_row(v_ref, j) for j in (0, 1, 13, 14, 15)}
     courant[-1] = recv(1, 8)
-    for n, (src, out) in enumerate(((t_in, t_out), (s_in, s_out))):
+    for n, out in enumerate((t_out, s_out)):
         aux = AUX_TRACER * n
-        for j in range(3, 13):
-            store_row(out, j, load_row(src, j))
         for side in (0, 1):
             if side == 0:
                 q = {11 + m: aux_ref[aux + 5 + m] for m in range(5)}
@@ -438,16 +479,11 @@
             if side == 1:
                 store_row(out, 2, q[2] - (aux_ref[aux + 10] - before))
         copies[n].start()
-    for n, (ref, src, out) in enumerate(((u_ref, u_in, u_out), (v_ref, v_in, v_out))):
+    for n, (ref, out) in enumerate(((u_ref, u_out), (v_ref, v_out))):
         base = 2 * AUX_TRACER + AUX_FLOW * n
-        for j in range(2, 14):
-            store_row(out, j, load_row(src, j))
         for side in (0, 1):
             edge, inward, beyond = (15, 14, 16) if side == 0 else (0, 1, -1)
             halo_wet = aux_ref[halo_at + 1 - side]
-            corner = recv(side, 10)
-            corner_depth = jnp.where(lane < W // 2, roll(corner, -2), roll(corner, 2))
-            corner_wet = halo_wet * wet_of(corner_depth)
             masks = zonal_masks(wet[edge], halo_wet, lane)
             at = (3, 4, 5, 7, 9) if side == 0 else (0, 1, 2, 6, 8)
             lap_edge, lap_in, partial, halo_lap, halo_f = (aux_ref[base + a] for a in at)
@@ -457,11 +493,8 @@
             step = across * (f_out - f)
             lap_edge = lap_edge + step
             lap_out = lap_out - step
-            if n == 0:
-                corner_f = corner
-            else:
-                corner_f = jnp.where(lane < W // 2, roll(corner, -1), roll(corner, 1))
-            halo_lap = halo_lap + corner_wet * (corner_f - halo_f)
+            corner_f = (corner_u, corner_v)[n][side]
+            halo_lap = halo_lap + halo_wet * corner_wet[side] * (corner_f - halo_f)
             inner_step = wet[edge] * wet[inward] * (lap_in - lap_edge)
             total = (
                 zonal_lap(lap_edge, halo_lap, masks, lane)
@@ -481,13 +514,14 @@
 AUX = 2 * AUX_TRACER + 2 * AUX_FLOW + 3
 
 
-def call(kernel, in_specs, out_specs, out_shapes, flops, args, scratch=()):
+def call(kernel, in_specs, out_specs, out_shapes, flops, args, scratch=(), aliases=()):
     return pl.pallas_call(
         kernel,
         out_shape=[jax.ShapeDtypeStruct(s, F32) for s in out_shapes],
         in_specs=in_specs,
         out_specs=out_specs,
         scratch_shapes=list(scratch),
+        input_output_aliases=dict(aliases),
         cost_estimate=pl.CostEstimate(flops=flops, bytes_accessed=1 << 20, transcendentals=0),
         compiler_params=pltpu.CompilerParams(vmem_limit_bytes=32 << 20),
     )(*args)
@@ -539,13 +573,14 @@
     outs = call(
         finish_kernel,
         [VMEM] * 10,
-        [HBM] * 4,
-        [FLAT] * 4,
+        [HBM] * 4 + [VMEM] * 4,
+        [FLAT] * 8,
         1 << 22,
         (u, v, depth, *parts, aux, got_e, got_o),
-        [pltpu.VMEM(FLAT, F32)] * 4 + [pltpu.SemaphoreType.DMA((4,))],
-    )
-    return tuple(x.reshape(K, J, W) for x in outs)
+        [pltpu.SemaphoreType.DMA((4,))],
+        {3: 4, 4: 5, 5: 6, 6: 7},
+    )
+    return tuple(x.reshape(K, J, W) for x in outs[:4])
 
 
 def solution(mesh):

time: 36.1 us -> 35.9 us (level)
  Pallas kernels: 7.82 us -> 7.22 us
    pallas_call x4, Pallas kernels: 7.82 us -> 7.22 us  [call(): pl.pallas_call(kernel, out_shape=[jax.ShapeDtypeStruct(s, F32) for s in o...]
where the time goes in v4:
time: 35.9 us; the launch traced here: 35.4 us
  starting transfers between devices  23.4 us (65%)
  Pallas kernels  7.22 us (20%)
  waiting for transfers between devices  2.2 us (6%)
  blocking collectives  1.84 us (5%)
  between operations  0.69 us (2%)
    ppermute x1, starting transfers between devices, body(): lax.ppermute(od, 'lon', [(i, ((i + 1 ^ 1) - 1) % n_lon) for i in range(n_...  13.4 us
    pallas_call x4, Pallas kernels, call(): pl.pallas_call(kernel, out_shape=[jax.ShapeDtypeStruct(s, F32) for s in o...  7.22 us
    ppermute x1, starting transfers between devices, body(): got_o = lax.ppermute(edge_o, ('lon', 'lat'), pairs_o)  5.2 us
    ppermute x1, starting transfers between devices, body(): got_e = lax.ppermute(edge_e, ('lon', 'lat'), pairs_e)  4.82 us
    ppermute x1, waiting for transfers between devices, body(): got_o = lax.ppermute(edge_o, ('lon', 'lat'), pairs_o)  1.88 us
    all_gather x1, blocking collectives, body(): lax.all_gather(ev, 'lon', axis_index_groups=[[i, i + 1] for i in range(0,...  1.84 us
  transfers between devices with their start and end apart: 3, of which 2 were waited for; matrix products, arithmetic and copies ran while one was open for 0% of the time, Pallas kernels for 12%

profile of v4, /device:TPU:6, one launch (start us, length us, event | category | flops | bytes accessed | tf_op | source)
XLA Modules:
  0.0 35.4 jit_solution(11606115098346454667)
XLA Ops:
  0.6 1.4 %shard_map.102 = (f32[256,128]{1,0:T(8,128)S(1)}, f32[256,128]{1,0:T(8,128)S(1)}, f32[256,128]{1,0:T(8,128)S(1)}, f32[256,128]{1,0:T(8,128)S(1)}, f32[16,128]{1,...) custom-call(f32[256,128]{1,0:T(8,128)} %bitcast.8, f32[256,128]{1,0:T(8,128)} %bitcast.9, ...), custom_call_target="tpu_custom_call" | custom-call | flops 1048576 | bytes 1048576 | tf_op jit(solution)/shard_map/pallas_call | solution.py:518
  2.1 13.4 %collective-permute-start = (f32[16,384]{1,0:T(8,128)S(1)}, f32[16,384]{1,0:T(8,128)S(1)}, u32[]{:S(2)}, u32[]{:S(2)}) collective-permute-start(f32[16,384]{1,0:T(8,128)S(1)} %get-tuple-element.31), channel_id=1, source_target_pairs={{0,504},{8,16},{16,8},{24,32},{32,24},{40,48},{48,40},{56,64},{64,... | collective-permute-start | bytes 73736 | tf_op jit(solution)/shard_map/ppermute | solution.py:542
  15.5 1.8 %all_gather.3.ev_ref = f32[32,384]{1,0:T(8,128)S(1)} all-gather(f32[16,384]{1,0:T(8,128)S(1)} %get-tuple-element.30), channel_id=1, replica_groups={{0,8},{16,24},{32,40},{48,56},{64,72},{80,88},{96,104},{112,120},{128,1..., dimensions={0}, use_global_device_ids=true | all-gather | bytes 73728 | tf_op jit(solution)/shard_map/all_gather | solution.py:543
  17.3 0.3 collective-permute-done.od_ref
  17.7 0.7 %shard_map.103 = (f32[12,16,128]{2,1,0:T(8,128)S(1)}, f32[21,8,128]{2,1,0:T(8,128)S(1)}, f32[21,8,128]{2,1,0:T(8,128)S(1)}) custom-call(f32[256,128]{1,0:T(8,128)S(1)} %get-tuple-element.27.t_ref, f32[256,128]{1,0:T(8,128)S(1)} %get-tuple-element.28.s_ref, f32[256,128]{1,0:T(8,128)S(1)} %get-tuple-element.24.u_ref, f32[256,128]{1,0:T(8,128)S(1)} %get-tuple-element.25.v_ref, ...), custom_call_target="tpu_custom_call" | custom-call | flops 1048576 | bytes 1048576 | tf_op jit(solution)/shard_map/pallas_call | solution.py:518
  18.4 4.8 %collective-permute-start.1 = (f32[21,8,128]{2,1,0:T(8,128)S(1)}, f32[21,8,128]{2,1,0:T(8,128)S(1)}, u32[]{:S(2)}, u32[]{:S(2)}) collective-permute-start(f32[21,8,128]{2,1,0:T(8,128)S(1)} %get-tuple-element.38), channel_id=1, source_target_pairs={{0,1},{1,0},{2,3},{3,2},{4,5},{5,4},{6,7},{7,6},{8,9},{9,8},{10,11... | collective-permute-start | bytes 258056 | tf_op jit(solution)/shard_map/ppermute | solution.py:562
  23.2 5.2 %collective-permute-start.2 = (f32[21,8,128]{2,1,0:T(8,128)S(1)}, f32[21,8,128]{2,1,0:T(8,128)S(1)}, u32[]{:S(2)}, u32[]{:S(2)}) collective-permute-start(f32[21,8,128]{2,1,0:T(8,128)S(1)} %get-tuple-element.39), channel_id=1, source_target_pairs={{1,2},{2,1},{3,4},{4,3},{5,6},{6,5},{7,511},{9,10},{10,9},{11,12},... | collective-permute-start | bytes 258056 | tf_op jit(solution)/shard_map/ppermute | solution.py:563
  28.4 4.1 %shard_map.104 = (f32[256,128]{1,0:T(8,128)S(1)}, f32[256,128]{1,0:T(8,128)S(1)}, f32[256,128]{1,0:T(8,128)S(1)}, f32[256,128]{1,0:T(8,128)S(1)}, f32[47,16,128]{2,1,0:T(8,128)S(1)}) custom-call(f32[256,128]{1,0:T(8,128)S(1)} %get-tuple-element.27.t_ref, f32[256,128]{1,0:T(8,128)S(1)} %get-tuple-element.28.s_ref, f32[256,128]{1,0:T(8,128)S(1)} %get-tuple-element.24.u_ref, ...), custom_call_target="tpu_custom_call" | custom-call | flops 16777216 | bytes 1048576 | tf_op jit(solution)/shard_map/pallas_call | solution.py:518
  32.5 0.0 collective-permute-done.1.e_ref
  32.5 1.9 %collective-permute-done.2.o_ref = f32[21,8,128]{2,1,0:T(8,128)S(1)} collective-permute-done((f32[21,8,128]{2,1,0:T(8,128)S(1)}, f32[21,8,128]{2,1,0:T(8,128)S(1)}, u32[]{:S(2)}, u32[]{:S(2)}) %collective-permute-start.2) | collective-permute-done | bytes 86048 | tf_op jit(solution)/shard_map/ppermute | solution.py:563
  34.4 1.0 %shard_map.105 = (f32[256,128]{1,0:T(8,128)}, f32[256,128]{1,0:T(8,128)}, f32[256,128]{1,0:T(8,128)}, f32[256,128]{1,0:T(8,128)}, f32[256,128]{1,0:T(8,128)S(1)}...) custom-call(f32[256,128]{1,0:T(8,128)S(1)} %get-tuple-element.24.u_r, ...), custom_call_target="tpu_custom_call", output_to_operand_aliasing={{4}: (3, {}), {5}: (4, {}), {6}: (5, {}), {7}: (6, {})} | custom-call | flops 4194304 | bytes 1048576 | tf_op jit(solution)/shard_map/pallas_call | solution.py:518
Async XLA Ops:
  2.1 15.6 %collective-permute-start = (f32[16,384]{1,0:T(8,128)S(1)}, f32[16,384]{1,0:T(8,128)S(1)}, u32[]{:S(2)}, u32[]{:S(2)}) collective-permute-start(f32[16,384]{1,0:T(8,128)S(1)} %get-tuple-element.31), channel_id=1, source_target_pairs={{0,504},{8,16},{16,8},{24,32},{32,24},{40,48},{48,40},{56,64},{64,... | collective-permute-start | bytes 73736 | tf_op jit(solution)/shard_map/ppermute | solution.py:542
  18.4 14.1 %collective-permute-start.1 = (f32[21,8,128]{2,1,0:T(8,128)S(1)}, f32[21,8,128]{2,1,0:T(8,128)S(1)}, u32[]{:S(2)}, u32[]{:S(2)}) collective-permute-start(f32[21,8,128]{2,1,0:T(8,128)S(1)} %get-tuple-element.38), channel_id=1, source_target_pairs={{0,1},{1,0},{2,3},{3,2},{4,5},{5,4},{6,7},{7,6},{8,9},{9,8},{10,11... | collective-permute-start | bytes 258056 | tf_op jit(solution)/shard_map/ppermute | solution.py:562
  23.2 11.2 %collective-permute-start.2 = (f32[21,8,128]{2,1,0:T(8,128)S(1)}, f32[21,8,128]{2,1,0:T(8,128)S(1)}, u32[]{:S(2)}, u32[]{:S(2)}) collective-permute-start(f32[21,8,128]{2,1,0:T(8,128)S(1)} %get-tuple-element.39), channel_id=1, source_target_pairs={{1,2},{2,1},{3,4},{4,3},{5,6},{6,5},{7,511},{9,10},{10,9},{11,12},... | collective-permute-start | bytes 258056 | tf_op jit(solution)/shard_map/ppermute | solution.py:563

commit v5 on v4

--- a/solution.py
+++ b/solution.py
@@ -1,3 +1,5 @@
+import functools
+
 import jax
 import jax.numpy as jnp
 from jax import lax
@@ -421,91 +423,99 @@
     return visc
 
 
-def finish_kernel(
-    u_ref, v_ref, d_ref, _t, _s, _u, _v, aux_ref, e_ref, o_ref, *outs
-):
-    finals, (t_out, s_out, u_out, v_out), sems = outs[:4], outs[4:8], outs[8]
+def finish_side(side, got_ref, u_ref, v_ref, d_ref, aux_ref, outs, finals, sems):
     lane = lanes()
+    t_out, s_out, u_out, v_out = outs
+    half = pl.ds(8 * (1 - side), 8)
     copies = [
-        pltpu.make_async_copy(src, dst, sems.at[n])
-        for n, (src, dst) in enumerate(zip((t_out, s_out, u_out, v_out), finals))
+        pltpu.make_async_copy(
+            src.reshape(K, J, W).at[:, half], dst.reshape(K, J, W).at[:, half], sems.at[n]
+        )
+        for n, (src, dst) in enumerate(zip(outs, finals))
     ]
-    even = (lax.axis_index("lat") & 1) == 0
     halo_at = 2 * AUX_TRACER + 2 * AUX_FLOW
     visc = aux_ref[halo_at + 2]
 
-    def recv(side, n):
-        e, o = e_ref[2 * n : 2 * n + 2].reshape(K, W), o_ref[2 * n : 2 * n + 2].reshape(K, W)
-        return jnp.where(even, e, o) if side == 0 else jnp.where(even, o, e)
-
-    wet = {j: wet_of(depth_row(d_ref, j)) for j in (0, 1, 2, 13, 14, 15)}
-    corner_u, corner_v, corner_wet = [], [], []
-    for side in (0, 1):
-        e, o = e_ref[SEND_ROWS - 1], o_ref[SEND_ROWS - 1]
-        tile = jnp.where(even, e, o) if side == 0 else jnp.where(even, o, e)
-        lane8 = lane[:8]
-        inside = (lane8 > 4) & (lane8 < W - 5)
-        row = jnp.where(inside[:1], tile[:1], roll(tile, W // 2)[4:5])
-        wet[16 if side == 0 else -1] = wet_of(jnp.broadcast_to(row, (K, W)))
-        part = [tile] + [
-            jnp.where(lane8 < W // 2, roll(tile, -m), roll(tile, m)) for m in range(1, 5)
-        ]
-        corner_u.append(jnp.concatenate([part[0], part[2]], axis=0))
-        corner_v.append(jnp.concatenate([part[1], part[3]], axis=0))
-        corner_wet.append(wet_of(jnp.concatenate([part[4], part[4]], axis=0)))
-    courant = {j: load_row(v_ref, j) for j in (0, 1, 13, 14, 15)}
-    courant[-1] = recv(1, 8)
+    def recv(n):
+        return got_ref[2 * n : 2 * n + 2].reshape(K, W)
+
+    faces = (13, 14, 15) if side == 0 else (-1, 0, 1)
+    edge, inward, beyond = (15, 14, 16) if side == 0 else (0, 1, -1)
+    wet = {j: wet_of(depth_row(d_ref, j)) for j in ((13, 14, 15) if side == 0 else (0, 1, 2))}
+    tile = got_ref[SEND_ROWS - 1]
+    lane8 = lane[:8]
+    inside = (lane8 > 4) & (lane8 < W - 5)
+    row = jnp.where(inside[:1], tile[:1], roll(tile, W // 2)[4:5])
+    wet[beyond] = wet_of(jnp.broadcast_to(row, (K, W)))
+    part = [tile] + [
+        jnp.where(lane8 < W // 2, roll(tile, -m), roll(tile, m)) for m in range(1, 5)
+    ]
+    corner_flow = [jnp.concatenate([part[n], part[n + 2]], axis=0) for n in range(2)]
+    corner_wet = wet_of(jnp.concatenate([part[4], part[4]], axis=0))
+    courant = {j: recv(8) if j < 0 else load_row(v_ref, j) for j in faces}
     for n, out in enumerate((t_out, s_out)):
         aux = AUX_TRACER * n
-        for side in (0, 1):
-            if side == 0:
-                q = {11 + m: aux_ref[aux + 5 + m] for m in range(5)}
-                q.update({16 + m: recv(side, 3 * n + m) for m in range(3)})
-                before, faces = aux_ref[aux + 11], (13, 14, 15)
-            else:
-                q = {j: aux_ref[aux + j] for j in range(5)}
-                q.update({-1 - m: recv(side, 3 * n + m) for m in range(3)})
-                before, faces = None, (-1, 0, 1)
-            step = {j: q[j + 1] - q[j] for j in q if j + 1 in q}
-            first = faces[0]
-            fall = rise_fall(step[first - 2], step[first - 1], step[first])[1]
-            cell = merid_cell(step, fall, first)
-            for j in faces:
-                after = merid_cell(step, cell[2], j + 1)
-                flux = merid_flux(courant[j], wet[j] * wet[j + 1], q[j], q[j + 1], cell, after)
-                if before is not None:
-                    store_row(out, j, q[j] - (flux - before))
-                cell, before = after, flux
-            if side == 1:
-                store_row(out, 2, q[2] - (aux_ref[aux + 10] - before))
+        if side == 0:
+            q = {11 + m: aux_ref[aux + 5 + m] for m in range(5)}
+            q.update({16 + m: recv(3 * n + m) for m in range(3)})
+            before = aux_ref[aux + 11]
+        else:
+            q = {j: aux_ref[aux + j] for j in range(5)}
+            q.update({-1 - m: recv(3 * n + m) for m in range(3)})
+            before = None
+        step = {j: q[j + 1] - q[j] for j in q if j + 1 in q}
+        first = faces[0]
+        fall = rise_fall(step[first - 2], step[first - 1], step[first])[1]
+        cell = merid_cell(step, fall, first)
+        for j in faces:
+            after = merid_cell(step, cell[2], j + 1)
+            flux = merid_flux(courant[j], wet[j] * wet[j + 1], q[j], q[j + 1], cell, after)
+            if before is not None:
+                store_row(out, j, q[j] - (flux - before))
+            cell, before = after, flux
+        if side == 1:
+            store_row(out, 2, q[2] - (aux_ref[aux + 10] - before))
         copies[n].start()
+    halo_wet = aux_ref[halo_at + 1 - side]
+    masks = zonal_masks(wet[edge], halo_wet, lane)
+    across = wet[edge] * wet[beyond]
     for n, (ref, out) in enumerate(((u_ref, u_out), (v_ref, v_out))):
         base = 2 * AUX_TRACER + AUX_FLOW * n
-        for side in (0, 1):
-            edge, inward, beyond = (15, 14, 16) if side == 0 else (0, 1, -1)
-            halo_wet = aux_ref[halo_at + 1 - side]
-            masks = zonal_masks(wet[edge], halo_wet, lane)
-            at = (3, 4, 5, 7, 9) if side == 0 else (0, 1, 2, 6, 8)
-            lap_edge, lap_in, partial, halo_lap, halo_f = (aux_ref[base + a] for a in at)
-            f, f_in = load_row(ref, edge), load_row(ref, inward)
-            f_out, lap_out = recv(side, 6 + 2 * n), recv(side, 7 + 2 * n)
-            across = wet[edge] * wet[beyond]
-            step = across * (f_out - f)
-            lap_edge = lap_edge + step
-            lap_out = lap_out - step
-            corner_f = (corner_u, corner_v)[n][side]
-            halo_lap = halo_lap + halo_wet * corner_wet[side] * (corner_f - halo_f)
-            inner_step = wet[edge] * wet[inward] * (lap_in - lap_edge)
-            total = (
-                zonal_lap(lap_edge, halo_lap, masks, lane)
-                + inner_step
-                + across * (lap_out - lap_edge)
-            )
-            store_row(out, edge, f - visc * total)
-            store_row(out, inward, f_in - visc * (partial - inner_step))
+        at = (3, 4, 5, 7, 9) if side == 0 else (0, 1, 2, 6, 8)
+        lap_edge, lap_in, partial, halo_lap, halo_f = (aux_ref[base + a] for a in at)
+        f, f_in = load_row(ref, edge), load_row(ref, inward)
+        f_out, lap_out = recv(6 + 2 * n), recv(7 + 2 * n)
+        step = across * (f_out - f)
+        lap_edge = lap_edge + step
+        lap_out = lap_out - step
+        halo_lap = halo_lap + halo_wet * corner_wet * (corner_flow[n] - halo_f)
+        inner_step = wet[edge] * wet[inward] * (lap_in - lap_edge)
+        total = (
+            zonal_lap(lap_edge, halo_lap, masks, lane)
+            + inner_step
+            + across * (lap_out - lap_edge)
+        )
+        store_row(out, edge, f - visc * total)
+        store_row(out, inward, f_in - visc * (partial - inner_step))
         copies[2 + n].start()
     for copy in copies:
         copy.wait()
+
+
+def finish_kernel(north_if_even, *refs):
+    u_ref, v_ref, d_ref, aux_ref, got_ref = refs[:5]
+    finals, outs, sems = refs[-9:-5], refs[-5:-1], refs[-1]
+    even = (lax.axis_index("lat") & 1) == 0
+
+    @pl.when(even)
+    def _():
+        side = 0 if north_if_even else 1
+        finish_side(side, got_ref, u_ref, v_ref, d_ref, aux_ref, outs, finals, sems)
+
+    @pl.when(jnp.logical_not(even))
+    def _():
+        side = 1 if north_if_even else 0
+        finish_side(side, got_ref, u_ref, v_ref, d_ref, aux_ref, outs, finals, sems)
 
 
 VMEM = pl.BlockSpec(memory_space=pltpu.VMEM)
@@ -570,15 +580,26 @@
         (t, s, u, v, depth, pltpu.with_memory_space_constraint(visc, pltpu.HBM), own, ev, od, swept),
         [pltpu.SMEM((K,), F32), pltpu.SemaphoreType.DMA],
     )
+    flow = (u, v, depth, aux)
     outs = call(
-        finish_kernel,
-        [VMEM] * 10,
+        functools.partial(finish_kernel, True),
+        [VMEM] * 9,
         [HBM] * 4 + [VMEM] * 4,
         [FLAT] * 8,
-        1 << 22,
-        (u, v, depth, *parts, aux, got_e, got_o),
+        1 << 21,
+        (*flow, got_e, *parts),
         [pltpu.SemaphoreType.DMA((4,))],
-        {3: 4, 4: 5, 5: 6, 6: 7},
+        {5: 4, 6: 5, 7: 6, 8: 7},
+    )
+    outs = call(
+        functools.partial(finish_kernel, False),
+        [VMEM] * 5 + [HBM] * 4 + [VMEM] * 4,
+        [HBM] * 4 + [VMEM] * 4,
+        [FLAT] * 8,
+        1 << 21,
+        (*flow, got_o, *outs),
+        [pltpu.SemaphoreType.DMA((4,))],
+        {5 + n: n for n in range(8)},
     )
     return tuple(x.reshape(K, J, W) for x in outs[:4])
 

time: 35.9 us -> 35.7 us (level)
  waiting for transfers between devices: 2.2 us -> 1.33 us
  Pallas kernels: 7.22 us -> 7.9 us
    ppermute x1, waiting for transfers between devices: 1.88 us -> 1.01 us  [body(): got_o = lax.ppermute(edge_o, ('lon', 'lat'), pairs_o)]
    pallas_call x4 -> x5, Pallas kernels: 7.22 us -> 7.9 us  [call(): pl.pallas_call(kernel, out_shape=[jax.ShapeDtypeStruct(s, F32) for s in o...]
  transfers between devices with their start and end apart: 3 -> 3, of which waited for: 2 -> 2; matrix products, arithmetic and copies ran while one was open for 0% -> 0% of each run, Pallas kernels for 12% -> 14%
where the time goes in v5:
time: 35.7 us; the launch traced here: 35.2 us
  starting transfers between devices  23.4 us (66%)
  Pallas kernels  7.9 us (22%)
  blocking collectives  1.84 us (5%)
  waiting for transfers between devices  1.33 us (4%)
  between operations  0.7 us (2%)
    ppermute x1, starting transfers between devices, body(): lax.ppermute(od, 'lon', [(i, ((i + 1 ^ 1) - 1) % n_lon) for i in range(n_...  13.4 us
    pallas_call x5, Pallas kernels, call(): pl.pallas_call(kernel, out_shape=[jax.ShapeDtypeStruct(s, F32) for s in o...  7.9 us
    ppermute x1, starting transfers between devices, body(): got_o = lax.ppermute(edge_o, ('lon', 'lat'), pairs_o)  5.2 us
    ppermute x1, starting transfers between devices, body(): got_e = lax.ppermute(edge_e, ('lon', 'lat'), pairs_e)  4.82 us
    all_gather x1, blocking collectives, body(): lax.all_gather(ev, 'lon', axis_index_groups=[[i, i + 1] for i in range(0,...  1.84 us
    ppermute x1, waiting for transfers between devices, body(): got_o = lax.ppermute(edge_o, ('lon', 'lat'), pairs_o)  1.01 us
  transfers between devices with their start and end apart: 3, of which 2 were waited for; matrix products, arithmetic and copies ran while one was open for 0% of the time, Pallas kernels for 14%

profile of v5, /device:TPU:6, one launch (start us, length us, event | category | flops | bytes accessed | tf_op | source)
XLA Modules:
  0.0 35.2 jit_solution(12549607537262850254)
XLA Ops:
  0.6 1.4 %shard_map.102 = (f32[256,128]{1,0:T(8,128)S(1)}, f32[256,128]{1,0:T(8,128)S(1)}, f32[256,128]{1,0:T(8,128)S(1)}, f32[256,128]{1,0:T(8,128)S(1)}, f32[16,128]{1,...) custom-call(f32[256,128]{1,0:T(8,128)} %bitcast.12, f32[256,128]{1,0:T(8,128)} %bitcast.13, ...), custom_call_target="tpu_custom_call" | custom-call | flops 1048576 | bytes 1048576 | tf_op jit(solution)/shard_map/pallas_call | solution.py:528
  2.1 13.4 %collective-permute-start = (f32[16,384]{1,0:T(8,128)S(1)}, f32[16,384]{1,0:T(8,128)S(1)}, u32[]{:S(2)}, u32[]{:S(2)}) collective-permute-start(f32[16,384]{1,0:T(8,128)S(1)} %get-tuple-element.39), channel_id=1, source_target_pairs={{0,504},{8,16},{16,8},{24,32},{32,24},{40,48},{48,40},{56,64},{64,... | collective-permute-start | bytes 73736 | tf_op jit(solution)/shard_map/ppermute | solution.py:552
  15.5 1.8 %all_gather.3.ev_ref = f32[32,384]{1,0:T(8,128)S(1)} all-gather(f32[16,384]{1,0:T(8,128)S(1)} %get-tuple-element.38), channel_id=1, replica_groups={{0,8},{16,24},{32,40},{48,56},{64,72},{80,88},{96,104},{112,120},{128,1..., dimensions={0}, use_global_device_ids=true | all-gather | bytes 73728 | tf_op jit(solution)/shard_map/all_gather | solution.py:553
  17.3 0.3 collective-permute-done.od_ref
  17.7 0.7 %shard_map.103 = (f32[12,16,128]{2,1,0:T(8,128)S(1)}, f32[21,8,128]{2,1,0:T(8,128)S(1)}, f32[21,8,128]{2,1,0:T(8,128)S(1)}) custom-call(f32[256,128]{1,0:T(8,128)S(1)} %get-tuple-element.35.t_ref, f32[256,128]{1,0:T(8,128)S(1)} %get-tuple-element.36.s_ref, f32[256,128]{1,0:T(8,128)S(1)} %get-tuple-element.32.u_ref.refs_0_, ...), custom_call_target="tpu_custom_call" | custom-call | flops 1048576 | bytes 1048576 | tf_op jit(solution)/shard_map/pallas_call | solution.py:528
  18.4 4.8 %collective-permute-start.2 = (f32[21,8,128]{2,1,0:T(8,128)S(1)}, f32[21,8,128]{2,1,0:T(8,128)S(1)}, u32[]{:S(2)}, u32[]{:S(2)}) collective-permute-start(f32[21,8,128]{2,1,0:T(8,128)S(1)} %get-tuple-element.43), channel_id=1, source_target_pairs={{0,1},{1,0},{2,3},{3,2},{4,5},{5,4},{6,7},{7,6},{8,9},{9,8},{10,11... | collective-permute-start | bytes 258056 | tf_op jit(solution)/shard_map/ppermute | solution.py:572
  23.2 5.2 %collective-permute-start.1 = (f32[21,8,128]{2,1,0:T(8,128)S(1)}, f32[21,8,128]{2,1,0:T(8,128)S(1)}, u32[]{:S(2)}, u32[]{:S(2)}) collective-permute-start(f32[21,8,128]{2,1,0:T(8,128)S(1)} %get-tuple-element.42), channel_id=1, source_target_pairs={{1,2},{2,1},{3,4},{4,3},{5,6},{6,5},{7,511},{9,10},{10,9},{11,12},... | collective-permute-start | bytes 258056 | tf_op jit(solution)/shard_map/ppermute | solution.py:573
  28.4 4.1 %shard_map.104 = (f32[256,128]{1,0:T(8,128)S(1)}, f32[256,128]{1,0:T(8,128)S(1)}, f32[256,128]{1,0:T(8,128)S(1)}, f32[256,128]{1,0:T(8,128)S(1)}, f32[47,16,128]{2,1,0:T(8,128)S(1)}) custom-call(f32[256,128]{1,0:T(8,128)S(1)} %get-tuple-element.35.t_ref, f32[256,128]{1,0:T(8,128)S(1)} %get-tuple-element.36.s_ref, ...), custom_call_target="tpu_custom_call" | custom-call | flops 16777216 | bytes 1048576 | tf_op jit(solution)/shard_map/pallas_call | solution.py:528
  32.5 0.0 collective-permute-done.2.refs_4_
  32.5 0.9 %shard_map.105 = (f32[256,128]{1,0:T(8,128)}, f32[256,128]{1,0:T(8,128)}, f32[256,128]{1,0:T(8,128)}, f32[256,128]{1,0:T(8,128)}, f32[256,128]{1,0:T(8,128)S(1)}...) custom-call(f32[256,128]{1,0:T(8,128)S(1)} %get-tuple-element.32.u_r, ...), custom_call_target="tpu_custom_call", output_to_operand_aliasing={{4}: (5, {}), {5}: (6, {}), {6}: (7, {}), {7}: (8, {})} | custom-call | flops 2097152 | bytes 1048576 | tf_op jit(solution)/shard_map/pallas_call | solution.py:528
  33.4 1.0 %collective-permute-done.1.refs_4_ = f32[21,8,128]{2,1,0:T(8,128)S(1)} collective-permute-done((f32[21,8,128]{2,1,0:T(8,128)S(1)}, f32[21,8,128]{2,1,0:T(8,128)S(1)}, u32[]{:S(2)}, u32[]{:S(2)}) %collective-permute-start.1) | collective-permute-done | bytes 86048 | tf_op jit(solution)/shard_map/ppermute | solution.py:573
  34.4 0.8 %shard_map.106 = (f32[256,128]{1,0:T(8,128)}, f32[256,128]{1,0:T(8,128)}, f32[256,128]{1,0:T(8,128)}, f32[256,128]{1,0:T(8,128)}, f32[256,128]{1,0:T(8,128)S(1)}...) custom-call(f32[256,128]{1,0:T(8,128)S(1)} %get-tuple-element.32.u_r, ...), custom_call_target="tpu_custom_call", output_to_operand_aliasing={{0}: (5, {}), {1}: (6, {}), {2}: (7, {}), {3}: (8, {}), {4}... | custom-call | flops 2097152 | bytes 1048576 | tf_op jit(solution)/shard_map/pallas_call | solution.py:528
Async XLA Ops:
  2.1 15.6 %collective-permute-start = (f32[16,384]{1,0:T(8,128)S(1)}, f32[16,384]{1,0:T(8,128)S(1)}, u32[]{:S(2)}, u32[]{:S(2)}) collective-permute-start(f32[16,384]{1,0:T(8,128)S(1)} %get-tuple-element.39), channel_id=1, source_target_pairs={{0,504},{8,16},{16,8},{24,32},{32,24},{40,48},{48,40},{56,64},{64,... | collective-permute-start | bytes 73736 | tf_op jit(solution)/shard_map/ppermute | solution.py:552
  18.4 14.1 %collective-permute-start.2 = (f32[21,8,128]{2,1,0:T(8,128)S(1)}, f32[21,8,128]{2,1,0:T(8,128)S(1)}, u32[]{:S(2)}, u32[]{:S(2)}) collective-permute-start(f32[21,8,128]{2,1,0:T(8,128)S(1)} %get-tuple-element.43), channel_id=1, source_target_pairs={{0,1},{1,0},{2,3},{3,2},{4,5},{5,4},{6,7},{7,6},{8,9},{9,8},{10,11... | collective-permute-start | bytes 258056 | tf_op jit(solution)/shard_map/ppermute | solution.py:572
  23.2 11.2 %collective-permute-start.1 = (f32[21,8,128]{2,1,0:T(8,128)S(1)}, f32[21,8,128]{2,1,0:T(8,128)S(1)}, u32[]{:S(2)}, u32[]{:S(2)}) collective-permute-start(f32[21,8,128]{2,1,0:T(8,128)S(1)} %get-tuple-element.42), channel_id=1, source_target_pairs={{1,2},{2,1},{3,4},{4,3},{5,6},{6,5},{7,511},{9,10},{10,9},{11,12},... | collective-permute-start | bytes 258056 | tf_op jit(solution)/shard_map/ppermute | solution.py:573

commit v6 on v5

--- a/solution.py
+++ b/solution.py
@@ -81,9 +81,10 @@
 def pack_columns(rows, phase):
     lane = lanes()
     packed = jnp.zeros((K, W), F32)
-    for j, row in enumerate(rows):
+    moved = [roll(row, WIN * j + phase + 3) for j, row in enumerate(rows)]
+    for j, row in enumerate(moved):
         first = WIN * j + phase
-        packed = jnp.where((lane >= first) & (lane < first + WIN), roll(row, first + 3), packed)
+        packed = jnp.where((lane >= first) & (lane < first + WIN), row, packed)
     return packed
 
 
@@ -145,17 +146,6 @@
     return out
 
 
-def seam_flux(q, c, wet):
-    step = roll(q, -1) - q
-    rise, fall = rise_fall(roll(step, 1), step, roll(step, -1))
-    down, up = limited(roll(fall, 1), rise)
-    near, far = weights(c)
-    out_right = q + (near * down + far * up)
-    near, far = weights(roll(c, 1))
-    out_left = q - (near * up + far * down)
-    return fall, c * wet * roll(wet, -1) * jnp.where(c > 0.0, out_right, roll(out_left, -1))
-
-
 def in_step(walks):
     out = [None] * len(walks)
     live = list(range(len(walks)))
@@ -172,16 +162,36 @@
 class Zonal:
     def __init__(self, packs, u_ref, d_ref):
         self.packs, self.u_ref, self.d_ref = packs, u_ref, d_ref
+        self.flux = {}
+        self.fall = {}
+
+    def seam_walks(self):
+        return [self.seam(n, side) for n in range(2) for side in (1, 2)]
+
+    def seam(self, n, side):
+        q, c, wet = self.packs[n][side], self.packs[2][side], wet_of(self.packs[3][side])
+        q_next, c_west, wet_next = roll(q, -1), roll(c, 1), roll(wet, -1)
+        yield
+        step = q_next - q
+        before, after = roll(step, 1), roll(step, -1)
+        yield
+        rise, fall = rise_fall(before, step, after)
+        fall_before = roll(fall, 1)
+        yield
+        down, up = limited(fall_before, rise)
+        near, far = weights(c_west)
+        from_right = roll(q - (near * up + far * down), -1)
+        yield
+        near, far = weights(c)
+        self.flux[n, side] = c * wet * wet_next * jnp.where(
+            c > 0.0, q + (near * down + far * up), from_right
+        )
+        self.fall[n, side] = fall_before
+
+    def fixes(self, n):
         lane = lanes()
         third = lane - WIN * ((lane * 43) >> 8) == 2
-        _, uw, ue = packs[2]
-        _, dw, de = packs[3]
-        ww, we = wet_of(dw), wet_of(de)
-        self.fix = []
-        for n in range(2):
-            fall_w, flux_w = seam_flux(packs[n][1], uw, ww)
-            _, flux_e = seam_flux(packs[n][2], ue, we)
-            self.fix.append((jnp.where(third, flux_e, roll(fall_w, 1)), flux_w))
+        return jnp.where(third, self.flux[n, 2], self.fall[n, 1]), self.flux[n, 1]
 
     def row(self, refs, j):
         lane = lanes()
@@ -191,7 +201,6 @@
         halo_wet = unpack(self.packs[3][0], j)
         halo_u = unpack(self.packs[2][0], j)
         halos = [unpack(self.packs[n][0], j) for n in range(2)]
-        fixes = [[unpack(x, j) for x in self.fix[n]] for n in range(2)]
         q = [load_row(ref, j) for ref in refs]
         yield
         halo_wet = wet_of(halo_wet)
@@ -207,6 +216,10 @@
         near, far = weights(u)
         near_w, far_w = weights(u_west)
         face = u * wet * wet_east
+        while (1, 2) not in self.flux:
+            yield
+        fixes = [[unpack(x, j) for x in self.fixes(n)] for n in range(2)]
+        yield
         forward = u > 0.0
         cells = [
             limited(jnp.where(lane == 0, fixes[n][0], falls[n]), edges[n][0]) for n in range(2)
@@ -247,36 +260,57 @@
     zonal = Zonal(packs, u_ref, d_ref)
     packs = [p[0] for p in packs]
     wet = {j: wet_of(depth_row(d_ref, j)) for j in (0, 1, 2, 13, 14, 15)}
-    halo_wet = {j: wet_of(unpack(packs[3], j)) for j in (0, 15)}
-    halves = []
     all_rows = (15, 14, 13, 0, 1, 2)
-    swept = []
-    for at in range(0, 6, 6):
-        swept += in_step([zonal.row((t_ref, s_ref), j) for j in all_rows[at : at + 6]])
-    planes_of = (swept[:3], swept[3:])
-    for side, rows in enumerate(((J - 1, J - 2, J - 3), (0, 1, 2))):
-        planes = planes_of[side]
-        for j, (t, s) in zip(rows, planes):
-            swept_ref[j if j < 3 else j - 10] = t
-            swept_ref[6 + (j if j < 3 else j - 10)] = s
-        half = [p[0] for p in planes] + [p[1] for p in planes]
-        j, inward = rows[0], rows[1]
-        masks = zonal_masks(wet[j], halo_wet[j], lane)
-        to_inner = wet[j] * wet[inward]
-        for ref, pack in ((u_ref, packs[2]), (v_ref, packs[4])):
-            f = load_row(ref, j)
-            partial = zonal_lap(f, unpack(pack, j), masks, lane) + to_inner * (load_row(ref, inward) - f)
-            half += [f, partial]
+
+    def partial_lap(ref, pack, j, inward):
+        f = load_row(ref, j)
+        halo, dry = unpack(pack, j), unpack(packs[3], j)
+        yield
+        right, left = east(f, halo, lane), west(f, halo, lane)
+        dry = wet_of(dry)
+        wet_r, wet_l = east(wet[j], dry, lane), west(wet[j], dry, lane)
+        yield
+        return wet[j] * (
+            wet_r * (right - f)
+            + wet_l * (left - f)
+            + wet[inward] * (load_row(ref, inward) - f)
+        )
+
+    def corner_tile(j):
         depth = depth_row(d_ref, j)[:8]
-        corner = jnp.where(sub8 < 4, depth, roll(depth, W // 2))
+        far = roll(depth, W // 2)
+        parts = []
         for at, (pack, top) in enumerate(
             ((packs[2], 0), (packs[4], 0), (packs[2], 8), (packs[4], 8), (packs[3], 0))
         ):
             home = -(WIN * j + 3)
             part = pack[top : top + 8]
-            corner = jnp.where(lane8 == at, roll(part, home + at), corner)
-            corner = jnp.where(lane8 == W - 1 - at, roll(part, home - at), corner)
-        halves.append((half, corner))
+            parts += [(at, roll(part, home + at)), (W - 1 - at, roll(part, home - at))]
+        yield
+        corner = jnp.where(sub8 < 4, depth, far)
+        for at, part in parts:
+            corner = jnp.where(lane8 == at, part, corner)
+        return corner
+
+    sides = ((J - 1, J - 2), (0, 1))
+    flows = ((u_ref, packs[2]), (v_ref, packs[4]))
+    seam_walks = zonal.seam_walks()
+    done = in_step(
+        seam_walks
+        + [zonal.row((t_ref, s_ref), j) for j in all_rows]
+        + [partial_lap(*flow, *rows) for rows in sides for flow in flows]
+        + [corner_tile(rows[0]) for rows in sides]
+    )[len(seam_walks) :]
+    halves = []
+    for side, (edge, _) in enumerate(sides):
+        planes = done[3 * side : 3 * side + 3]
+        for j, (t, s) in zip(all_rows[3 * side : 3 * side + 3], planes):
+            swept_ref[j if j < 3 else j - 10] = t
+            swept_ref[6 + (j if j < 3 else j - 10)] = s
+        half = [p[0] for p in planes] + [p[1] for p in planes]
+        for n, (ref, _) in enumerate(flows):
+            half += [load_row(ref, edge), done[6 + 2 * side + n]]
+        halves.append((half, done[10 + side]))
     lat = lax.axis_index("lat")
     even = (lat & 1) == 0
     (north, north_c), (south, south_c) = halves
@@ -335,6 +369,8 @@
     aux_ref,
     visc_ref,
     sem,
+    mask_ref,
+    lap_ref,
 ):
     copy = pltpu.make_async_copy(visc_hbm, visc_ref, sem)
     copy.start()
@@ -345,8 +381,9 @@
     for j in (0, 1, 2, 13, 14, 15):
         for n in range(2):
             rows[n][j] = swept_ref[6 * n + (j if j < 3 else j - 10)]
-    for at in range(3, 13, 3):
-        group = range(at, min(at + 3, 13))
+    in_step(zonal.seam_walks())
+    for at in range(3, 13, 10):
+        group = range(at, min(at + 10, 13))
         for j, (t, s) in zip(group, in_step([zonal.row((t_ref, s_ref), j) for j in group])):
             rows[0][j], rows[1][j] = t, s
     wet = [wet_of(depth_row(d_ref, j)) for j in range(J)]
@@ -369,45 +406,70 @@
             cell, before = after, flux
     wet_w, wet_e = wet_of(packs[3][1]), wet_of(packs[3][2])
     low = low_half(lane)
+    halo_wet = {}
+
+    def mask_row(j):
+        halo = unpack(packs[3][0], j)
+        yield
+        halo = wet_of(halo)
+        if j in (0, J - 1):
+            halo_wet[j] = halo
+        right, left = east(wet[j], halo, lane), west(wet[j], halo, lane)
+        yield
+        mask_ref[j] = wet[j] * right
+        mask_ref[J + j] = wet[j] * left
+        if j < J - 1:
+            mask_ref[2 * J + j] = wet[j] * wet[j + 1]
+
+    def lap_row(n, packed, load, j, first, last):
+        here = load(n, j)
+        halo = unpack(packed, j)
+        yield
+        right, left = east(here, halo, lane), west(here, halo, lane)
+        yield
+        total = mask_ref[j] * (right - here) - mask_ref[J + j] * (here - left)
+        if j > first:
+            total = total - mask_ref[2 * J + j - 1] * (here - load(n, j - 1))
+        if j < last:
+            total = total + mask_ref[2 * J + j] * (load(n, j + 1) - here)
+        return total
+
+    def walk(makers):
+        for at in range(0, len(makers), 16):
+            in_step([m() for m in makers[at : at + 16]])
+
+    walk([functools.partial(mask_row, j) for j in range(J)])
+    flows = ((u_ref, packs[2], u_out), (v_ref, packs[4], v_out))
+
+    def inner(n, j):
+        lap_ref[J * n + j] = yield from lap_row(n, flows[n][1][0], lambda n, j: load_row(flows[n][0], j), j, 0, J - 1)
+
+    walk([functools.partial(inner, n, j) for j in range(J) for n in range(2)])
+    halo_laps = [
+        jnp.where(low, seam_lap(pack[1], wet_w), seam_lap(pack[2], wet_e)) for _, pack, _ in flows
+    ]
     copy.wait()
     visc = viscosity(visc_ref)
-    halo_wet = [wet_of(unpack(packs[3][0], j)) for j in range(J)]
-    masks = [zonal_masks(wet[j], halo_wet[j], lane) for j in range(J)]
-    pair = [wet[j] * wet[j + 1] for j in range(J - 1)]
-    for n, (ref, pack, out) in enumerate(((u_ref, packs[2], u_out), (v_ref, packs[4], v_out))):
+
+    def outer(n, j):
+        total = yield from lap_row(n, halo_laps[n], lambda n, j: lap_ref[J * n + j], j, 1, J - 2)
         base = 2 * AUX_TRACER + AUX_FLOW * n
-        halo_lap = jnp.where(low, seam_lap(pack[1], wet_w), seam_lap(pack[2], wet_e))
-        f = [load_row(ref, j) for j in range(J)]
-        lap = []
-        step = None
-        for j in range(J):
-            total = zonal_lap(f[j], unpack(pack[0], j), masks[j], lane)
-            if step is not None:
-                total = total - step
-            if j < J - 1:
-                step = pair[j] * (f[j + 1] - f[j])
-                total = total + step
-            lap.append(total)
-        step = None
-        for j in range(1, J - 1):
-            total = zonal_lap(lap[j], unpack(halo_lap, j), masks[j], lane)
-            if step is not None:
-                total = total - step
-            if j < J - 2:
-                step = pair[j] * (lap[j + 1] - lap[j])
-                total = total + step
-            if j == 1:
-                aux_ref[base + 2] = total
-            elif j == J - 2:
-                aux_ref[base + 5] = total
-            else:
-                store_row(out, j, f[j] - visc * total)
-        aux_ref[base + 0] = lap[0]
-        aux_ref[base + 1] = lap[1]
-        aux_ref[base + 3] = lap[J - 1]
-        aux_ref[base + 4] = lap[J - 2]
-        aux_ref[base + 6] = unpack(halo_lap, 0)
-        aux_ref[base + 7] = unpack(halo_lap, J - 1)
+        if j == 1:
+            aux_ref[base + 2] = total
+        elif j == J - 2:
+            aux_ref[base + 5] = total
+        else:
+            store_row(flows[n][2], j, load_row(flows[n][0], j) - visc * total)
+
+    walk([functools.partial(outer, n, j) for j in range(1, J - 1) for n in range(2)])
+    for n, (_, pack, _) in enumerate(flows):
+        base = 2 * AUX_TRACER + AUX_FLOW * n
+        aux_ref[base + 0] = lap_ref[J * n]
+        aux_ref[base + 1] = lap_ref[J * n + 1]
+        aux_ref[base + 3] = lap_ref[J * n + J - 1]
+        aux_ref[base + 4] = lap_ref[J * n + J - 2]
+        aux_ref[base + 6] = unpack(halo_laps[n], 0)
+        aux_ref[base + 7] = unpack(halo_laps[n], J - 1)
         aux_ref[base + 8] = unpack(pack[0], 0)
         aux_ref[base + 9] = unpack(pack[0], J - 1)
     aux_ref[2 * AUX_TRACER + 2 * AUX_FLOW] = halo_wet[0]
@@ -578,7 +640,12 @@
         [FLAT] * 4 + [(AUX, K, W)],
         1 << 24,
         (t, s, u, v, depth, pltpu.with_memory_space_constraint(visc, pltpu.HBM), own, ev, od, swept),
-        [pltpu.SMEM((K,), F32), pltpu.SemaphoreType.DMA],
+        [
+            pltpu.SMEM((K,), F32),
+            pltpu.SemaphoreType.DMA,
+            pltpu.VMEM((3 * J, K, W), F32),
+            pltpu.VMEM((2 * J, K, W), F32),
+        ],
     )
     flow = (u, v, depth, aux)
     outs = call(

time: 35.7 us -> 35.7 us (level)
  Pallas kernels: 7.9 us -> 5.75 us
  waiting for transfers between devices: 1.33 us -> 3.45 us
    pallas_call x5, Pallas kernels: 7.9 us -> 5.75 us  [call(): pl.pallas_call(kernel, out_shape=[jax.ShapeDtypeStruct(s, F32) for s in o...]
    ppermute x1, waiting for transfers between devices: 1.01 us -> 3.13 us  [body(): got_o = lax.ppermute(edge_o, ('lon', 'lat'), pairs_o)]
  transfers between devices with their start and end apart: 3 -> 3, of which waited for: 2 -> 2; matrix products, arithmetic and copies ran while one was open for 0% -> 0% of each run, Pallas kernels for 14% -> 8%
where the time goes in v6:
time: 35.7 us; the launch traced here: 35.2 us
  starting transfers between devices  23.4 us (66%)
  Pallas kernels  5.75 us (16%)
  waiting for transfers between devices  3.45 us (10%)
  blocking collectives  1.84 us (5%)
  between operations  0.7 us (2%)
    ppermute x1, starting transfers between devices, body(): lax.ppermute(od, 'lon', [(i, ((i + 1 ^ 1) - 1) % n_lon) for i in range(n_...  13.4 us
    pallas_call x5, Pallas kernels, call(): pl.pallas_call(kernel, out_shape=[jax.ShapeDtypeStruct(s, F32) for s in o...  5.75 us
    ppermute x1, starting transfers between devices, body(): got_o = lax.ppermute(edge_o, ('lon', 'lat'), pairs_o)  5.2 us
    ppermute x1, starting transfers between devices, body(): got_e = lax.ppermute(edge_e, ('lon', 'lat'), pairs_e)  4.81 us
    ppermute x1, waiting for transfers between devices, body(): got_o = lax.ppermute(edge_o, ('lon', 'lat'), pairs_o)  3.13 us
    all_gather x1, blocking collectives, body(): lax.all_gather(ev, 'lon', axis_index_groups=[[i, i + 1] for i in range(0,...  1.84 us
  transfers between devices with their start and end apart: 3, of which 2 were waited for; matrix products, arithmetic and copies ran while one was open for 0% of the time, Pallas kernels for 8%

profile of v6, /device:TPU:6, one launch (start us, length us, event | category | flops | bytes accessed | tf_op | source)
XLA Modules:
  0.0 35.2 jit_solution(9943784593825901400)
XLA Ops:
  0.6 1.4 %shard_map.102 = (f32[256,128]{1,0:T(8,128)S(1)}, f32[256,128]{1,0:T(8,128)S(1)}, f32[256,128]{1,0:T(8,128)S(1)}, f32[256,128]{1,0:T(8,128)S(1)}, f32[16,128]{1,...) custom-call(f32[256,128]{1,0:T(8,128)} %bitcast.12, f32[256,128]{1,0:T(8,128)} %bitcast.13, ...), custom_call_target="tpu_custom_call" | custom-call | flops 1048576 | bytes 1048576 | tf_op jit(solution)/shard_map/pallas_call | solution.py:590
  2.1 13.4 %collective-permute-start = (f32[16,384]{1,0:T(8,128)S(1)}, f32[16,384]{1,0:T(8,128)S(1)}, u32[]{:S(2)}, u32[]{:S(2)}) collective-permute-start(f32[16,384]{1,0:T(8,128)S(1)} %get-tuple-element.39), channel_id=1, source_target_pairs={{0,504},{8,16},{16,8},{24,32},{32,24},{40,48},{48,40},{56,64},{64,... | collective-permute-start | bytes 73736 | tf_op jit(solution)/shard_map/ppermute | solution.py:614
  15.5 1.8 %all_gather.3.ev_ref = f32[32,384]{1,0:T(8,128)S(1)} all-gather(f32[16,384]{1,0:T(8,128)S(1)} %get-tuple-element.38), channel_id=1, replica_groups={{0,8},{16,24},{32,40},{48,56},{64,72},{80,88},{96,104},{112,120},{128,1..., dimensions={0}, use_global_device_ids=true | all-gather | bytes 73728 | tf_op jit(solution)/shard_map/all_gather | solution.py:615
  17.3 0.3 collective-permute-done.od_ref
  17.7 0.7 %shard_map.103 = (f32[12,16,128]{2,1,0:T(8,128)S(1)}, f32[21,8,128]{2,1,0:T(8,128)S(1)}, f32[21,8,128]{2,1,0:T(8,128)S(1)}) custom-call(f32[256,128]{1,0:T(8,128)S(1)} %get-tuple-element.35.t_ref, f32[256,128]{1,0:T(8,128)S(1)} %get-tuple-element.36.s_ref, f32[256,128]{1,0:T(8,128)S(1)} %get-tuple-element.32.u_ref.refs_0_, ...), custom_call_target="tpu_custom_call" | custom-call | flops 1048576 | bytes 1048576 | tf_op jit(solution)/shard_map/pallas_call | solution.py:590
  18.3 4.8 %collective-permute-start.2 = (f32[21,8,128]{2,1,0:T(8,128)S(1)}, f32[21,8,128]{2,1,0:T(8,128)S(1)}, u32[]{:S(2)}, u32[]{:S(2)}) collective-permute-start(f32[21,8,128]{2,1,0:T(8,128)S(1)} %get-tuple-element.43), channel_id=1, source_target_pairs={{0,1},{1,0},{2,3},{3,2},{4,5},{5,4},{6,7},{7,6},{8,9},{9,8},{10,11... | collective-permute-start | bytes 258056 | tf_op jit(solution)/shard_map/ppermute | solution.py:634
  23.1 5.2 %collective-permute-start.1 = (f32[21,8,128]{2,1,0:T(8,128)S(1)}, f32[21,8,128]{2,1,0:T(8,128)S(1)}, u32[]{:S(2)}, u32[]{:S(2)}) collective-permute-start(f32[21,8,128]{2,1,0:T(8,128)S(1)} %get-tuple-element.42), channel_id=1, source_target_pairs={{1,2},{2,1},{3,4},{4,3},{5,6},{6,5},{7,511},{9,10},{10,9},{11,12},... | collective-permute-start | bytes 258056 | tf_op jit(solution)/shard_map/ppermute | solution.py:635
  28.4 2.0 %shard_map.104 = (f32[256,128]{1,0:T(8,128)S(1)}, f32[256,128]{1,0:T(8,128)S(1)}, f32[256,128]{1,0:T(8,128)S(1)}, f32[256,128]{1,0:T(8,128)S(1)}, f32[47,16,128]{2,1,0:T(8,128)S(1)}) custom-call(f32[256,128]{1,0:T(8,128)S(1)} %get-tuple-element.35.t_ref, f32[256,128]{1,0:T(8,128)S(1)} %get-tuple-element.36.s_ref, ...), custom_call_target="tpu_custom_call" | custom-call | flops 16777216 | bytes 1048576 | tf_op jit(solution)/shard_map/pallas_call | solution.py:590
  30.3 0.0 collective-permute-done.2.refs_4_
  30.3 0.9 %shard_map.105 = (f32[256,128]{1,0:T(8,128)}, f32[256,128]{1,0:T(8,128)}, f32[256,128]{1,0:T(8,128)}, f32[256,128]{1,0:T(8,128)}, f32[256,128]{1,0:T(8,128)S(1)}...) custom-call(f32[256,128]{1,0:T(8,128)S(1)} %get-tuple-element.32.u_r, ...), custom_call_target="tpu_custom_call", output_to_operand_aliasing={{4}: (5, {}), {5}: (6, {}), {6}: (7, {}), {7}: (8, {})} | custom-call | flops 2097152 | bytes 1048576 | tf_op jit(solution)/shard_map/pallas_call | solution.py:590
  31.2 3.1 %collective-permute-done.1.refs_4_ = f32[21,8,128]{2,1,0:T(8,128)S(1)} collective-permute-done((f32[21,8,128]{2,1,0:T(8,128)S(1)}, f32[21,8,128]{2,1,0:T(8,128)S(1)}, u32[]{:S(2)}, u32[]{:S(2)}) %collective-permute-start.1) | collective-permute-done | bytes 86048 | tf_op jit(solution)/shard_map/ppermute | solution.py:635
  34.3 0.8 %shard_map.106 = (f32[256,128]{1,0:T(8,128)}, f32[256,128]{1,0:T(8,128)}, f32[256,128]{1,0:T(8,128)}, f32[256,128]{1,0:T(8,128)}, f32[256,128]{1,0:T(8,128)S(1)}...) custom-call(f32[256,128]{1,0:T(8,128)S(1)} %get-tuple-element.32.u_r, ...), custom_call_target="tpu_custom_call", output_to_operand_aliasing={{0}: (5, {}), {1}: (6, {}), {2}: (7, {}), {3}: (8, {}), {4}... | custom-call | flops 2097152 | bytes 1048576 | tf_op jit(solution)/shard_map/pallas_call | solution.py:590
Async XLA Ops:
  2.1 15.6 %collective-permute-start = (f32[16,384]{1,0:T(8,128)S(1)}, f32[16,384]{1,0:T(8,128)S(1)}, u32[]{:S(2)}, u32[]{:S(2)}) collective-permute-start(f32[16,384]{1,0:T(8,128)S(1)} %get-tuple-element.39), channel_id=1, source_target_pairs={{0,504},{8,16},{16,8},{24,32},{32,24},{40,48},{48,40},{56,64},{64,... | collective-permute-start | bytes 73736 | tf_op jit(solution)/shard_map/ppermute | solution.py:614
  18.3 12.0 %collective-permute-start.2 = (f32[21,8,128]{2,1,0:T(8,128)S(1)}, f32[21,8,128]{2,1,0:T(8,128)S(1)}, u32[]{:S(2)}, u32[]{:S(2)}) collective-permute-start(f32[21,8,128]{2,1,0:T(8,128)S(1)} %get-tuple-element.43), channel_id=1, source_target_pairs={{0,1},{1,0},{2,3},{3,2},{4,5},{5,4},{6,7},{7,6},{8,9},{9,8},{10,11... | collective-permute-start | bytes 258056 | tf_op jit(solution)/shard_map/ppermute | solution.py:634
  23.1 11.2 %collective-permute-start.1 = (f32[21,8,128]{2,1,0:T(8,128)S(1)}, f32[21,8,128]{2,1,0:T(8,128)S(1)}, u32[]{:S(2)}, u32[]{:S(2)}) collective-permute-start(f32[21,8,128]{2,1,0:T(8,128)S(1)} %get-tuple-element.42), channel_id=1, source_target_pairs={{1,2},{2,1},{3,4},{4,3},{5,6},{6,5},{7,511},{9,10},{10,9},{11,12},... | collective-permute-start | bytes 258056 | tf_op jit(solution)/shard_map/ppermute | solution.py:635

commit v7 on v6

--- a/solution.py
+++ b/solution.py
@@ -491,7 +491,7 @@
     half = pl.ds(8 * (1 - side), 8)
     copies = [
         pltpu.make_async_copy(
-            src.reshape(K, J, W).at[:, half], dst.reshape(K, J, W).at[:, half], sems.at[n]
+            src.reshape(K, J, W).at[:, half], dst.reshape(K, J, W).at[:, half], sems.at[4 * side + n]
         )
         for n, (src, dst) in enumerate(zip(outs, finals))
     ]
@@ -560,24 +560,46 @@
         store_row(out, edge, f - visc * total)
         store_row(out, inward, f_in - visc * (partial - inner_step))
         copies[2 + n].start()
-    for copy in copies:
-        copy.wait()
-
-
-def finish_kernel(north_if_even, *refs):
-    u_ref, v_ref, d_ref, aux_ref, got_ref = refs[:5]
-    finals, outs, sems = refs[-9:-5], refs[-5:-1], refs[-1]
-    even = (lax.axis_index("lat") & 1) == 0
+    return copies
+
+
+def first_kernel(u_ref, v_ref, d_ref, aux_ref, even_ref, o_ref, *refs):
+    fixed = (u_ref, v_ref, d_ref, aux_ref, refs[-5:-1], refs[-9:-5], refs[-1])
+    lat = lax.axis_index("lat")
+    even = (lat & 1) == 0
+    top = lat == lax.axis_size("lat") - 1
 
     @pl.when(even)
     def _():
-        side = 0 if north_if_even else 1
-        finish_side(side, got_ref, u_ref, v_ref, d_ref, aux_ref, outs, finals, sems)
-
-    @pl.when(jnp.logical_not(even))
+        copies = finish_side(0, even_ref, *fixed) + finish_side(1, o_ref, *fixed)
+        for copy in copies:
+            copy.wait()
+
+    @pl.when(jnp.logical_not(even | top))
     def _():
-        side = 1 if north_if_even else 0
-        finish_side(side, got_ref, u_ref, v_ref, d_ref, aux_ref, outs, finals, sems)
+        for copy in finish_side(0, o_ref, *fixed):
+            copy.wait()
+
+
+def last_kernel(u_ref, v_ref, d_ref, aux_ref, odd_ref, f_ref, o_ref, *refs):
+    fixed = (u_ref, v_ref, d_ref, aux_ref, refs[-5:-1], refs[-9:-5], refs[-1])
+    lat = lax.axis_index("lat")
+    odd = (lat & 1) == 1
+    top = lat == lax.axis_size("lat") - 1
+
+    @pl.when(odd & jnp.logical_not(top))
+    def _():
+        for copy in finish_side(1, odd_ref, *fixed):
+            copy.wait()
+
+    low_lon = lax.axis_index("lon") < lax.axis_size("lon") // 2
+    for mine, seam_ref in ((low_lon, o_ref), (jnp.logical_not(low_lon), f_ref)):
+
+        @pl.when(top & mine)
+        def _(seam_ref=seam_ref):
+            copies = finish_side(1, odd_ref, *fixed) + finish_side(0, seam_ref, *fixed)
+            for copy in copies:
+                copy.wait()
 
 
 VMEM = pl.BlockSpec(memory_space=pltpu.VMEM)
@@ -623,16 +645,19 @@
         1 << 20,
         (t, s, u, v, depth, own, ev, od),
     )
-    pairs_e, pairs_o = [], []
+    to_even, to_odd, pairs_o, pairs_f = [], [], [], []
     top = n_lat - 1
     for p in range(n_lon):
         for l in range(n_lat):
-            pairs_e.append((p * n_lat + l, p * n_lat + (l ^ 1)))
+            (to_even if l & 1 else to_odd).append((p * n_lat + l, p * n_lat + (l ^ 1)))
             if 0 < l < top:
                 pairs_o.append((p * n_lat + l, p * n_lat + ((l + 1) ^ 1) - 1))
-        pairs_o.append((p * n_lat + top, (n_lon - 1 - p) * n_lat + top))
-    got_e = lax.ppermute(edge_e, ("lon", "lat"), pairs_e)
+        across = (p * n_lat + top, (n_lon - 1 - p) * n_lat + top)
+        (pairs_f if p < n_lon // 2 else pairs_o).append(across)
+    got_even = lax.ppermute(edge_e, ("lon", "lat"), to_even)
     got_o = lax.ppermute(edge_o, ("lon", "lat"), pairs_o)
+    got_odd = lax.ppermute(edge_e, ("lon", "lat"), to_odd)
+    got_f = lax.ppermute(edge_o, ("lon", "lat"), pairs_f)
     *parts, aux = call(
         inner_kernel,
         [VMEM] * 5 + [HBM] + [VMEM] * 4,
@@ -649,24 +674,24 @@
     )
     flow = (u, v, depth, aux)
     outs = call(
-        functools.partial(finish_kernel, True),
-        [VMEM] * 9,
+        first_kernel,
+        [VMEM] * 10,
         [HBM] * 4 + [VMEM] * 4,
         [FLAT] * 8,
         1 << 21,
-        (*flow, got_e, *parts),
-        [pltpu.SemaphoreType.DMA((4,))],
-        {5: 4, 6: 5, 7: 6, 8: 7},
+        (*flow, got_even, got_o, *parts),
+        [pltpu.SemaphoreType.DMA((8,))],
+        {6 + n: 4 + n for n in range(4)},
     )
     outs = call(
-        functools.partial(finish_kernel, False),
-        [VMEM] * 5 + [HBM] * 4 + [VMEM] * 4,
+        last_kernel,
+        [VMEM] * 7 + [HBM] * 4 + [VMEM] * 4,
         [HBM] * 4 + [VMEM] * 4,
         [FLAT] * 8,
         1 << 21,
-        (*flow, got_o, *outs),
-        [pltpu.SemaphoreType.DMA((4,))],
-        {5 + n: n for n in range(8)},
+        (*flow, got_odd, got_f, got_o, *outs),
+        [pltpu.SemaphoreType.DMA((8,))],
+        {7 + n: n for n in range(8)},
     )
     return tuple(x.reshape(K, J, W) for x in outs[:4])
 

time: 35.7 us -> 35.5 us (level)
  the two profiles are of different devices: /device:TPU:6 before, /device:TPU:39 now
where the time goes in v7:
time: 35.5 us; the launch traced here: 35.2 us
  starting transfers between devices  18 us (51%)
  blocking collectives  10 us (28%)
  Pallas kernels  5.23 us (15%)
  waiting for transfers between devices  1.22 us (3%)
  between operations  0.73 us (2%)
    all_gather x1, blocking collectives, body(): lax.all_gather(ev, 'lon', axis_index_groups=[[i, i + 1] for i in range(0,...  10 us
    ppermute x1, starting transfers between devices, body(): got_f = lax.ppermute(edge_o, ('lon', 'lat'), pairs_f)  8.18 us
    pallas_call x5, Pallas kernels, call(): pl.pallas_call(kernel, out_shape=[jax.ShapeDtypeStruct(s, F32) for s in o...  5.23 us
    ppermute x1, starting transfers between devices, body(): got_even = lax.ppermute(edge_e, ('lon', 'lat'), to_even)  4.35 us
    ppermute x1, starting transfers between devices, body(): lax.ppermute(od, 'lon', [(i, ((i + 1 ^ 1) - 1) % n_lon) for i in range(n_...  2.87 us
    ppermute x1, starting transfers between devices, body(): got_o = lax.ppermute(edge_o, ('lon', 'lat'), pairs_o)  1.29 us
    ppermute x1, starting transfers between devices, body(): got_odd = lax.ppermute(edge_e, ('lon', 'lat'), to_odd)  1.29 us
    ppermute x1, waiting for transfers between devices, body(): got_o = lax.ppermute(edge_o, ('lon', 'lat'), pairs_o)  1.21 us
  transfers between devices with their start and end apart: 5, of which 1 were waited for; matrix products, arithmetic and copies ran while one was open for 0% of the time, Pallas kernels for 6%

profile of v7, /device:TPU:39, one launch (start us, length us, event | category | flops | bytes accessed | tf_op | source)
XLA Modules:
  0.0 35.2 jit_solution(12213407182843291843)
XLA Ops:
  0.6 1.4 %shard_map.102 = (f32[256,128]{1,0:T(8,128)S(1)}, f32[256,128]{1,0:T(8,128)S(1)}, f32[256,128]{1,0:T(8,128)S(1)}, f32[256,128]{1,0:T(8,128)S(1)}, f32[16,128]{1,...) custom-call(f32[256,128]{1,0:T(8,128)} %bitcast.8, f32[256,128]{1,0:T(8,128)} %bitcast.9, ...), custom_call_target="tpu_custom_call" | custom-call | flops 1048576 | bytes 1048576 | tf_op jit(solution)/shard_map/pallas_call | solution.py:612
  2.1 2.9 %collective-permute-start = (f32[16,384]{1,0:T(8,128)S(1)}, f32[16,384]{1,0:T(8,128)S(1)}, u32[]{:S(2)}, u32[]{:S(2)}) collective-permute-start(f32[16,384]{1,0:T(8,128)S(1)} %get-tuple-element.39), channel_id=1, source_target_pairs={{0,504},{8,16},{16,8},{24,32},{32,24},{40,48},{48,40},{56,64},{64,... | collective-permute-start | bytes 73736 | tf_op jit(solution)/shard_map/ppermute | solution.py:636
  4.9 10.0 %all_gather.3.ev_ref = f32[32,384]{1,0:T(8,128)S(1)} all-gather(f32[16,384]{1,0:T(8,128)S(1)} %get-tuple-element.38), channel_id=1, replica_groups={{0,8},{16,24},{32,40},{48,56},{64,72},{80,88},{96,104},{112,120},{128,1..., dimensions={0}, use_global_device_ids=true | all-gather | bytes 73728 | tf_op jit(solution)/shard_map/all_gather | solution.py:637
  15.0 0.0 collective-permute-done.od_ref
  15.0 0.7 %shard_map.103 = (f32[12,16,128]{2,1,0:T(8,128)S(1)}, f32[21,8,128]{2,1,0:T(8,128)S(1)}, f32[21,8,128]{2,1,0:T(8,128)S(1)}) custom-call(f32[256,128]{1,0:T(8,128)S(1)} %get-tuple-element.35.t_ref, f32[256,128]{1,0:T(8,128)S(1)} %get-tuple-element.36.s_ref, f32[256,128]{1,0:T(8,128)S(1)} %get-tuple-element.32.u_ref, f32[256,128]{1,0:T(8,128)S(1)} %get-tuple-element.33.v_ref, ...), custom_call_target="tpu_custom_call" | custom-call | flops 1048576 | bytes 1048576 | tf_op jit(solution)/shard_map/pallas_call | solution.py:612
  15.7 4.3 %collective-permute-start.4 = (f32[21,8,128]{2,1,0:T(8,128)S(1)}, f32[21,8,128]{2,1,0:T(8,128)S(1)}, u32[]{:S(2)}, u32[]{:S(2)}) collective-permute-start(f32[21,8,128]{2,1,0:T(8,128)S(1)} %get-tuple-element.42), channel_id=1, source_target_pairs={{1,0},{3,2},{5,4},{7,6},{9,8},{11,10},{13,12},{15,14},{17,16},{19,... | collective-permute-start | bytes 258056 | tf_op jit(solution)/shard_map/ppermute | solution.py:657
  20.1 1.3 %collective-permute-start.3 = (f32[21,8,128]{2,1,0:T(8,128)S(1)}, f32[21,8,128]{2,1,0:T(8,128)S(1)}, u32[]{:S(2)}, u32[]{:S(2)}) collective-permute-start(f32[21,8,128]{2,1,0:T(8,128)S(1)} %get-tuple-element.43), channel_id=1, source_target_pairs={{1,2},{2,1},{3,4},{4,3},{5,6},{6,5},{9,10},{10,9},{11,12},{12,11},... | collective-permute-start | bytes 258056 | tf_op jit(solution)/shard_map/ppermute | solution.py:658
  21.4 1.3 %collective-permute-start.1 = (f32[21,8,128]{2,1,0:T(8,128)S(1)}, f32[21,8,128]{2,1,0:T(8,128)S(1)}, u32[]{:S(2)}, u32[]{:S(2)}) collective-permute-start(f32[21,8,128]{2,1,0:T(8,128)S(1)} %get-tuple-element.42), channel_id=1, source_target_pairs={{0,1},{2,3},{4,5},{6,7},{8,9},{10,11},{12,13},{14,15},{16,17},{18,... | collective-permute-start | bytes 258056 | tf_op jit(solution)/shard_map/ppermute | solution.py:659
  22.7 8.2 %collective-permute-start.2 = (f32[21,8,128]{2,1,0:T(8,128)S(1)}, f32[21,8,128]{2,1,0:T(8,128)S(1)}, u32[]{:S(2)}, u32[]{:S(2)}) collective-permute-start(f32[21,8,128]{2,1,0:T(8,128)S(1)} %get-tuple-element.43), channel_id=1, source_target_pairs={{7,511},{15,503},{23,495},{31,487},{39,479},{47,471},{55,463},{63,... | collective-permute-start | bytes 258056 | tf_op jit(solution)/shard_map/ppermute | solution.py:660
  30.9 2.0 %shard_map.104 = (f32[256,128]{1,0:T(8,128)S(1)}, f32[256,128]{1,0:T(8,128)S(1)}, f32[256,128]{1,0:T(8,128)S(1)}, f32[256,128]{1,0:T(8,128)S(1)}, f32[47,16,128]{2,1,0:T(8,128)S(1)}) custom-call(f32[256,128]{1,0:T(8,128)S(1)} %get-tuple-element.35.t_ref, f32[256,128]{1,0:T(8,128)S(1)} %get-tuple-element.36.s_ref, f32[256,128]{1,0:T(8,128)S(1)} %get-tuple-element.32.u_ref, ...), custom_call_target="tpu_custom_call" | custom-call | flops 16777216 | bytes 1048576 | tf_op jit(solution)/shard_map/pallas_call | solution.py:612
  32.8 0.0 collective-permute-done.4.even_ref
  32.8 1.2 %collective-permute-done.3.o_ref = f32[21,8,128]{2,1,0:T(8,128)S(1)} collective-permute-done((f32[21,8,128]{2,1,0:T(8,128)S(1)}, f32[21,8,128]{2,1,0:T(8,128)S(1)}, u32[]{:S(2)}, u32[]{:S(2)}) %collective-permute-start.3) | collective-permute-done | bytes 86048 | tf_op jit(solution)/shard_map/ppermute | solution.py:658
  34.1 0.1 shard_map.105
  34.1 0.0 collective-permute-done.1.odd_ref
  34.1 0.0 collective-permute-done.2.f_ref
  34.2 1.0 %shard_map.106 = (f32[256,128]{1,0:T(8,128)}, f32[256,128]{1,0:T(8,128)}, f32[256,128]{1,0:T(8,128)}, f32[256,128]{1,0:T(8,128)}, f32[256,128]{1,0:T(8,128)S(1)}...) custom-call(f32[256,128]{1,0:T(8,128)S(1)} %get-tuple-element.32.u_r, ...), custom_call_target="tpu_custom_call", output_to_operand_aliasing={{0}: (7, {}), {1}: (8, {}), {2}: (9, {}), {3}: (10, {}), {4... | custom-call | flops 2097152 | bytes 1048576 | tf_op jit(solution)/shard_map/pallas_call | solution.py:612
Async XLA Ops:
  2.1 12.9 %collective-permute-start = (f32[16,384]{1,0:T(8,128)S(1)}, f32[16,384]{1,0:T(8,128)S(1)}, u32[]{:S(2)}, u32[]{:S(2)}) collective-permute-start(f32[16,384]{1,0:T(8,128)S(1)} %get-tuple-element.39), channel_id=1, source_target_pairs={{0,504},{8,16},{16,8},{24,32},{32,24},{40,48},{48,40},{56,64},{64,... | collective-permute-start | bytes 73736 | tf_op jit(solution)/shard_map/ppermute | solution.py:636
  15.7 17.1 %collective-permute-start.4 = (f32[21,8,128]{2,1,0:T(8,128)S(1)}, f32[21,8,128]{2,1,0:T(8,128)S(1)}, u32[]{:S(2)}, u32[]{:S(2)}) collective-permute-start(f32[21,8,128]{2,1,0:T(8,128)S(1)} %get-tuple-element.42), channel_id=1, source_target_pairs={{1,0},{3,2},{5,4},{7,6},{9,8},{11,10},{13,12},{15,14},{17,16},{19,... | collective-permute-start | bytes 258056 | tf_op jit(solution)/shard_map/ppermute | solution.py:657
  20.1 14.0 %collective-permute-start.3 = (f32[21,8,128]{2,1,0:T(8,128)S(1)}, f32[21,8,128]{2,1,0:T(8,128)S(1)}, u32[]{:S(2)}, u32[]{:S(2)}) collective-permute-start(f32[21,8,128]{2,1,0:T(8,128)S(1)} %get-tuple-element.43), channel_id=1, source_target_pairs={{1,2},{2,1},{3,4},{4,3},{5,6},{6,5},{9,10},{10,9},{11,12},{12,11},... | collective-permute-start | bytes 258056 | tf_op jit(solution)/shard_map/ppermute | solution.py:658
  21.4 12.7 %collective-permute-start.1 = (f32[21,8,128]{2,1,0:T(8,128)S(1)}, f32[21,8,128]{2,1,0:T(8,128)S(1)}, u32[]{:S(2)}, u32[]{:S(2)}) collective-permute-start(f32[21,8,128]{2,1,0:T(8,128)S(1)} %get-tuple-element.42), channel_id=1, source_target_pairs={{0,1},{2,3},{4,5},{6,7},{8,9},{10,11},{12,13},{14,15},{16,17},{18,... | collective-permute-start | bytes 258056 | tf_op jit(solution)/shard_map/ppermute | solution.py:659
  22.7 11.5 %collective-permute-start.2 = (f32[21,8,128]{2,1,0:T(8,128)S(1)}, f32[21,8,128]{2,1,0:T(8,128)S(1)}, u32[]{:S(2)}, u32[]{:S(2)}) collective-permute-start(f32[21,8,128]{2,1,0:T(8,128)S(1)} %get-tuple-element.43), channel_id=1, source_target_pairs={{7,511},{15,503},{23,495},{31,487},{39,479},{47,471},{55,463},{63,... | collective-permute-start | bytes 258056 | tf_op jit(solution)/shard_map/ppermute | solution.py:660

commit v8 on v7

--- a/solution.py
+++ b/solution.py
@@ -252,7 +252,7 @@
 
 
 def edge_kernel(
-    t_ref, s_ref, u_ref, v_ref, d_ref, own_ref, ev_ref, od_ref, swept_ref, e_ref, o_ref
+    t_ref, s_ref, u_ref, v_ref, d_ref, own_ref, ev_ref, od_ref, swept_ref, e_ref, o_ref, a_ref, f_ref
 ):
     lane = lanes()
     lane8, sub8 = lane[:8], lax.broadcasted_iota(jnp.int32, (8, W), 0)
@@ -329,6 +329,26 @@
             elif n == 20:
                 x = jnp.where((lane8 < 4) | (lane8 > W - 5), -x, x)
             o_ref[n] = x
+
+    late = (lat == lax.axis_size("lat") - 1) & seam_first()
+
+    @pl.when(late)
+    def _():
+        a_ref[...] = o_ref[...]
+        f_ref[...] = e_ref[...]
+
+    @pl.when(jnp.logical_not(late))
+    def _():
+        a_ref[...] = e_ref[...]
+        f_ref[...] = o_ref[...]
+
+
+def low_longitude():
+    return lax.axis_index("lon") < lax.axis_size("lon") // 2
+
+
+def seam_first():
+    return jnp.logical_not(low_longitude()) & (lax.axis_index("lon") < lax.axis_size("lon") - 1)
 
 
 def merid_cell(step, fall_before, j):
@@ -563,43 +583,59 @@
     return copies
 
 
+def at_once(copies):
+    for copy in copies:
+        copy.wait()
+
+
 def first_kernel(u_ref, v_ref, d_ref, aux_ref, even_ref, o_ref, *refs):
     fixed = (u_ref, v_ref, d_ref, aux_ref, refs[-5:-1], refs[-9:-5], refs[-1])
     lat = lax.axis_index("lat")
+    top = lax.axis_size("lat") - 1
     even = (lat & 1) == 0
-    top = lat == lax.axis_size("lat") - 1
-
-    @pl.when(even)
-    def _():
-        copies = finish_side(0, even_ref, *fixed) + finish_side(1, o_ref, *fixed)
-        for copy in copies:
-            copy.wait()
-
-    @pl.when(jnp.logical_not(even | top))
-    def _():
-        for copy in finish_side(0, o_ref, *fixed):
-            copy.wait()
-
-
-def last_kernel(u_ref, v_ref, d_ref, aux_ref, odd_ref, f_ref, o_ref, *refs):
+    late = (lat == top - 1) & seam_first()
+
+    @pl.when(even & jnp.logical_not(late))
+    def _():
+        at_once(finish_side(0, even_ref, *fixed) + finish_side(1, o_ref, *fixed))
+
+    @pl.when(late)
+    def _():
+        at_once(finish_side(1, o_ref, *fixed))
+
+    @pl.when(jnp.logical_not(even | (lat == top)))
+    def _():
+        at_once(finish_side(0, o_ref, *fixed))
+
+
+def last_kernel(u_ref, v_ref, d_ref, aux_ref, odd_ref, f_ref, even_ref, o_ref, *refs):
     fixed = (u_ref, v_ref, d_ref, aux_ref, refs[-5:-1], refs[-9:-5], refs[-1])
     lat = lax.axis_index("lat")
-    odd = (lat & 1) == 1
-    top = lat == lax.axis_size("lat") - 1
-
-    @pl.when(odd & jnp.logical_not(top))
-    def _():
-        for copy in finish_side(1, odd_ref, *fixed):
-            copy.wait()
-
-    low_lon = lax.axis_index("lon") < lax.axis_size("lon") // 2
-    for mine, seam_ref in ((low_lon, o_ref), (jnp.logical_not(low_lon), f_ref)):
-
-        @pl.when(top & mine)
-        def _(seam_ref=seam_ref):
-            copies = finish_side(1, odd_ref, *fixed) + finish_side(0, seam_ref, *fixed)
-            for copy in copies:
-                copy.wait()
+    top = lax.axis_size("lat") - 1
+    low = low_longitude()
+    high = jnp.logical_not(low)
+
+    @pl.when(((lat & 1) == 1) & (lat != top))
+    def _():
+        at_once(finish_side(1, odd_ref, *fixed))
+
+    first = lax.axis_index("lon") == 0
+
+    @pl.when((lat == top) & low & jnp.logical_not(first))
+    def _():
+        at_once(finish_side(1, odd_ref, *fixed) + finish_side(0, even_ref, *fixed))
+
+    @pl.when((lat == top) & first)
+    def _():
+        at_once(finish_side(1, odd_ref, *fixed) + finish_side(0, o_ref, *fixed))
+
+    @pl.when((lat == top) & high)
+    def _():
+        at_once(finish_side(1, odd_ref, *fixed) + finish_side(0, f_ref, *fixed))
+
+    @pl.when((lat == top - 1) & seam_first())
+    def _():
+        at_once(finish_side(0, f_ref, *fixed))
 
 
 VMEM = pl.BlockSpec(memory_space=pltpu.VMEM)
@@ -637,27 +673,33 @@
     ev = lax.all_gather(
         ev, "lon", axis_index_groups=[[i, i + 1] for i in range(0, n_lon, 2)], tiled=True
     )
-    swept, edge_e, edge_o = call(
+    swept, edge_e, edge_o, edge_a, edge_f = call(
         edge_kernel,
         [VMEM] * 8,
-        [VMEM] * 3,
-        [(12, K, W), (SEND_ROWS, 8, W), (SEND_ROWS, 8, W)],
+        [VMEM] * 5,
+        [(12, K, W)] + [(SEND_ROWS, 8, W)] * 4,
         1 << 20,
         (t, s, u, v, depth, own, ev, od),
     )
-    to_even, to_odd, pairs_o, pairs_f = [], [], [], []
+    to_even, to_odd, pairs_o, last = [], [], [], []
     top = n_lat - 1
     for p in range(n_lon):
+        low = p < n_lon // 2
+        ahead = not low and p < n_lon - 1
         for l in range(n_lat):
-            (to_even if l & 1 else to_odd).append((p * n_lat + l, p * n_lat + (l ^ 1)))
+            pair = (p * n_lat + l, p * n_lat + (l ^ 1))
+            if l & 1:
+                (last if ahead and l == top else to_even).append(pair)
+            else:
+                to_odd.append(pair)
             if 0 < l < top:
                 pairs_o.append((p * n_lat + l, p * n_lat + ((l + 1) ^ 1) - 1))
         across = (p * n_lat + top, (n_lon - 1 - p) * n_lat + top)
-        (pairs_f if p < n_lon // 2 else pairs_o).append(across)
-    got_even = lax.ppermute(edge_e, ("lon", "lat"), to_even)
+        (last if low else to_even if ahead else pairs_o).append(across)
+    got_even = lax.ppermute(edge_a, ("lon", "lat"), to_even)
     got_o = lax.ppermute(edge_o, ("lon", "lat"), pairs_o)
     got_odd = lax.ppermute(edge_e, ("lon", "lat"), to_odd)
-    got_f = lax.ppermute(edge_o, ("lon", "lat"), pairs_f)
+    got_f = lax.ppermute(edge_f, ("lon", "lat"), last)
     *parts, aux = call(
         inner_kernel,
         [VMEM] * 5 + [HBM] + [VMEM] * 4,
@@ -685,13 +727,13 @@
     )
     outs = call(
         last_kernel,
-        [VMEM] * 7 + [HBM] * 4 + [VMEM] * 4,
+        [VMEM] * 8 + [HBM] * 4 + [VMEM] * 4,
         [HBM] * 4 + [VMEM] * 4,
         [FLAT] * 8,
         1 << 21,
-        (*flow, got_odd, got_f, got_o, *outs),
+        (*flow, got_odd, got_f, got_even, got_o, *outs),
         [pltpu.SemaphoreType.DMA((8,))],
-        {7 + n: n for n in range(8)},
+        {8 + n: n for n in range(8)},
     )
     return tuple(x.reshape(K, J, W) for x in outs[:4])
 

time: 35.5 us -> 34.7 us (0.977)
  the two profiles are of different devices: /device:TPU:39 before, /device:TPU:1 now
where the time goes in v8:
time: 34.7 us; the launch traced here: 34.5 us
  starting transfers between devices  16.7 us (48%)
  blocking collectives  11.8 us (34%)
  Pallas kernels  5.21 us (15%)
  between operations  0.74 us (2%)
    all_gather x1, blocking collectives, body(): lax.all_gather(ev, 'lon', axis_index_groups=[[i, i + 1] for i in range(0,...  11.8 us
    ppermute x1, starting transfers between devices, body(): got_odd = lax.ppermute(edge_e, ('lon', 'lat'), to_odd)  9.45 us
    pallas_call x5, Pallas kernels, call(): pl.pallas_call(kernel, out_shape=[jax.ShapeDtypeStruct(s, F32) for s in o...  5.21 us
    ppermute x1, starting transfers between devices, body(): lax.ppermute(od, 'lon', [(i, ((i + 1 ^ 1) - 1) % n_lon) for i in range(n_...  4.59 us
    ppermute x1, starting transfers between devices, body(): got_even = lax.ppermute(edge_a, ('lon', 'lat'), to_even)  1.29 us
  transfers between devices with their start and end apart: 5, of which 0 were waited for; matrix products, arithmetic and copies ran while one was open for 0% of the time, Pallas kernels for 9%

profile of v8, /device:TPU:1, one launch (start us, length us, event | category | flops | bytes accessed | tf_op | source)
XLA Modules:
  0.0 34.5 jit_solution(17644259022659851624)
XLA Ops:
  0.6 1.4 %shard_map.102 = (f32[256,128]{1,0:T(8,128)S(1)}, f32[256,128]{1,0:T(8,128)S(1)}, f32[256,128]{1,0:T(8,128)S(1)}, f32[256,128]{1,0:T(8,128)S(1)}, f32[16,128]{1,...) custom-call(f32[256,128]{1,0:T(8,128)} %bitcast.12, f32[256,128]{1,0:T(8,128)} %bitcast.13, ...), custom_call_target="tpu_custom_call" | custom-call | flops 1048576 | bytes 1048576 | tf_op jit(solution)/shard_map/pallas_call | solution.py:648
  2.1 4.6 %collective-permute-start = (f32[16,384]{1,0:T(8,128)S(1)}, f32[16,384]{1,0:T(8,128)S(1)}, u32[]{:S(2)}, u32[]{:S(2)}) collective-permute-start(f32[16,384]{1,0:T(8,128)S(1)} %get-tuple-element.41), channel_id=1, source_target_pairs={{0,504},{8,16},{16,8},{24,32},{32,24},{40,48},{48,40},{56,64},{64,... | collective-permute-start | bytes 73736 | tf_op jit(solution)/shard_map/ppermute | solution.py:672
  6.7 11.8 %all_gather.3.ev_ref = f32[32,384]{1,0:T(8,128)S(1)} all-gather(f32[16,384]{1,0:T(8,128)S(1)} %get-tuple-element.40), channel_id=1, replica_groups={{0,8},{16,24},{32,40},{48,56},{64,72},{80,88},{96,104},{112,120},{128,1..., dimensions={0}, use_global_device_ids=true | all-gather | bytes 73728 | tf_op jit(solution)/shard_map/all_gather | solution.py:673
  18.5 0.0 collective-permute-done.od_ref
  18.5 0.7 %shard_map.103 = (f32[12,16,128]{2,1,0:T(8,128)S(1)}, f32[21,8,128]{2,1,0:T(8,128)S(1)}, f32[21,8,128]{2,1,0:T(8,128)S(1)}, f32[21,8,128]{2,1,0:T(8,128)S(1)}, f32[21,8,128]{2,1,0:T(8,128)S(1)}) custom-call(f32[256,128]{1,0:T(8,128)S(1)} %get-tuple-element.37.t_ref, f32[256,128]{1,0:T(8,128)S(1)} %get-tuple-element.38.s_ref, ...), custom_call_target="tpu_custom_call" | custom-call | flops 1048576 | bytes 1048576 | tf_op jit(solution)/shard_map/pallas_call | solution.py:648
  19.2 1.3 %collective-permute-start.3 = (f32[21,8,128]{2,1,0:T(8,128)S(1)}, f32[21,8,128]{2,1,0:T(8,128)S(1)}, u32[]{:S(2)}, u32[]{:S(2)}) collective-permute-start(f32[21,8,128]{2,1,0:T(8,128)S(1)} %get-tuple-element.46), channel_id=1, source_target_pairs={{1,0},{3,2},{5,4},{7,6},{9,8},{11,10},{13,12},{15,14},{17,16},{19,... | collective-permute-start | bytes 258056 | tf_op jit(solution)/shard_map/ppermute | solution.py:699
  20.5 0.7 %collective-permute-start.4 = (f32[21,8,128]{2,1,0:T(8,128)S(1)}, f32[21,8,128]{2,1,0:T(8,128)S(1)}, u32[]{:S(2)}, u32[]{:S(2)}) collective-permute-start(f32[21,8,128]{2,1,0:T(8,128)S(1)} %get-tuple-element.47), channel_id=1, source_target_pairs={{1,2},{2,1},{3,4},{4,3},{5,6},{6,5},{9,10},{10,9},{11,12},{12,11},... | collective-permute-start | bytes 258056 | tf_op jit(solution)/shard_map/ppermute | solution.py:700
  21.2 9.5 %collective-permute-start.1 = (f32[21,8,128]{2,1,0:T(8,128)S(1)}, f32[21,8,128]{2,1,0:T(8,128)S(1)}, u32[]{:S(2)}, u32[]{:S(2)}) collective-permute-start(f32[21,8,128]{2,1,0:T(8,128)S(1)} %get-tuple-element.44), channel_id=1, source_target_pairs={{0,1},{2,3},{4,5},{6,7},{8,9},{10,11},{12,13},{14,15},{16,17},{18,... | collective-permute-start | bytes 258056 | tf_op jit(solution)/shard_map/ppermute | solution.py:701
  30.6 0.7 %collective-permute-start.2 = (f32[21,8,128]{2,1,0:T(8,128)S(1)}, f32[21,8,128]{2,1,0:T(8,128)S(1)}, u32[]{:S(2)}, u32[]{:S(2)}) collective-permute-start(f32[21,8,128]{2,1,0:T(8,128)S(1)} %get-tuple-element.45), channel_id=1, source_target_pairs={{7,511},{15,503},{23,495},{31,487},{39,479},{47,471},{55,463},{63,... | collective-permute-start | bytes 258056 | tf_op jit(solution)/shard_map/ppermute | solution.py:702
  31.3 2.0 %shard_map.104 = (f32[256,128]{1,0:T(8,128)S(1)}, f32[256,128]{1,0:T(8,128)S(1)}, f32[256,128]{1,0:T(8,128)S(1)}, f32[256,128]{1,0:T(8,128)S(1)}, f32[47,16,128]{2,1,0:T(8,128)S(1)}) custom-call(f32[256,128]{1,0:T(8,128)S(1)} %get-tuple-element.37.t_ref, f32[256,128]{1,0:T(8,128)S(1)} %get-tuple-element.38.s_ref, f32[256,128]{1,0:T(8,128)S(1)} %get-tuple-element.34.u_ref, ...), custom_call_target="tpu_custom_call" | custom-call | flops 16777216 | bytes 1048576 | tf_op jit(solution)/shard_map/pallas_call | solution.py:648
  33.3 0.0 collective-permute-done.3.even_ref
  33.3 0.0 collective-permute-done.4.o_ref
  33.3 1.0 %shard_map.105 = (f32[256,128]{1,0:T(8,128)}, f32[256,128]{1,0:T(8,128)}, f32[256,128]{1,0:T(8,128)}, f32[256,128]{1,0:T(8,128)}, f32[256,128]{1,0:T(8,128)S(1)}...) custom-call(f32[256,128]{1,0:T(8,128)S(1)} %get-tuple-element.34.u_r, ...), custom_call_target="tpu_custom_call", output_to_operand_aliasing={{4}: (6, {}), {5}: (7, {}), {6}: (8, {}), {7}: (9, {})} | custom-call | flops 2097152 | bytes 1048576 | tf_op jit(solution)/shard_map/pallas_call | solution.py:648
  34.3 0.0 collective-permute-done.1.odd_ref
  34.3 0.0 collective-permute-done.2.f_ref
  34.3 0.1 shard_map.106
Async XLA Ops:
  2.1 16.4 %collective-permute-start = (f32[16,384]{1,0:T(8,128)S(1)}, f32[16,384]{1,0:T(8,128)S(1)}, u32[]{:S(2)}, u32[]{:S(2)}) collective-permute-start(f32[16,384]{1,0:T(8,128)S(1)} %get-tuple-element.41), channel_id=1, source_target_pairs={{0,504},{8,16},{16,8},{24,32},{32,24},{40,48},{48,40},{56,64},{64,... | collective-permute-start | bytes 73736 | tf_op jit(solution)/shard_map/ppermute | solution.py:672
  19.2 14.1 %collective-permute-start.3 = (f32[21,8,128]{2,1,0:T(8,128)S(1)}, f32[21,8,128]{2,1,0:T(8,128)S(1)}, u32[]{:S(2)}, u32[]{:S(2)}) collective-permute-start(f32[21,8,128]{2,1,0:T(8,128)S(1)} %get-tuple-element.46), channel_id=1, source_target_pairs={{1,0},{3,2},{5,4},{7,6},{9,8},{11,10},{13,12},{15,14},{17,16},{19,... | collective-permute-start | bytes 258056 | tf_op jit(solution)/shard_map/ppermute | solution.py:699
  20.5 12.8 %collective-permute-start.4 = (f32[21,8,128]{2,1,0:T(8,128)S(1)}, f32[21,8,128]{2,1,0:T(8,128)S(1)}, u32[]{:S(2)}, u32[]{:S(2)}) collective-permute-start(f32[21,8,128]{2,1,0:T(8,128)S(1)} %get-tuple-element.47), channel_id=1, source_target_pairs={{1,2},{2,1},{3,4},{4,3},{5,6},{6,5},{9,10},{10,9},{11,12},{12,11},... | collective-permute-start | bytes 258056 | tf_op jit(solution)/shard_map/ppermute | solution.py:700
  21.2 13.2 %collective-permute-start.1 = (f32[21,8,128]{2,1,0:T(8,128)S(1)}, f32[21,8,128]{2,1,0:T(8,128)S(1)}, u32[]{:S(2)}, u32[]{:S(2)}) collective-permute-start(f32[21,8,128]{2,1,0:T(8,128)S(1)} %get-tuple-element.44), channel_id=1, source_target_pairs={{0,1},{2,3},{4,5},{6,7},{8,9},{10,11},{12,13},{14,15},{16,17},{18,... | collective-permute-start | bytes 258056 | tf_op jit(solution)/shard_map/ppermute | solution.py:701
  30.6 3.7 %collective-permute-start.2 = (f32[21,8,128]{2,1,0:T(8,128)S(1)}, f32[21,8,128]{2,1,0:T(8,128)S(1)}, u32[]{:S(2)}, u32[]{:S(2)}) collective-permute-start(f32[21,8,128]{2,1,0:T(8,128)S(1)} %get-tuple-element.45), channel_id=1, source_target_pairs={{7,511},{15,503},{23,495},{31,487},{39,479},{47,471},{55,463},{63,... | collective-permute-start | bytes 258056 | tf_op jit(solution)/shard_map/ppermute | solution.py:702

commit v9 on v8

--- a/solution.py
+++ b/solution.py
@@ -603,10 +603,6 @@
     def _():
         at_once(finish_side(1, o_ref, *fixed))
 
-    @pl.when(jnp.logical_not(even | (lat == top)))
-    def _():
-        at_once(finish_side(0, o_ref, *fixed))
-
 
 def last_kernel(u_ref, v_ref, d_ref, aux_ref, odd_ref, f_ref, even_ref, o_ref, *refs):
     fixed = (u_ref, v_ref, d_ref, aux_ref, refs[-5:-1], refs[-9:-5], refs[-1])
@@ -615,9 +611,13 @@
     low = low_longitude()
     high = jnp.logical_not(low)
 
-    @pl.when(((lat & 1) == 1) & (lat != top))
-    def _():
-        at_once(finish_side(1, odd_ref, *fixed))
+    @pl.when(lat == 1)
+    def _():
+        at_once(finish_side(0, o_ref, *fixed) + finish_side(1, even_ref, *fixed))
+
+    @pl.when(((lat & 1) == 1) & (lat != 1) & (lat != top))
+    def _():
+        at_once(finish_side(0, o_ref, *fixed) + finish_side(1, odd_ref, *fixed))
 
     first = lax.axis_index("lon") == 0
 
@@ -691,7 +691,7 @@
             if l & 1:
                 (last if ahead and l == top else to_even).append(pair)
             else:
-                to_odd.append(pair)
+                (to_odd if l else to_even).append(pair)
             if 0 < l < top:
                 pairs_o.append((p * n_lat + l, p * n_lat + ((l + 1) ^ 1) - 1))
         across = (p * n_lat + top, (n_lon - 1 - p) * n_lat + top)

time: 34.7 us -> 34.6 us (level)
  the two profiles are of different devices: /device:TPU:1 before, /device:TPU:262 now
where the time goes in v9:
time: 34.6 us; the launch traced here: 34.3 us
  starting transfers between devices  16.6 us (48%)
  waiting for transfers between devices  9.25 us (27%)
  Pallas kernels  5.85 us (17%)
  blocking collectives  1.84 us (5%)
  between operations  0.73 us (2%)
    ppermute x1, starting transfers between devices, body(): got_o = lax.ppermute(edge_o, ('lon', 'lat'), pairs_o)  9.35 us
    ppermute x1, waiting for transfers between devices, body(): got_f = lax.ppermute(edge_f, ('lon', 'lat'), last)  6.08 us
    pallas_call x5, Pallas kernels, call(): pl.pallas_call(kernel, out_shape=[jax.ShapeDtypeStruct(s, F32) for s in o...  5.85 us
    ppermute x1, starting transfers between devices, body(): lax.ppermute(od, 'lon', [(i, ((i + 1 ^ 1) - 1) % n_lon) for i in range(n_...  4.04 us
    ppermute x1, waiting for transfers between devices, body(): lax.ppermute(od, 'lon', [(i, ((i + 1 ^ 1) - 1) % n_lon) for i in range(n_...  3.17 us
    all_gather x1, blocking collectives, body(): lax.all_gather(ev, 'lon', axis_index_groups=[[i, i + 1] for i in range(0,...  1.84 us
    ppermute x1, starting transfers between devices, body(): got_odd = lax.ppermute(edge_e, ('lon', 'lat'), to_odd)  1.29 us
    ppermute x1, starting transfers between devices, body(): got_f = lax.ppermute(edge_f, ('lon', 'lat'), last)  1.29 us
  transfers between devices with their start and end apart: 5, of which 2 were waited for; matrix products, arithmetic and copies ran while one was open for 0% of the time, Pallas kernels for 8%

profile of v9, /device:TPU:262, one launch (start us, length us, event | category | flops | bytes accessed | tf_op | source)
XLA Modules:
  0.0 34.3 jit_solution(11668732245767959846)
XLA Ops:
  0.6 1.4 %shard_map.102 = (f32[256,128]{1,0:T(8,128)S(1)}, f32[256,128]{1,0:T(8,128)S(1)}, f32[256,128]{1,0:T(8,128)S(1)}, f32[256,128]{1,0:T(8,128)S(1)}, f32[16,128]{1,...) custom-call(f32[256,128]{1,0:T(8,128)} %bitcast.12, f32[256,128]{1,0:T(8,128)} %bitcast.13, ...), custom_call_target="tpu_custom_call" | custom-call | flops 1048576 | bytes 1048576 | tf_op jit(solution)/shard_map/pallas_call | solution.py:648
  2.1 4.0 %collective-permute-start = (f32[16,384]{1,0:T(8,128)S(1)}, f32[16,384]{1,0:T(8,128)S(1)}, u32[]{:S(2)}, u32[]{:S(2)}) collective-permute-start(f32[16,384]{1,0:T(8,128)S(1)} %get-tuple-element.41), channel_id=1, source_target_pairs={{0,504},{8,16},{16,8},{24,32},{32,24},{40,48},{48,40},{56,64},{64,... | collective-permute-start | bytes 73736 | tf_op jit(solution)/shard_map/ppermute | solution.py:672
  6.1 1.8 %all_gather.3.ev_ref = f32[32,384]{1,0:T(8,128)S(1)} all-gather(f32[16,384]{1,0:T(8,128)S(1)} %get-tuple-element.40), channel_id=1, replica_groups={{0,8},{16,24},{32,40},{48,56},{64,72},{80,88},{96,104},{112,120},{128,1..., dimensions={0}, use_global_device_ids=true | all-gather | bytes 73728 | tf_op jit(solution)/shard_map/all_gather | solution.py:673
  8.0 3.2 %collective-permute-done.od_ref = f32[16,384]{1,0:T(8,128)S(1)} collective-permute-done((f32[16,384]{1,0:T(8,128)S(1)}, f32[16,384]{1,0:T(8,128)S(1)}, u32[]{:S(2)}, u32[]{:S(2)}) %collective-permute-start) | collective-permute-done | bytes 24608 | tf_op jit(solution)/shard_map/ppermute | solution.py:672
  11.1 0.7 %shard_map.103 = (f32[12,16,128]{2,1,0:T(8,128)S(1)}, f32[21,8,128]{2,1,0:T(8,128)S(1)}, f32[21,8,128]{2,1,0:T(8,128)S(1)}, f32[21,8,128]{2,1,0:T(8,128)S(1)}, f32[21,8,128]{2,1,0:T(8,128)S(1)}) custom-call(f32[256,128]{1,0:T(8,128)S(1)} %get-tuple-element.37.t_ref, f32[256,128]{1,0:T(8,128)S(1)} %get-tuple-element.38.s_ref, ...), custom_call_target="tpu_custom_call" | custom-call | flops 1048576 | bytes 1048576 | tf_op jit(solution)/shard_map/pallas_call | solution.py:648
  11.8 0.7 %collective-permute-start.3 = (f32[21,8,128]{2,1,0:T(8,128)S(1)}, f32[21,8,128]{2,1,0:T(8,128)S(1)}, u32[]{:S(2)}, u32[]{:S(2)}) collective-permute-start(f32[21,8,128]{2,1,0:T(8,128)S(1)} %get-tuple-element.46), channel_id=1, source_target_pairs={{0,1},{1,0},{3,2},{5,4},{7,6},{8,9},{9,8},{11,10},{13,12},{15,14},... | collective-permute-start | bytes 258056 | tf_op jit(solution)/shard_map/ppermute | solution.py:699
  12.5 9.3 %collective-permute-start.4 = (f32[21,8,128]{2,1,0:T(8,128)S(1)}, f32[21,8,128]{2,1,0:T(8,128)S(1)}, u32[]{:S(2)}, u32[]{:S(2)}) collective-permute-start(f32[21,8,128]{2,1,0:T(8,128)S(1)} %get-tuple-element.47), channel_id=1, source_target_pairs={{1,2},{2,1},{3,4},{4,3},{5,6},{6,5},{9,10},{10,9},{11,12},{12,11},... | collective-permute-start | bytes 258056 | tf_op jit(solution)/shard_map/ppermute | solution.py:700
  21.8 1.3 %collective-permute-start.1 = (f32[21,8,128]{2,1,0:T(8,128)S(1)}, f32[21,8,128]{2,1,0:T(8,128)S(1)}, u32[]{:S(2)}, u32[]{:S(2)}) collective-permute-start(f32[21,8,128]{2,1,0:T(8,128)S(1)} %get-tuple-element.44), channel_id=1, source_target_pairs={{2,3},{4,5},{6,7},{10,11},{12,13},{14,15},{18,19},{20,21},{22,23},... | collective-permute-start | bytes 258056 | tf_op jit(solution)/shard_map/ppermute | solution.py:701
  23.1 1.3 %collective-permute-start.2 = (f32[21,8,128]{2,1,0:T(8,128)S(1)}, f32[21,8,128]{2,1,0:T(8,128)S(1)}, u32[]{:S(2)}, u32[]{:S(2)}) collective-permute-start(f32[21,8,128]{2,1,0:T(8,128)S(1)} %get-tuple-element.45), channel_id=1, source_target_pairs={{7,511},{15,503},{23,495},{31,487},{39,479},{47,471},{55,463},{63,... | collective-permute-start | bytes 258056 | tf_op jit(solution)/shard_map/ppermute | solution.py:702
  24.4 2.0 %shard_map.104 = (f32[256,128]{1,0:T(8,128)S(1)}, f32[256,128]{1,0:T(8,128)S(1)}, f32[256,128]{1,0:T(8,128)S(1)}, f32[256,128]{1,0:T(8,128)S(1)}, f32[47,16,128]{2,1,0:T(8,128)S(1)}) custom-call(f32[256,128]{1,0:T(8,128)S(1)} %get-tuple-element.37.t_ref, f32[256,128]{1,0:T(8,128)S(1)} %get-tuple-element.38.s_ref, f32[256,128]{1,0:T(8,128)S(1)} %get-tuple-element.34.u_ref, ...), custom_call_target="tpu_custom_call" | custom-call | flops 16777216 | bytes 1048576 | tf_op jit(solution)/shard_map/pallas_call | solution.py:648
  26.4 0.0 collective-permute-done.3.even_ref
  26.4 0.0 collective-permute-done.4.o_ref
  26.4 0.9 %shard_map.105 = (f32[256,128]{1,0:T(8,128)}, f32[256,128]{1,0:T(8,128)}, f32[256,128]{1,0:T(8,128)}, f32[256,128]{1,0:T(8,128)}, f32[256,128]{1,0:T(8,128)S(1)}...) custom-call(f32[256,128]{1,0:T(8,128)S(1)} %get-tuple-element.34.u_r, ...), custom_call_target="tpu_custom_call", output_to_operand_aliasing={{4}: (6, {}), {5}: (7, {}), {6}: (8, {}), {7}: (9, {})} | custom-call | flops 2097152 | bytes 1048576 | tf_op jit(solution)/shard_map/pallas_call | solution.py:648
  27.3 0.0 collective-permute-done.1.odd_ref
  27.3 6.1 %collective-permute-done.2.f_ref = f32[21,8,128]{2,1,0:T(8,128)S(1)} collective-permute-done((f32[21,8,128]{2,1,0:T(8,128)S(1)}, f32[21,8,128]{2,1,0:T(8,128)S(1)}, u32[]{:S(2)}, u32[]{:S(2)}) %collective-permute-start.2) | collective-permute-done | bytes 86048 | tf_op jit(solution)/shard_map/ppermute | solution.py:702
  33.4 0.9 %shard_map.106 = (f32[256,128]{1,0:T(8,128)}, f32[256,128]{1,0:T(8,128)}, f32[256,128]{1,0:T(8,128)}, f32[256,128]{1,0:T(8,128)}, f32[256,128]{1,0:T(8,128)S(1)}...) custom-call(f32[256,128]{1,0:T(8,128)S(1)} %get-tuple-element.34.u_r, ...), custom_call_target="tpu_custom_call", output_to_operand_aliasing={{0}: (8, {}), {1}: (9, {}), {2}: (10, {}), {3}: (11, {}), {... | custom-call | flops 2097152 | bytes 1048576 | tf_op jit(solution)/shard_map/pallas_call | solution.py:648
Async XLA Ops:
  2.1 9.1 %collective-permute-start = (f32[16,384]{1,0:T(8,128)S(1)}, f32[16,384]{1,0:T(8,128)S(1)}, u32[]{:S(2)}, u32[]{:S(2)}) collective-permute-start(f32[16,384]{1,0:T(8,128)S(1)} %get-tuple-element.41), channel_id=1, source_target_pairs={{0,504},{8,16},{16,8},{24,32},{32,24},{40,48},{48,40},{56,64},{64,... | collective-permute-start | bytes 73736 | tf_op jit(solution)/shard_map/ppermute | solution.py:672
  11.8 14.6 %collective-permute-start.3 = (f32[21,8,128]{2,1,0:T(8,128)S(1)}, f32[21,8,128]{2,1,0:T(8,128)S(1)}, u32[]{:S(2)}, u32[]{:S(2)}) collective-permute-start(f32[21,8,128]{2,1,0:T(8,128)S(1)} %get-tuple-element.46), channel_id=1, source_target_pairs={{0,1},{1,0},{3,2},{5,4},{7,6},{8,9},{9,8},{11,10},{13,12},{15,14},... | collective-permute-start | bytes 258056 | tf_op jit(solution)/shard_map/ppermute | solution.py:699
  12.5 13.9 %collective-permute-start.4 = (f32[21,8,128]{2,1,0:T(8,128)S(1)}, f32[21,8,128]{2,1,0:T(8,128)S(1)}, u32[]{:S(2)}, u32[]{:S(2)}) collective-permute-start(f32[21,8,128]{2,1,0:T(8,128)S(1)} %get-tuple-element.47), channel_id=1, source_target_pairs={{1,2},{2,1},{3,4},{4,3},{5,6},{6,5},{9,10},{10,9},{11,12},{12,11},... | collective-permute-start | bytes 258056 | tf_op jit(solution)/shard_map/ppermute | solution.py:700
  21.8 5.5 %collective-permute-start.1 = (f32[21,8,128]{2,1,0:T(8,128)S(1)}, f32[21,8,128]{2,1,0:T(8,128)S(1)}, u32[]{:S(2)}, u32[]{:S(2)}) collective-permute-start(f32[21,8,128]{2,1,0:T(8,128)S(1)} %get-tuple-element.44), channel_id=1, source_target_pairs={{2,3},{4,5},{6,7},{10,11},{12,13},{14,15},{18,19},{20,21},{22,23},... | collective-permute-start | bytes 258056 | tf_op jit(solution)/shard_map/ppermute | solution.py:701
  23.1 10.3 %collective-permute-start.2 = (f32[21,8,128]{2,1,0:T(8,128)S(1)}, f32[21,8,128]{2,1,0:T(8,128)S(1)}, u32[]{:S(2)}, u32[]{:S(2)}) collective-permute-start(f32[21,8,128]{2,1,0:T(8,128)S(1)} %get-tuple-element.45), channel_id=1, source_target_pairs={{7,511},{15,503},{23,495},{31,487},{39,479},{47,471},{55,463},{63,... | collective-permute-start | bytes 258056 | tf_op jit(solution)/shard_map/ppermute | solution.py:702

commit v10 on v9

--- a/solution.py
+++ b/solution.py
@@ -407,7 +407,8 @@
         for j, (t, s) in zip(group, in_step([zonal.row((t_ref, s_ref), j) for j in group])):
             rows[0][j], rows[1][j] = t, s
     wet = [wet_of(depth_row(d_ref, j)) for j in range(J)]
-    for n, out in enumerate((t_out, s_out)):
+
+    def meridional(n, out):
         q = rows[n]
         for at, j in enumerate((0, 1, 2, 3, 4, 11, 12, 13, 14, 15)):
             aux_ref[AUX_TRACER * n + at] = q[j]
@@ -416,6 +417,7 @@
         before = None
         for j in range(2, 13):
             after = merid_cell(step, cell[2], j + 1)
+            yield
             flux = merid_flux(load_row(v_ref, j), wet[j] * wet[j + 1], q[j], q[j + 1], cell, after)
             if j == 2:
                 aux_ref[AUX_TRACER * n + 10] = flux
@@ -424,6 +426,8 @@
             if j == 12:
                 aux_ref[AUX_TRACER * n + 11] = flux
             cell, before = after, flux
+
+    merids = [meridional(0, t_out), meridional(1, s_out)]
     wet_w, wet_e = wet_of(packs[3][1]), wet_of(packs[3][2])
     low = low_half(lane)
     halo_wet = {}
@@ -464,7 +468,7 @@
     def inner(n, j):
         lap_ref[J * n + j] = yield from lap_row(n, flows[n][1][0], lambda n, j: load_row(flows[n][0], j), j, 0, J - 1)
 
-    walk([functools.partial(inner, n, j) for j in range(J) for n in range(2)])
+    in_step(merids + [inner(n, j) for j in range(J) for n in range(2)])
     halo_laps = [
         jnp.where(low, seam_lap(pack[1], wet_w), seam_lap(pack[2], wet_e)) for _, pack, _ in flows
     ]

time: 34.6 us -> 34.9 us (level)
  the two profiles are of different devices: /device:TPU:262 before, /device:TPU:38 now
where the time goes in v10:
time: 34.9 us; the launch traced here: 34.6 us
  starting transfers between devices  26.4 us (76%)
  Pallas kernels  5.58 us (16%)
  blocking collectives  1.84 us (5%)
  between operations  0.74 us (2%)
    ppermute x1, starting transfers between devices, body(): lax.ppermute(od, 'lon', [(i, ((i + 1 ^ 1) - 1) % n_lon) for i in range(n_...  10.7 us
    ppermute x1, starting transfers between devices, body(): got_f = lax.ppermute(edge_f, ('lon', 'lat'), last)  8.18 us
    pallas_call x5, Pallas kernels, call(): pl.pallas_call(kernel, out_shape=[jax.ShapeDtypeStruct(s, F32) for s in o...  5.58 us
    ppermute x1, starting transfers between devices, body(): got_even = lax.ppermute(edge_a, ('lon', 'lat'), to_even)  4.93 us
    all_gather x1, blocking collectives, body(): lax.all_gather(ev, 'lon', axis_index_groups=[[i, i + 1] for i in range(0,...  1.84 us
    ppermute x1, starting transfers between devices, body(): got_o = lax.ppermute(edge_o, ('lon', 'lat'), pairs_o)  1.29 us
    ppermute x1, starting transfers between devices, body(): got_odd = lax.ppermute(edge_e, ('lon', 'lat'), to_odd)  1.29 us
  transfers between devices with their start and end apart: 5, of which 0 were waited for; matrix products, arithmetic and copies ran while one was open for 0% of the time, Pallas kernels for 7%

profile of v10, /device:TPU:38, one launch (start us, length us, event | category | flops | bytes accessed | tf_op | source)
XLA Modules:
  0.0 34.6 jit_solution(11075804196917494207)
XLA Ops:
  0.6 1.4 %shard_map.102 = (f32[256,128]{1,0:T(8,128)S(1)}, f32[256,128]{1,0:T(8,128)S(1)}, f32[256,128]{1,0:T(8,128)S(1)}, f32[256,128]{1,0:T(8,128)S(1)}, f32[16,128]{1,...) custom-call(f32[256,128]{1,0:T(8,128)} %bitcast.12, f32[256,128]{1,0:T(8,128)} %bitcast.13, ...), custom_call_target="tpu_custom_call" | custom-call | flops 1048576 | bytes 1048576 | tf_op jit(solution)/shard_map/pallas_call | solution.py:652
  2.1 10.7 %collective-permute-start = (f32[16,384]{1,0:T(8,128)S(1)}, f32[16,384]{1,0:T(8,128)S(1)}, u32[]{:S(2)}, u32[]{:S(2)}) collective-permute-start(f32[16,384]{1,0:T(8,128)S(1)} %get-tuple-element.41), channel_id=1, source_target_pairs={{0,504},{8,16},{16,8},{24,32},{32,24},{40,48},{48,40},{56,64},{64,... | collective-permute-start | bytes 73736 | tf_op jit(solution)/shard_map/ppermute | solution.py:676
  12.8 1.8 %all_gather.3.ev_ref = f32[32,384]{1,0:T(8,128)S(1)} all-gather(f32[16,384]{1,0:T(8,128)S(1)} %get-tuple-element.40), channel_id=1, replica_groups={{0,8},{16,24},{32,40},{48,56},{64,72},{80,88},{96,104},{112,120},{128,1..., dimensions={0}, use_global_device_ids=true | all-gather | bytes 73728 | tf_op jit(solution)/shard_map/all_gather | solution.py:677
  14.6 0.0 collective-permute-done.od_ref
  14.6 0.8 %shard_map.103 = (f32[12,16,128]{2,1,0:T(8,128)S(1)}, f32[21,8,128]{2,1,0:T(8,128)S(1)}, f32[21,8,128]{2,1,0:T(8,128)S(1)}, f32[21,8,128]{2,1,0:T(8,128)S(1)}, f32[21,8,128]{2,1,0:T(8,128)S(1)}) custom-call(f32[256,128]{1,0:T(8,128)S(1)} %get-tuple-element.37.t_ref, f32[256,128]{1,0:T(8,128)S(1)} %get-tuple-element.38.s_ref, ...), custom_call_target="tpu_custom_call" | custom-call | flops 1048576 | bytes 1048576 | tf_op jit(solution)/shard_map/pallas_call | solution.py:652
  15.4 4.9 %collective-permute-start.3 = (f32[21,8,128]{2,1,0:T(8,128)S(1)}, f32[21,8,128]{2,1,0:T(8,128)S(1)}, u32[]{:S(2)}, u32[]{:S(2)}) collective-permute-start(f32[21,8,128]{2,1,0:T(8,128)S(1)} %get-tuple-element.46), channel_id=1, source_target_pairs={{0,1},{1,0},{3,2},{5,4},{7,6},{8,9},{9,8},{11,10},{13,12},{15,14},... | collective-permute-start | bytes 258056 | tf_op jit(solution)/shard_map/ppermute | solution.py:703
  20.4 1.3 %collective-permute-start.4 = (f32[21,8,128]{2,1,0:T(8,128)S(1)}, f32[21,8,128]{2,1,0:T(8,128)S(1)}, u32[]{:S(2)}, u32[]{:S(2)}) collective-permute-start(f32[21,8,128]{2,1,0:T(8,128)S(1)} %get-tuple-element.47), channel_id=1, source_target_pairs={{1,2},{2,1},{3,4},{4,3},{5,6},{6,5},{9,10},{10,9},{11,12},{12,11},... | collective-permute-start | bytes 258056 | tf_op jit(solution)/shard_map/ppermute | solution.py:704
  21.7 1.3 %collective-permute-start.1 = (f32[21,8,128]{2,1,0:T(8,128)S(1)}, f32[21,8,128]{2,1,0:T(8,128)S(1)}, u32[]{:S(2)}, u32[]{:S(2)}) collective-permute-start(f32[21,8,128]{2,1,0:T(8,128)S(1)} %get-tuple-element.44), channel_id=1, source_target_pairs={{2,3},{4,5},{6,7},{10,11},{12,13},{14,15},{18,19},{20,21},{22,23},... | collective-permute-start | bytes 258056 | tf_op jit(solution)/shard_map/ppermute | solution.py:705
  23.0 8.2 %collective-permute-start.2 = (f32[21,8,128]{2,1,0:T(8,128)S(1)}, f32[21,8,128]{2,1,0:T(8,128)S(1)}, u32[]{:S(2)}, u32[]{:S(2)}) collective-permute-start(f32[21,8,128]{2,1,0:T(8,128)S(1)} %get-tuple-element.45), channel_id=1, source_target_pairs={{7,511},{15,503},{23,495},{31,487},{39,479},{47,471},{55,463},{63,... | collective-permute-start | bytes 258056 | tf_op jit(solution)/shard_map/ppermute | solution.py:706
  31.2 2.2 %shard_map.104 = (f32[256,128]{1,0:T(8,128)S(1)}, f32[256,128]{1,0:T(8,128)S(1)}, f32[256,128]{1,0:T(8,128)S(1)}, f32[256,128]{1,0:T(8,128)S(1)}, f32[47,16,128]{2,1,0:T(8,128)S(1)}) custom-call(f32[256,128]{1,0:T(8,128)S(1)} %get-tuple-element.37.t_ref, f32[256,128]{1,0:T(8,128)S(1)} %get-tuple-element.38.s_ref, f32[256,128]{1,0:T(8,128)S(1)} %get-tuple-element.34.u_ref, ...), custom_call_target="tpu_custom_call" | custom-call | flops 16777216 | bytes 1048576 | tf_op jit(solution)/shard_map/pallas_call | solution.py:652
  33.4 0.0 collective-permute-done.3.even_ref
  33.4 0.0 collective-permute-done.4.o_ref
  33.4 0.1 shard_map.105
  33.5 0.0 collective-permute-done.1.odd_ref
  33.5 0.0 collective-permute-done.2.f_ref
  33.6 1.0 %shard_map.106 = (f32[256,128]{1,0:T(8,128)}, f32[256,128]{1,0:T(8,128)}, f32[256,128]{1,0:T(8,128)}, f32[256,128]{1,0:T(8,128)}, f32[256,128]{1,0:T(8,128)S(1)}...) custom-call(f32[256,128]{1,0:T(8,128)S(1)} %get-tuple-element.34.u_r, ...), custom_call_target="tpu_custom_call", output_to_operand_aliasing={{0}: (8, {}), {1}: (9, {}), {2}: (10, {}), {3}: (11, {}), {... | custom-call | flops 2097152 | bytes 1048576 | tf_op jit(solution)/shard_map/pallas_call | solution.py:652
Async XLA Ops:
  2.1 12.6 %collective-permute-start = (f32[16,384]{1,0:T(8,128)S(1)}, f32[16,384]{1,0:T(8,128)S(1)}, u32[]{:S(2)}, u32[]{:S(2)}) collective-permute-start(f32[16,384]{1,0:T(8,128)S(1)} %get-tuple-element.41), channel_id=1, source_target_pairs={{0,504},{8,16},{16,8},{24,32},{32,24},{40,48},{48,40},{56,64},{64,... | collective-permute-start | bytes 73736 | tf_op jit(solution)/shard_map/ppermute | solution.py:676
  15.4 18.0 %collective-permute-start.3 = (f32[21,8,128]{2,1,0:T(8,128)S(1)}, f32[21,8,128]{2,1,0:T(8,128)S(1)}, u32[]{:S(2)}, u32[]{:S(2)}) collective-permute-start(f32[21,8,128]{2,1,0:T(8,128)S(1)} %get-tuple-element.46), channel_id=1, source_target_pairs={{0,1},{1,0},{3,2},{5,4},{7,6},{8,9},{9,8},{11,10},{13,12},{15,14},... | collective-permute-start | bytes 258056 | tf_op jit(solution)/shard_map/ppermute | solution.py:703
  20.4 13.1 %collective-permute-start.4 = (f32[21,8,128]{2,1,0:T(8,128)S(1)}, f32[21,8,128]{2,1,0:T(8,128)S(1)}, u32[]{:S(2)}, u32[]{:S(2)}) collective-permute-start(f32[21,8,128]{2,1,0:T(8,128)S(1)} %get-tuple-element.47), channel_id=1, source_target_pairs={{1,2},{2,1},{3,4},{4,3},{5,6},{6,5},{9,10},{10,9},{11,12},{12,11},... | collective-permute-start | bytes 258056 | tf_op jit(solution)/shard_map/ppermute | solution.py:704
  21.7 11.9 %collective-permute-start.1 = (f32[21,8,128]{2,1,0:T(8,128)S(1)}, f32[21,8,128]{2,1,0:T(8,128)S(1)}, u32[]{:S(2)}, u32[]{:S(2)}) collective-permute-start(f32[21,8,128]{2,1,0:T(8,128)S(1)} %get-tuple-element.44), channel_id=1, source_target_pairs={{2,3},{4,5},{6,7},{10,11},{12,13},{14,15},{18,19},{20,21},{22,23},... | collective-permute-start | bytes 258056 | tf_op jit(solution)/shard_map/ppermute | solution.py:705
  23.0 10.6 %collective-permute-start.2 = (f32[21,8,128]{2,1,0:T(8,128)S(1)}, f32[21,8,128]{2,1,0:T(8,128)S(1)}, u32[]{:S(2)}, u32[]{:S(2)}) collective-permute-start(f32[21,8,128]{2,1,0:T(8,128)S(1)} %get-tuple-element.45), channel_id=1, source_target_pairs={{7,511},{15,503},{23,495},{31,487},{39,479},{47,471},{55,463},{63,... | collective-permute-start | bytes 258056 | tf_op jit(solution)/shard_map/ppermute | solution.py:706

commit v11 on v10

--- a/solution.py
+++ b/solution.py
@@ -340,6 +340,9 @@
     @pl.when(jnp.logical_not(late))
     def _():
         a_ref[...] = e_ref[...]
+
+    @pl.when((lat == lax.axis_size("lat") - 1) & jnp.logical_not(late))
+    def _():
         f_ref[...] = o_ref[...]
 
 

time: 34.9 us -> 34.9 us (level)
  no operation moved by 1% of the time
where the time goes in v11:
time: 34.9 us; the launch traced here: 34.6 us
  starting transfers between devices  26.4 us (76%)
  Pallas kernels  5.58 us (16%)
  blocking collectives  1.84 us (5%)
  between operations  0.74 us (2%)
    ppermute x1, starting transfers between devices, body(): lax.ppermute(od, 'lon', [(i, ((i + 1 ^ 1) - 1) % n_lon) for i in range(n_...  10.7 us
    ppermute x1, starting transfers between devices, body(): got_f = lax.ppermute(edge_f, ('lon', 'lat'), last)  8.18 us
    pallas_call x5, Pallas kernels, call(): pl.pallas_call(kernel, out_shape=[jax.ShapeDtypeStruct(s, F32) for s in o...  5.58 us
    ppermute x1, starting transfers between devices, body(): got_even = lax.ppermute(edge_a, ('lon', 'lat'), to_even)  4.94 us
    all_gather x1, blocking collectives, body(): lax.all_gather(ev, 'lon', axis_index_groups=[[i, i + 1] for i in range(0,...  1.84 us
    ppermute x1, starting transfers between devices, body(): got_o = lax.ppermute(edge_o, ('lon', 'lat'), pairs_o)  1.29 us
    ppermute x1, starting transfers between devices, body(): got_odd = lax.ppermute(edge_e, ('lon', 'lat'), to_odd)  1.29 us
  transfers between devices with their start and end apart: 5, of which 0 were waited for; matrix products, arithmetic and copies ran while one was open for 0% of the time, Pallas kernels for 7%

profile of v11, /device:TPU:38, one launch (start us, length us, event | category | flops | bytes accessed | tf_op | source)
XLA Modules:
  0.0 34.6 jit_solution(15477793421322958665)
XLA Ops:
  0.6 1.4 %shard_map.102 = (f32[256,128]{1,0:T(8,128)S(1)}, f32[256,128]{1,0:T(8,128)S(1)}, f32[256,128]{1,0:T(8,128)S(1)}, f32[256,128]{1,0:T(8,128)S(1)}, f32[16,128]{1,...) custom-call(f32[256,128]{1,0:T(8,128)} %bitcast.12, f32[256,128]{1,0:T(8,128)} %bitcast.13, ...), custom_call_target="tpu_custom_call" | custom-call | flops 1048576 | bytes 1048576 | tf_op jit(solution)/shard_map/pallas_call | solution.py:655
  2.1 10.7 %collective-permute-start = (f32[16,384]{1,0:T(8,128)S(1)}, f32[16,384]{1,0:T(8,128)S(1)}, u32[]{:S(2)}, u32[]{:S(2)}) collective-permute-start(f32[16,384]{1,0:T(8,128)S(1)} %get-tuple-element.41), channel_id=1, source_target_pairs={{0,504},{8,16},{16,8},{24,32},{32,24},{40,48},{48,40},{56,64},{64,... | collective-permute-start | bytes 73736 | tf_op jit(solution)/shard_map/ppermute | solution.py:679
  12.8 1.8 %all_gather.3.ev_ref = f32[32,384]{1,0:T(8,128)S(1)} all-gather(f32[16,384]{1,0:T(8,128)S(1)} %get-tuple-element.40), channel_id=1, replica_groups={{0,8},{16,24},{32,40},{48,56},{64,72},{80,88},{96,104},{112,120},{128,1..., dimensions={0}, use_global_device_ids=true | all-gather | bytes 73728 | tf_op jit(solution)/shard_map/all_gather | solution.py:680
  14.6 0.0 collective-permute-done.od_ref
  14.6 0.8 %shard_map.103 = (f32[12,16,128]{2,1,0:T(8,128)S(1)}, f32[21,8,128]{2,1,0:T(8,128)S(1)}, f32[21,8,128]{2,1,0:T(8,128)S(1)}, f32[21,8,128]{2,1,0:T(8,128)S(1)}, f32[21,8,128]{2,1,0:T(8,128)S(1)}) custom-call(f32[256,128]{1,0:T(8,128)S(1)} %get-tuple-element.37.t_ref, f32[256,128]{1,0:T(8,128)S(1)} %get-tuple-element.38.s_ref, ...), custom_call_target="tpu_custom_call" | custom-call | flops 1048576 | bytes 1048576 | tf_op jit(solution)/shard_map/pallas_call | solution.py:655
  15.4 4.9 %collective-permute-start.3 = (f32[21,8,128]{2,1,0:T(8,128)S(1)}, f32[21,8,128]{2,1,0:T(8,128)S(1)}, u32[]{:S(2)}, u32[]{:S(2)}) collective-permute-start(f32[21,8,128]{2,1,0:T(8,128)S(1)} %get-tuple-element.46), channel_id=1, source_target_pairs={{0,1},{1,0},{3,2},{5,4},{7,6},{8,9},{9,8},{11,10},{13,12},{15,14},... | collective-permute-start | bytes 258056 | tf_op jit(solution)/shard_map/ppermute | solution.py:706
  20.4 1.3 %collective-permute-start.4 = (f32[21,8,128]{2,1,0:T(8,128)S(1)}, f32[21,8,128]{2,1,0:T(8,128)S(1)}, u32[]{:S(2)}, u32[]{:S(2)}) collective-permute-start(f32[21,8,128]{2,1,0:T(8,128)S(1)} %get-tuple-element.47), channel_id=1, source_target_pairs={{1,2},{2,1},{3,4},{4,3},{5,6},{6,5},{9,10},{10,9},{11,12},{12,11},... | collective-permute-start | bytes 258056 | tf_op jit(solution)/shard_map/ppermute | solution.py:707
  21.7 1.3 %collective-permute-start.1 = (f32[21,8,128]{2,1,0:T(8,128)S(1)}, f32[21,8,128]{2,1,0:T(8,128)S(1)}, u32[]{:S(2)}, u32[]{:S(2)}) collective-permute-start(f32[21,8,128]{2,1,0:T(8,128)S(1)} %get-tuple-element.44), channel_id=1, source_target_pairs={{2,3},{4,5},{6,7},{10,11},{12,13},{14,15},{18,19},{20,21},{22,23},... | collective-permute-start | bytes 258056 | tf_op jit(solution)/shard_map/ppermute | solution.py:708
  23.0 8.2 %collective-permute-start.2 = (f32[21,8,128]{2,1,0:T(8,128)S(1)}, f32[21,8,128]{2,1,0:T(8,128)S(1)}, u32[]{:S(2)}, u32[]{:S(2)}) collective-permute-start(f32[21,8,128]{2,1,0:T(8,128)S(1)} %get-tuple-element.45), channel_id=1, source_target_pairs={{7,511},{15,503},{23,495},{31,487},{39,479},{47,471},{55,463},{63,... | collective-permute-start | bytes 258056 | tf_op jit(solution)/shard_map/ppermute | solution.py:709
  31.2 2.2 %shard_map.104 = (f32[256,128]{1,0:T(8,128)S(1)}, f32[256,128]{1,0:T(8,128)S(1)}, f32[256,128]{1,0:T(8,128)S(1)}, f32[256,128]{1,0:T(8,128)S(1)}, f32[47,16,128]{2,1,0:T(8,128)S(1)}) custom-call(f32[256,128]{1,0:T(8,128)S(1)} %get-tuple-element.37.t_ref, f32[256,128]{1,0:T(8,128)S(1)} %get-tuple-element.38.s_ref, f32[256,128]{1,0:T(8,128)S(1)} %get-tuple-element.34.u_ref, ...), custom_call_target="tpu_custom_call" | custom-call | flops 16777216 | bytes 1048576 | tf_op jit(solution)/shard_map/pallas_call | solution.py:655
  33.4 0.0 collective-permute-done.3.even_ref
  33.4 0.0 collective-permute-done.4.o_ref
  33.4 0.1 shard_map.105
  33.5 0.0 collective-permute-done.1.odd_ref
  33.5 0.0 collective-permute-done.2.f_ref
  33.6 1.0 %shard_map.106 = (f32[256,128]{1,0:T(8,128)}, f32[256,128]{1,0:T(8,128)}, f32[256,128]{1,0:T(8,128)}, f32[256,128]{1,0:T(8,128)}, f32[256,128]{1,0:T(8,128)S(1)}...) custom-call(f32[256,128]{1,0:T(8,128)S(1)} %get-tuple-element.34.u_r, ...), custom_call_target="tpu_custom_call", output_to_operand_aliasing={{0}: (8, {}), {1}: (9, {}), {2}: (10, {}), {3}: (11, {}), {... | custom-call | flops 2097152 | bytes 1048576 | tf_op jit(solution)/shard_map/pallas_call | solution.py:655
Async XLA Ops:
  2.1 12.6 %collective-permute-start = (f32[16,384]{1,0:T(8,128)S(1)}, f32[16,384]{1,0:T(8,128)S(1)}, u32[]{:S(2)}, u32[]{:S(2)}) collective-permute-start(f32[16,384]{1,0:T(8,128)S(1)} %get-tuple-element.41), channel_id=1, source_target_pairs={{0,504},{8,16},{16,8},{24,32},{32,24},{40,48},{48,40},{56,64},{64,... | collective-permute-start | bytes 73736 | tf_op jit(solution)/shard_map/ppermute | solution.py:679
  15.4 18.0 %collective-permute-start.3 = (f32[21,8,128]{2,1,0:T(8,128)S(1)}, f32[21,8,128]{2,1,0:T(8,128)S(1)}, u32[]{:S(2)}, u32[]{:S(2)}) collective-permute-start(f32[21,8,128]{2,1,0:T(8,128)S(1)} %get-tuple-element.46), channel_id=1, source_target_pairs={{0,1},{1,0},{3,2},{5,4},{7,6},{8,9},{9,8},{11,10},{13,12},{15,14},... | collective-permute-start | bytes 258056 | tf_op jit(solution)/shard_map/ppermute | solution.py:706
  20.4 13.1 %collective-permute-start.4 = (f32[21,8,128]{2,1,0:T(8,128)S(1)}, f32[21,8,128]{2,1,0:T(8,128)S(1)}, u32[]{:S(2)}, u32[]{:S(2)}) collective-permute-start(f32[21,8,128]{2,1,0:T(8,128)S(1)} %get-tuple-element.47), channel_id=1, source_target_pairs={{1,2},{2,1},{3,4},{4,3},{5,6},{6,5},{9,10},{10,9},{11,12},{12,11},... | collective-permute-start | bytes 258056 | tf_op jit(solution)/shard_map/ppermute | solution.py:707
  21.7 11.9 %collective-permute-start.1 = (f32[21,8,128]{2,1,0:T(8,128)S(1)}, f32[21,8,128]{2,1,0:T(8,128)S(1)}, u32[]{:S(2)}, u32[]{:S(2)}) collective-permute-start(f32[21,8,128]{2,1,0:T(8,128)S(1)} %get-tuple-element.44), channel_id=1, source_target_pairs={{2,3},{4,5},{6,7},{10,11},{12,13},{14,15},{18,19},{20,21},{22,23},... | collective-permute-start | bytes 258056 | tf_op jit(solution)/shard_map/ppermute | solution.py:708
  23.0 10.6 %collective-permute-start.2 = (f32[21,8,128]{2,1,0:T(8,128)S(1)}, f32[21,8,128]{2,1,0:T(8,128)S(1)}, u32[]{:S(2)}, u32[]{:S(2)}) collective-permute-start(f32[21,8,128]{2,1,0:T(8,128)S(1)} %get-tuple-element.45), channel_id=1, source_target_pairs={{7,511},{15,503},{23,495},{31,487},{39,479},{47,471},{55,463},{63,... | collective-permute-start | bytes 258056 | tf_op jit(solution)/shard_map/ppermute | solution.py:709
